TPU v7x, 512 devices: a whole 4x8x8 slice. The times are simulated.
512 devices in a mesh: row: 16 (over z, x_hi), col: 32 (over y, x_lo, core).
Axes of the slice: x: 4 (x_hi: 2, x_lo: 2; x = x_hi * 2 + x_lo), y: 8, z: 8, core: 2. Of those that a mesh axis runs over, the one named last changes fastest.
Arguments:
- alignment: bfloat16 [256, 256, 256], P('col', 'row'), may hold values from -6 to 6
- pair_features: bfloat16 [256, 256, 128], P('row', 'col'), may hold values from -6 to 6
- query_matrix: bfloat16 [256, 256], replicated, may hold values from -0.375 to 0.375
- key_matrix: bfloat16 [256, 256], replicated, may hold values from -0.375 to 0.375
- value_matrix: bfloat16 [256, 256], replicated, may hold values from -0.375 to 0.375
- gate_matrix: bfloat16 [256, 256], replicated, may hold values from -0.375 to 0.375
- output_matrix: bfloat16 [256, 256], replicated, may hold values from -0.375 to 0.375
- bias_weight: bfloat16 [128, 8], replicated, may hold values from -29 to 29
- left_factor_weight: bfloat16 [256, 32], replicated, may hold values from -0.375 to 0.375
- right_factor_weight: bfloat16 [256, 32], replicated, may hold values from -0.375 to 0.375
- outer_weight: bfloat16 [1024, 128], replicated, may hold values from -3 to 3
- outgoing_project: bfloat16 [128, 512], replicated, may hold values from -0.5 to 0.5
- outgoing_gate: bfloat16 [128, 128], replicated, may hold values from -0.5 to 0.5
- outgoing_output: bfloat16 [128, 128], replicated, may hold values from -0.5 to 0.5
- incoming_project: bfloat16 [128, 512], replicated, may hold values from -0.5 to 0.5
- incoming_gate: bfloat16 [128, 128], replicated, may hold values from -0.5 to 0.5
- incoming_output: bfloat16 [128, 128], replicated, may hold values from -0.5 to 0.5
Outputs:
- new_alignment: bfloat16 [256, 256, 256], P('col', 'row')
- new_pair: bfloat16 [256, 256, 128], P('row', 'col')
All inputs are finite; a program needn't handle non-finite values.
Results may differ from a plain program's by a relative error of at most 0.022.
Values may be sent and summed in bfloat16 or wider, within the bound.
No kernel may reach another device: no remote copies, remote signals or barrier semaphores. Data moves between devices by JAX's collectives and lax.ppermute only.
A program may use at most 64 MiB of HBM per device.

v0:
```python
import jax
import jax.numpy as jnp
from jax import lax
from jax.sharding import PartitionSpec as P


def broadcast(value, axis, source):
    kept = jnp.where(lax.axis_index(axis) == source, value, 0).astype(value.dtype)
    return lax.psum(kept, axis)


def layer_norm(values):
    values = values.astype(jnp.float32)
    center = values - jnp.mean(values, axis=-1, keepdims=True)
    variance = jnp.mean(center * center, axis=-1, keepdims=True)
    return center * lax.rsqrt(variance + 1e-05)


def project(values, weight):
    return jnp.dot(values, weight, preferred_element_type=jnp.float32)


def edges(pair_x, in_weight, gate_x):
    normed = layer_norm(pair_x).astype(jnp.bfloat16)
    proj = project(normed, in_weight)
    width = in_weight.shape[1] // 4
    left = (jax.nn.sigmoid(proj[..., :width]) * proj[..., width : 2 * width]).astype(jnp.bfloat16)
    right = (jax.nn.sigmoid(proj[..., 2 * width : 3 * width]) * proj[..., 3 * width :]).astype(
        jnp.bfloat16
    )
    gate = jax.nn.sigmoid(project(normed, gate_x))
    return (jnp.transpose(left, (2, 0, 1)), jnp.transpose(right, (2, 0, 1)), gate)


def finish(pair_x, combined_cf, gate, out_weight):
    combined_norm = layer_norm(jnp.transpose(combined_cf, (1, 2, 0))).astype(jnp.bfloat16)
    return (pair_x.astype(jnp.float32) + gate * project(combined_norm, out_weight)).astype(
        jnp.bfloat16
    )


def on_device(
    alignment,
    pair_features,
    query_matrix,
    key_matrix,
    value_matrix,
    gate_matrix,
    output_matrix,
    bias_weight,
    left_factor_weight,
    right_factor_weight,
    outer_weight,
    outgoing_project,
    outgoing_gate,
    outgoing_output,
    incoming_project,
    incoming_gate,
    incoming_output,
):
    seq_count, row_len, channels = alignment.shape
    col_len = pair_features.shape[1]
    heads = bias_weight.shape[1]
    head_dim = channels // heads
    ratio = row_len // col_len
    col_index = lax.axis_index("col")
    row_index = lax.axis_index("row")
    owner_row = col_index // ratio
    offset = col_index % ratio * col_len
    normed = layer_norm(alignment).astype(jnp.bfloat16)
    queries = (
        project(normed, query_matrix)
        .astype(jnp.bfloat16)
        .reshape(seq_count, row_len, heads, head_dim)
    )
    gates = jax.nn.sigmoid(project(normed, gate_matrix))
    both_weights = jnp.concatenate([key_matrix, value_matrix], axis=1)
    keys_values = project(lax.all_gather(normed, "row", axis=1, tiled=True), both_weights).astype(
        jnp.bfloat16
    )
    full_len = keys_values.shape[1]
    keys = keys_values[..., :channels].reshape(seq_count, full_len, heads, head_dim)
    values = keys_values[..., channels:].reshape(seq_count, full_len, heads, head_dim)
    pair_normed = layer_norm(pair_features).astype(jnp.bfloat16)
    bias_local = jnp.einsum(
        "ijc,ch->hij", pair_normed, bias_weight, preferred_element_type=jnp.float32
    ).astype(jnp.bfloat16)
    bias = lax.all_gather(bias_local, "col", axis=2, tiled=True).astype(jnp.float32)
    scores = (
        jnp.einsum("sihd,sjhd->shij", queries, keys, preferred_element_type=jnp.float32)
        * head_dim ** (-0.5)
        + bias[None]
    )
    highest = jnp.max(scores, axis=-1, keepdims=True)
    expo = jnp.exp(scores - highest)
    weights = (expo / jnp.sum(expo, axis=-1, keepdims=True)).astype(jnp.bfloat16)
    attended = jnp.einsum(
        "shij,sjhd->sihd", weights, values, preferred_element_type=jnp.float32
    ).reshape(seq_count, row_len, channels)
    gated = (gates * attended).astype(jnp.bfloat16)
    new_alignment = (alignment.astype(jnp.float32) + project(gated, output_matrix)).astype(
        jnp.bfloat16
    )
    outer_dim = left_factor_weight.shape[1]
    outer_normed = layer_norm(new_alignment).astype(jnp.bfloat16)
    left_local = project(outer_normed, left_factor_weight).astype(jnp.bfloat16)
    right_local = project(outer_normed, right_factor_weight).astype(jnp.bfloat16)
    left_all, right_rows_all = (
        lax.all_gather(
            left_local.reshape(seq_count, row_len * outer_dim), "col", axis=0, tiled=True
        ),
        lax.all_gather(
            right_local.reshape(seq_count, row_len * outer_dim), "col", axis=0, tiled=True
        ),
    )
    total_seqs = left_all.shape[0]
    right_select_outer = lax.dynamic_slice_in_dim(
        right_rows_all.reshape(total_seqs, row_len, outer_dim), offset, col_len, 1
    )
    right_all = broadcast(
        right_select_outer.reshape(total_seqs, col_len * outer_dim), "row", owner_row
    )
    products = jnp.einsum("sa,sb->ab", left_all, right_all, preferred_element_type=jnp.float32) * (
        1.0 / total_seqs
    )
    outer = products.reshape(row_len, outer_dim, col_len, outer_dim).transpose(0, 2, 1, 3)
    outer = outer.reshape(row_len, col_len, outer_dim * outer_dim).astype(jnp.bfloat16)
    pair_one = (pair_features.astype(jnp.float32) + project(outer, outer_weight)).astype(
        jnp.bfloat16
    )
    left_cf, right_cf, gate_one = edges(pair_one, outgoing_project, outgoing_gate)
    left_rows, right_rows = (
        lax.all_gather(left_cf, "col", axis=2, tiled=True),
        lax.all_gather(right_cf, "col", axis=2, tiled=True),
    )
    right_select = lax.dynamic_slice_in_dim(right_rows, offset, col_len, 1)
    right_own = broadcast(right_select, "row", owner_row)
    combined = jnp.einsum("cik,cjk->cij", left_rows, right_own, preferred_element_type=jnp.float32)
    pair_two = finish(pair_one, combined, gate_one, outgoing_output)
    left_in, right_in, gate_two = edges(pair_two, incoming_project, incoming_gate)
    left_cols, right_cols = (
        lax.all_gather(left_in, "row", axis=1, tiled=True),
        lax.all_gather(right_in, "row", axis=1, tiled=True),
    )
    owned = [broadcast(left_cols, "col", row_index * ratio + position) for position in range(ratio)]
    left_own = jnp.concatenate(owned, axis=2)
    combined_in = jnp.einsum(
        "cki,ckj->cij", left_own, right_cols, preferred_element_type=jnp.float32
    )
    new_pair = finish(pair_two, combined_in, gate_two, incoming_output)
    return (new_alignment, new_pair)


def solution(mesh):
    return jax.shard_map(
        on_device,
        mesh=mesh,
        in_specs=(
            P("col", "row", None),
            P("row", "col", None),
            P(),
            P(),
            P(),
            P(),
            P(),
            P(),
            P(),
            P(),
            P(),
            P(),
            P(),
            P(),
            P(),
            P(),
            P(),
        ),
        out_specs=(P("col", "row", None), P("row", "col", None)),
        check_vma=False,
    )
```

profile of v0, /device:TPU:1, one launch (start us, length us, event | category | flops | bytes accessed | tf_op | source)
XLA Modules:
  0.0 891.6 jit_solution(10023177219985992045)
XLA Ops:
  7.2 1.0 convert_reduce_fusion
  8.3 1.0 fusion.38
  9.3 1.6 fusion.39
  11.0 1.2 convolution_convert_fusion.1
  12.1 0.9 reshape.121
  13.0 0.8 convert_reduce_fusion.2
  14.0 0.9 fusion.52
  15.1 1.0 fusion.24
  16.2 38.5 %all_gather.25 = bf16[8,16,256]{1,0,2:T(8,128)(2,1)S(1)} all-gather(bf16[8,16,8]{1,0,2:T(8,128)(2,1)S(1)} %copy.134), channel_id=1, replica_groups=mesh['row'=16,'col'=32] {'col'}, dimensions={2}, use_global_device_ids=true | all-gather | bytes 67584 | tf_op jit(solution)/shard_map/all_gather | solution.py:88
  55.1 40.7 %all-gather.4.cloned.1.call-done = bf16[8,256,256]{2,1,0:T(8,128)(2,1)} async-done(((bf16[8,16,256]{2,1,0:T(8,128)(2,1)}), bf16[8,256,256]{2,1,0:T(8,128)(2,1)}) %all-gather.4.cloned.1.call-update) | async-done | bytes 1048592 | tf_op jit(solution)/shard_map/all_gather | solution.py:78
  95.8 1.9 convolution_convert_fusion
  98.5 1.2 fusion.3
  100.6 2.7 convolution_bitcast_fusion
  103.3 1.2 copy.136
  105.7 37.6 %all_gather.27 = bf16[256,512]{1,0:T(8,128)(2,1)S(1)} all-gather(bf16[8,512]{1,0:T(8,128)(2,1)S(1)} %reshape.125), channel_id=1, replica_groups=mesh['row'=16,'col'=32] {'col'}, dimensions={0}, use_global_device_ids=true | all-gather | bytes 270336 | tf_op jit(solution)/shard_map/all_gather | solution.py:112
  144.5 31.5 %all_gather.26 = bf16[256,512]{1,0:T(8,128)(2,1)S(1)} all-gather(bf16[8,512]{1,0:T(8,128)(2,1)S(1)} %reshape.124), channel_id=1, replica_groups=mesh['row'=16,'col'=32] {'col'}, dimensions={0}, use_global_device_ids=true | all-gather | bytes 270336 | tf_op jit(solution)/shard_map/all_gather | solution.py:109
  176.0 115.1 %all-reduce.5.cloned.1.call-done = bf16[256,256]{0,1:T(8,128)(2,1)} async-done(((bf16[256,256]{0,1:T(8,128)(2,1)}), bf16[256,256]{0,1:T(8,128)(2,1)}) %all-reduce.5.cloned.1.call-update) | async-done | bytes 131088 | tf_op jit(solution)/shard_map/psum | solution.py:9
  291.1 1.2 fusion.4
  293.0 1.1 convert_element_type.129
  296.5 72.4 %all-gather.8.cloned.1.call-done = bf16[128,16,256]{0,2,1:T(8,128)(2,1)} async-done(((bf16[128,16,8]{0,2,1:T(8,128)(2,1)}), bf16[128,16,256]{0,2,1:T(8,128)(2,1)}) %all-gather.8.cloned.1.call-update) | async-done | bytes 1048592 | tf_op jit(solution)/shard_map/all_gather | solution.py:134
  368.9 1.9 dynamic-slice_select_fusion
  371.1 63.6 %all-gather.6.cloned.1.call-done = bf16[128,16,256]{0,2,1:T(8,128)(2,1)} async-done(((bf16[128,16,8]{0,2,1:T(8,128)(2,1)}), bf16[128,16,256]{0,2,1:T(8,128)(2,1)}) %all-gather.6.cloned.1.call-update) | async-done | bytes 1048592 | tf_op jit(solution)/shard_map/all_gather | solution.py:133
  434.6 8.5 copy.143
  443.2 147.1 %all-reduce.7.cloned.1.call-done = bf16[128,8,256]{0,2,1:T(8,128)(2,1)} async-done(((bf16[128,8,256]{0,2,1:T(8,128)(2,1)}), bf16[128,8,256]{0,2,1:T(8,128)(2,1)}) %all-reduce.7.cloned.1.call-update) | async-done | bytes 524304 | tf_op jit(solution)/shard_map/psum | solution.py:9
  590.3 1.4 copy.144
  591.7 4.6 bitcast_reduce_fusion.1
  598.0 35.7 %all_gather.30 = bf16[128,256,8]{0,2,1:T(8,128)(2,1)S(1)} all-gather(bf16[128,16,8]{0,2,1:T(8,128)(2,1)S(1)} %get-tuple-element.8), channel_id=1, replica_groups=mesh['row'=16,'col'=32] {'row'}, dimensions={1}, use_global_device_ids=true | all-gather | bytes 557056 | tf_op jit(solution)/shard_map/all_gather | solution.py:142
  634.4 1.1 broadcast_select_fusion.1
  635.5 31.8 %all_gather.31 = bf16[128,256,8]{0,2,1:T(8,128)(2,1)S(1)} all-gather(bf16[128,16,8]{0,2,1:T(8,128)(2,1)S(1)} %get-tuple-element.9), channel_id=1, replica_groups=mesh['row'=16,'col'=32] {'row'}, dimensions={1}, use_global_device_ids=true | all-gather | bytes 557056 | tf_op jit(solution)/shard_map/all_gather | solution.py:143
  668.1 213.6 %all-reduce.9.cloned.1.call-done = (bf16[128,256,8]{1,2,0:T(8,128)(2,1)}, bf16[128,256,8]{1,2,0:T(8,128)(2,1)}) async-done(((bf16[128,256,8]{1,2,0:T(8,128)(2,1)}, bf16[128,256,8]{1,2,0:T(8,128)(2,1)}), (bf16[128,256,8]{1,2,0:T(8,128)(2,1)}, bf16[128,256,8]{1,2,0:T(8,128)(2,1)})) %all-reduce.9.cloned.1.call-update) | async-done | bytes 1048592 | tf_op jit(solution)/shard_map/psum | solution.py:9
  881.7 1.6 bitcast_reduce_fusion
  883.9 0.8 fusion.21
  (110 shorter events, 11.7 us)
Async XLA Ops:
  7.2 287.0 %copy-start = (bf16[1024,128]{1,0:T(8,128)(2,1)S(1)}, bf16[1024,128]{1,0:T(8,128)(2,1)}, u32[]{:S(2)}) copy-start(bf16[1024,128]{1,0:T(8,128)(2,1)} %param.27) | copy-start | bytes 786436
  7.2 88.6 %copy-start.6 = (bf16[256,256]{1,0:T(8,128)(2,1)S(1)}, bf16[256,256]{1,0:T(8,128)(2,1)}, u32[]{:S(2)}) copy-start(bf16[256,256]{1,0:T(8,128)(2,1)} %param.20) | copy-start | bytes 393220
  7.2 88.6 %copy-start.5 = (bf16[256,256]{1,0:T(8,128)(2,1)S(1)}, bf16[256,256]{1,0:T(8,128)(2,1)}, u32[]{:S(2)}) copy-start(bf16[256,256]{1,0:T(8,128)(2,1)} %param.21) | copy-start | bytes 393220
  7.2 88.5 %all-gather.4.cloned.1.call-start = ((), (), s32[]{:S(2)}) async-start(), calls=%async_computation | async-start | bytes 1114112 | tf_op jit(solution)/shard_map/all_gather | solution.py:78
  10.9 280.2 %all-reduce.5.cloned.1.call-start = ((), (), s32[]{:S(2)}) async-start(), calls=%async_computation.1 | async-start | bytes 262144 | tf_op jit(solution)/shard_map/psum | solution.py:9
  100.6 4.1 copy-start.1
  100.6 4.1 copy-start.10
  100.6 4.1 copy-start.11
  103.3 2.1 copy-start.14
  103.3 40.9 %copy-start.15 = (bf16[256,32]{0,1:T(8,128)(2,1)S(1)}, bf16[256,32]{0,1:T(8,128)(2,1)}, u32[]{:S(2)}) copy-start(bf16[256,32]{0,1:T(8,128)(2,1)} %param.25) | copy-start | bytes 49156
  105.2 187.8 %copy-start.7 = (bf16[8,16,256]{2,1,0:T(8,128)(2,1)}, bf16[8,16,256]{2,1,0:T(8,128)(2,1)S(1)}, u32[]{:S(2)}) copy-start(bf16[8,16,256]{2,1,0:T(8,128)(2,1)S(1)} %get-tuple-element.13) | copy-start | bytes 196612
  144.1 224.7 %all-gather.8.cloned.1.call-start = ((), (), s32[]{:S(2)}) async-start(), calls=%async_computation.3 | async-start | bytes 1081344 | tf_op jit(solution)/shard_map/all_gather | solution.py:134
  292.3 1.9 copy-start.2
  292.7 2.2 copy-start.3
  293.0 77.8 %copy-start.12 = (bf16[128,128]{1,0:T(8,128)(2,1)S(1)}, bf16[128,128]{1,0:T(8,128)(2,1)}, u32[]{:S(2)}) copy-start(bf16[128,128]{1,0:T(8,128)(2,1)} %param.29) | copy-start | bytes 98308
  295.8 138.8 %all-gather.6.cloned.1.call-start = ((), (), s32[]{:S(2)}) async-start(), calls=%async_computation.2 | async-start | bytes 1081344 | tf_op jit(solution)/shard_map/all_gather | solution.py:133
  296.4 293.8 %all-reduce.7.cloned.1.call-start = ((), (), s32[]{:S(2)}) async-start(), calls=%async_computation.4 | async-start | bytes 1048576 | tf_op jit(solution)/shard_map/psum | solution.py:9
  370.8 511.0 %all-reduce.9.cloned.1.call-start = ((), (), s32[]{:S(2)}) async-start(), calls=%async_computation.5 | async-start | bytes 2097152 | tf_op jit(solution)/shard_map/psum | solution.py:9
  591.7 5.3 copy-start.8
  591.7 6.0 copy-start.4
  634.3 33.5 %copy-start.13 = (bf16[128,128]{1,0:T(8,128)(2,1)S(1)}, bf16[128,128]{1,0:T(8,128)(2,1)}, u32[]{:S(2)}) copy-start(bf16[128,128]{1,0:T(8,128)(2,1)} %param.32) | copy-start | bytes 98308
  667.3 216.7 %copy-start.9 = (bf16[128,128]{1,0:T(8,128)(2,1)S(1)}, bf16[128,128]{1,0:T(8,128)(2,1)}, u32[]{:S(2)}) copy-start(bf16[128,128]{1,0:T(8,128)(2,1)} %param.33) | copy-start | bytes 98308
Sparse Core Ops, SparseCore 0:
  11.7 84.0 all-gather.3
  144.3 146.7 all-reduce.4
  296.0 72.8 all-gather.7
  371.0 63.6 all-gather.5
  437.6 152.5 all-reduce.6
  635.6 246.0 all-reduce.8
where the time goes:
time: 892 us
  waiting for transfers between devices  653 us (73%)
  blocking collectives  175 us (20%)
  local copies, waits for them, and re-layouts  19 us (2%)
  matrix products  18.5 us (2%)
  between operations  14.7 us (2%)
  other arithmetic  11 us (1%)
    psum x3, waiting for transfers between devices, broadcast(): return lax.psum(kept, axis)  476 us
    all_gather x1, waiting for transfers between devices, on_device(): lax.all_gather(right_cf, 'col', axis=2, tiled=True)  72.4 us
    all_gather x1, waiting for transfers between devices, on_device(): lax.all_gather(left_cf, 'col', axis=2, tiled=True)  63.6 us
    all_gather x1, waiting for transfers between devices, on_device(): lax.all_gather(normed, 'row', axis=1, tiled=True)  40.7 us
    all_gather x1, blocking collectives, on_device(): lax.all_gather(bias_local, 'col', axis=2, tiled=True).astype(jnp.float32)  38.5 us
    all_gather x1, blocking collectives, on_device(): lax.all_gather(right_local.reshape(seq_count, row_len * outer_dim), 'col'...  37.6 us
    all_gather x1, blocking collectives, on_device(): lax.all_gather(left_in, 'row', axis=1, tiled=True)  35.7 us
    all_gather x1, blocking collectives, on_device(): lax.all_gather(right_in, 'row', axis=1, tiled=True)  31.8 us
  transfers between devices with their start and end apart: 6, of which 6 were waited for; matrix products, arithmetic and copies ran while one was open for 2% of the time, Pallas kernels for 0%

commit v1 on v0

v1 whole, which is shorter than its diff:
```python
import jax
import jax.numpy as jnp
from jax import lax
from jax.experimental import pallas as pl
from jax.experimental.pallas import tpu as pltpu
from jax.sharding import PartitionSpec as P

F32 = jnp.float32
BF16 = jnp.bfloat16
ROWS, COLS, CHIPS = 16, 32, 16
SAME_CORE = [[2 * chip + core for chip in range(CHIPS)] for core in range(2)]
SWAP = [(c, c ^ 1) for c in range(COLS)]
TURN = [
    (r * COLS + c, (c // 2) * COLS + 2 * r + c % 2) for r in range(ROWS) for c in range(COLS)
]


def layer_norm(values):
    values = values.astype(F32)
    center = values - jnp.mean(values, axis=-1, keepdims=True)
    variance = jnp.mean(center * center, axis=-1, keepdims=True)
    return center * lax.rsqrt(variance + 1e-05)


def project(values, weight):
    return jnp.dot(values, weight, preferred_element_type=F32)


def exchange(chunks, axis, groups=None):
    return lax.all_to_all(chunks, axis, 0, 0, axis_index_groups=groups)


def spread(block, axis, count, groups=None):
    return exchange(jnp.broadcast_to(block[None], (count,) + block.shape), axis, groups)


def edges(pair_x, in_weight, gate_x):
    normed = layer_norm(pair_x).astype(BF16)
    proj = project(normed, in_weight)
    width = in_weight.shape[1] // 4
    left = (jax.nn.sigmoid(proj[..., :width]) * proj[..., width : 2 * width]).astype(BF16)
    right = (jax.nn.sigmoid(proj[..., 2 * width : 3 * width]) * proj[..., 3 * width :]).astype(BF16)
    gate = jax.nn.sigmoid(project(normed, gate_x))
    return left, right, gate


def finish(pair_x, combined, gate, out_weight):
    combined_norm = layer_norm(combined).astype(BF16)
    return (pair_x.astype(F32) + gate * project(combined_norm, out_weight)).astype(BF16)


def partial_kernel(tile_ref, line_ref, out_ref):
    depth = tile_ref.shape[1]
    lines = line_ref.shape[0]

    def one(g, carry):
        tiles = [tile_ref[g, k].astype(F32) for k in range(depth)]
        for n in range(lines):
            total = tiles[0] * line_ref[n, 0:1, :]
            for k in range(1, depth):
                total = total + tiles[k] * line_ref[n, k : k + 1, :]
            out_ref[g, n] = total.astype(BF16)
        return carry

    lax.fori_loop(0, tile_ref.shape[0], one, 0)


def partial_sums(tiles, lines):
    groups, depth, height, width = tiles.shape
    count = lines.shape[0]
    return pl.pallas_call(
        partial_kernel,
        out_shape=jax.ShapeDtypeStruct((groups, count, height, width), BF16),
        cost_estimate=pl.CostEstimate(
            flops=2 * groups * count * height * width * depth,
            bytes_accessed=2 * groups * height * width * (count + depth),
            transcendentals=0,
        ),
    )(tiles, lines.astype(F32))


def attention(
    alignment, pair_features, query_matrix, key_matrix, value_matrix, gate_matrix, output_matrix, bias_weight
):
    seq_count, row_len, channels = alignment.shape
    heads = bias_weight.shape[1]
    head_dim = channels // heads
    pair_normed = layer_norm(pair_features).astype(BF16)
    bias_local = jnp.einsum(
        "ijc,ch->jhi", pair_normed, bias_weight, preferred_element_type=F32
    ).astype(BF16)
    col_len = bias_local.shape[0]
    bias = spread(bias_local.reshape(col_len, heads * row_len), "col", COLS)
    full_len = COLS * col_len
    bias = bias.reshape(full_len, heads * row_len).T.reshape(heads, row_len, full_len).astype(F32)
    normed = layer_norm(alignment).astype(BF16)
    queries = project(normed, query_matrix).astype(BF16).reshape(seq_count, row_len, heads, head_dim)
    gates = jax.nn.sigmoid(project(normed, gate_matrix))
    both_weights = jnp.concatenate([key_matrix, value_matrix], axis=1)
    everyone = spread(normed, "row", ROWS)
    everyone = jnp.transpose(everyone, (1, 0, 2, 3)).reshape(seq_count, full_len, channels)
    keys_values = project(everyone, both_weights).astype(BF16)
    keys = keys_values[..., :channels].reshape(seq_count, full_len, heads, head_dim)
    values = keys_values[..., channels:].reshape(seq_count, full_len, heads, head_dim)
    scores = (
        jnp.einsum("sihd,sjhd->shij", queries, keys, preferred_element_type=F32) * head_dim ** (-0.5)
        + bias[None]
    )
    highest = jnp.max(scores, axis=-1, keepdims=True)
    expo = jnp.exp(scores - highest)
    weights = (expo / jnp.sum(expo, axis=-1, keepdims=True)).astype(BF16)
    attended = jnp.einsum("shij,sjhd->sihd", weights, values, preferred_element_type=F32)
    gated = (gates * attended.reshape(seq_count, row_len, channels)).astype(BF16)
    return (alignment.astype(F32) + project(gated, output_matrix)).astype(BF16)


def on_device(
    alignment,
    pair_features,
    query_matrix,
    key_matrix,
    value_matrix,
    gate_matrix,
    output_matrix,
    bias_weight,
    left_factor_weight,
    right_factor_weight,
    outer_weight,
    outgoing_project,
    outgoing_gate,
    outgoing_output,
    incoming_project,
    incoming_gate,
    incoming_output,
):
    seq_count, row_len, channels = alignment.shape
    col_len, pair_dim = pair_features.shape[1:]
    core = lax.axis_index("col") % 2
    new_alignment = attention(
        alignment, pair_features, query_matrix, key_matrix, value_matrix, gate_matrix, output_matrix, bias_weight
    )
    outer_dim = left_factor_weight.shape[1]
    outer_normed = layer_norm(new_alignment).astype(BF16)
    right = project(outer_normed, right_factor_weight).astype(BF16)
    left = project(outer_normed, left_factor_weight).astype(BF16)
    width = col_len * outer_dim
    halves = right.reshape(seq_count, 2, width).transpose(1, 0, 2)
    halves = jnp.broadcast_to(halves[None], (CHIPS,) + halves.shape).reshape(COLS, seq_count, width)
    right_half = exchange(halves, "col").reshape(COLS * seq_count, width)
    right_all = lax.ppermute(right_half, ("row", "col"), TURN)
    left_all = spread(left.reshape(seq_count, row_len * outer_dim), "col", COLS)
    total_seqs = COLS * seq_count
    left_all = left_all.reshape(total_seqs, row_len * outer_dim)
    products = jnp.einsum("sa,sb->ab", left_all, right_all, preferred_element_type=F32) * (
        1.0 / total_seqs
    )
    outer = products.reshape(row_len, outer_dim, col_len, outer_dim).transpose(0, 2, 1, 3)
    outer = outer.reshape(row_len, col_len, outer_dim * outer_dim).astype(BF16)
    pair_one = (pair_features.astype(F32) + project(outer, outer_weight)).astype(BF16)

    left_edge, right_edge, gate_one = edges(pair_one, outgoing_project, outgoing_gate)
    right_edge = right_edge.reshape(2, col_len, col_len, pair_dim)
    mine = lax.dynamic_index_in_dim(right_edge, core, 0, keepdims=False)
    theirs = lax.dynamic_index_in_dim(right_edge, 1 - core, 0, keepdims=False)
    swapped = lax.ppermute(jnp.concatenate([left_edge, theirs], axis=0), "col", SWAP)
    lines = jnp.concatenate([left_edge, swapped[:row_len]], axis=1)
    tiles = jnp.concatenate([mine, swapped[row_len:]], axis=1).transpose(1, 0, 2)
    partial = partial_sums(spread(tiles, "row", ROWS), lines)
    partial = exchange(partial, "col", SAME_CORE)
    combined = jnp.sum(partial.astype(F32), axis=0)
    pair_two = finish(pair_one, combined, gate_one, outgoing_output)

    left_edge, right_edge, gate_two = edges(pair_two, incoming_project, incoming_gate)
    lines = right_edge.transpose(1, 0, 2)
    own = spread(left_edge, "col", CHIPS, SAME_CORE)
    other = lax.ppermute(own, "col", SWAP)
    own_sums = partial_sums(own, lines)
    other_sums = partial_sums(other, lines)
    first = jnp.where(core == 0, own_sums, other_sums)
    second = jnp.where(core == 0, other_sums, own_sums)
    partial = exchange(jnp.stack([first, second], axis=1), "row")
    combined_in = jnp.sum(partial.astype(F32), axis=0)
    combined_in = combined_in.transpose(0, 2, 1, 3).reshape(row_len, col_len, pair_dim)
    new_pair = finish(pair_two, combined_in, gate_two, incoming_output)
    return (new_alignment, new_pair)


def solution(mesh):
    rep = (P(),) * 15
    return jax.shard_map(
        on_device,
        mesh=mesh,
        in_specs=(P("col", "row", None), P("row", "col", None)) + rep,
        out_specs=(P("col", "row", None), P("row", "col", None)),
        check_vma=False,
    )
```

time: 892 us -> 230 us (0.26)
  waiting for transfers between devices: 653 us -> 99.1 us
  blocking collectives: 175 us -> 16.9 us
  starting transfers between devices: 0.24 us -> 71.6 us
  between operations: 14.7 us -> 1.4 us
  matrix products: 18.5 us -> 8.44 us
    psum x3 -> x0, waiting for transfers between devices: 476 us -> none  [broadcast(): return lax.psum(kept, axis)]
    all_gather x3 -> x0, waiting for transfers between devices: 177 us -> none  [the longest x1 72.4 us: on_device(): lax.all_gather(right_cf, 'col', axis=2, tiled=True)]
    all_gather x5 -> x0, blocking collectives: 175 us -> none  [the longest x1 38.5 us: on_device(): lax.all_gather(bias_local, 'col', axis=2, tiled=True).astype(jnp.float32)]
    all_to_all x0 -> x7, waiting for transfers between devices: none -> 98.3 us  [exchange(): return lax.all_to_all(chunks, axis, 0, 0, axis_index_groups=groups)]
    all_to_all x0 -> x7, starting transfers between devices: none -> 60.3 us  [exchange(): return lax.all_to_all(chunks, axis, 0, 0, axis_index_groups=groups)]
    all_to_all x0 -> x1, blocking collectives: none -> 16.9 us  [exchange(): return lax.all_to_all(chunks, axis, 0, 0, axis_index_groups=groups)]
    ppermute x0 -> x3, starting transfers between devices: none -> 11.2 us  [the longest x1 7.12 us: on_device(): other = lax.ppermute(own, 'col', SWAP)]
    all_gather x5 -> x0, local copies, waits for them, and re-layouts: 10.1 us -> none  [the longest x1 8.54 us: on_device(): lax.all_gather(left_cf, 'col', axis=2, tiled=True)]
  transfers between devices with their start and end apart: 6 -> 10, of which waited for: 6 -> 8; matrix products, arithmetic and copies ran while one was open for 2% -> 3% of each run, Pallas kernels for 0% -> 1%
where the time goes in v1:
time: 230 us; the launch traced here: 229 us
  waiting for transfers between devices  99.1 us (43%)
  starting transfers between devices  71.6 us (31%)
  blocking collectives  16.9 us (7%)
  local copies, waits for them, and re-layouts  14 us (6%)
  other arithmetic  9.28 us (4%)
  matrix products  8.44 us (4%)
  Pallas kernels  8.4 us (4%)
    all_to_all x7, waiting for transfers between devices, exchange(): return lax.all_to_all(chunks, axis, 0, 0, axis_index_groups=groups)  98.3 us
    all_to_all x7, starting transfers between devices, exchange(): return lax.all_to_all(chunks, axis, 0, 0, axis_index_groups=groups)  60.3 us
    all_to_all x1, blocking collectives, exchange(): return lax.all_to_all(chunks, axis, 0, 0, axis_index_groups=groups)  16.9 us
    pallas_call x3, Pallas kernels, partial_sums(): pl.pallas_call(partial_kernel, out_shape=jax.ShapeDtypeStruct((groups, co...  8.4 us
    ppermute x1, starting transfers between devices, on_device(): other = lax.ppermute(own, 'col', SWAP)  7.12 us
  transfers between devices with their start and end apart: 10, of which 8 were waited for; matrix products, arithmetic and copies ran while one was open for 3% of the time, Pallas kernels for 1%

profile of v1, /device:TPU:1, one launch (start us, length us, event | category | flops | bytes accessed | tf_op | source)
XLA Modules:
  0.0 229.1 jit_solution(1843362805723031170)
XLA Ops:
  0.7 0.9 convert_reduce_fusion.6
  1.6 0.9 fusion.52
  5.0 10.4 %all-to-all-start.1 = ((bf16[32,8,128]{2,1,0:T(8,128)(2,1)}), bf16[32,8,128]{2,1,0:T(8,128)(2,1)S(1)}, u32[]{:S(2)}, u32[]{:S(2)}) async-start(bf16[32,8,128]{2,1,0:T(8,128)(2,1)} %broadcast_in_dim.18), calls=%async_computation.1 | async-start | bytes 131072 | tf_op jit(solution)/shard_map/all_to_all | solution.py:30
  15.4 0.9 convert_reduce_fusion.3
  16.4 1.0 fusion.34
  17.4 0.9 fusion.35
  18.4 5.5 %all-to-all-done.1 = bf16[32,8,128]{2,1,0:T(8,128)(2,1)S(1)} async-done(((bf16[32,8,128]{2,1,0:T(8,128)(2,1)}), bf16[32,8,128]{2,1,0:T(8,128)(2,1)S(1)}, u32[]{:S(2)}, u32[]{:S(2)}) %all-to-all-start.1) | async-done | bytes 65568 | tf_op jit(solution)/shard_map/all_to_all | solution.py:30
  23.9 1.1 broadcast_in_dim.16
  24.9 11.5 %all-to-all-start = ((bf16[16,8,16,256]{3,2,1,0:T(8,128)(2,1)}), bf16[16,8,16,256]{3,2,1,0:T(8,128)(2,1)S(1)}, u32[]{:S(2)}, u32[]{:S(2)}) async-start(bf16[16,8,16,256]{3,2,1,0:T(8,128)(2,1)} %broadcast_in_dim.16), calls=%async_computation | async-start | bytes 2097152 | tf_op jit(solution)/shard_map/all_to_all | solution.py:30
  36.7 0.9 reshape.163
  38.4 25.2 %all-to-all-done = bf16[16,8,16,256]{3,2,1,0:T(8,128)(2,1)S(1)} async-done(((bf16[16,8,16,256]{3,2,1,0:T(8,128)(2,1)}), bf16[16,8,16,256]{3,2,1,0:T(8,128)(2,1)S(1)}, u32[]{:S(2)}, u32[]{:S(2)}) %all-to-all-start) | async-done | bytes 1048608 | tf_op jit(solution)/shard_map/all_to_all | solution.py:30
  65.2 1.3 fusion.3
  67.4 1.9 convolution_bitcast_fusion
  69.6 1.4 convert_reduce_fusion.4
  72.2 7.5 %all-to-all-start.3 = ((bf16[32,8,256]{2,1,0:T(8,128)(2,1)}), bf16[32,8,256]{2,1,0:T(8,128)(2,1)S(1)}, u32[]{:S(2)}, u32[]{:S(2)}) async-start(bf16[32,8,256]{2,1,0:T(8,128)(2,1)} %bitcast.18), calls=%async_computation.3 | async-start | bytes 262144 | tf_op jit(solution)/shard_map/all_to_all | solution.py:30
  80.1 9.1 %all-to-all-done.3 = bf16[32,8,256]{2,1,0:T(8,128)(2,1)S(1)} async-done(((bf16[32,8,256]{2,1,0:T(8,128)(2,1)}), bf16[32,8,256]{2,1,0:T(8,128)(2,1)S(1)}, u32[]{:S(2)}, u32[]{:S(2)}) %all-to-all-start.3) | async-done | bytes 131104 | tf_op jit(solution)/shard_map/all_to_all | solution.py:30
  89.9 4.0 %all-to-all-start.2 = ((bf16[32,8,512]{2,1,0:T(8,128)(2,1)}), bf16[32,8,512]{2,1,0:T(8,128)(2,1)S(1)}, u32[]{:S(2)}, u32[]{:S(2)}) async-start(bf16[32,8,512]{2,1,0:T(8,128)(2,1)} %broadcast_in_dim.20), calls=%async_computation.2 | async-start | bytes 524288 | tf_op jit(solution)/shard_map/all_to_all | solution.py:30
  94.6 10.8 %all-to-all-done.2 = bf16[32,8,512]{2,1,0:T(8,128)(2,1)S(1)} async-done(((bf16[32,8,512]{2,1,0:T(8,128)(2,1)}), bf16[32,8,512]{2,1,0:T(8,128)(2,1)S(1)}, u32[]{:S(2)}, u32[]{:S(2)}) %all-to-all-start.2) | async-done | bytes 262176 | tf_op jit(solution)/shard_map/all_to_all | solution.py:30
  106.4 1.1 convert_element_type.153
  108.3 3.5 %collective-permute-start.1 = (bf16[24,8,128]{2,0,1:T(8,128)(2,1)S(1)}, bf16[24,8,128]{2,0,1:T(8,128)(2,1)S(1)}, u32[]{:S(2)}, u32[]{:S(2)}) collective-permute-start(bf16[24,8,128]{2,0,1:T(8,128)(2,1)S(1)} %pad_maximum_fusion.1), channel_id=1, source_target_pairs={{0,1},{1,0},{2,3},{3,2},{4,5},{5,4},{6,7},{7,6},{8,9},{9,8},{10,11... | collective-permute-start | bytes 147464 | tf_op jit(solution)/shard_map/ppermute | solution.py:165
  113.6 14.5 %all-to-all-start.4 = ((bf16[16,16,8,128]{3,2,1,0:T(8,128)(2,1)}), bf16[16,16,8,128]{3,2,1,0:T(8,128)(2,1)S(1)}, u32[]{:S(2)}, u32[]{:S(2)}) async-start(bf16[16,16,8,128]{3,2,1,0:T(8,128)(2,1)} %broadcast_in_dim.22), calls=%async_computation.4 | async-start | bytes 1048576 | tf_op jit(solution)/shard_map/all_to_all | solution.py:30
  128.8 16.8 %all-to-all-done.4.tile_ref = bf16[16,16,8,128]{3,2,1,0:T(8,128)(2,1)S(1)} async-done(((bf16[16,16,8,128]{3,2,1,0:T(8,128)(2,1)}), bf16[16,16,8,128]{3,2,1,0:T(8,128)(2,1)S(1)}, u32[]{:S(2)}, u32[]{:S(2)}) %all-to-all-start.4) | async-done | bytes 524320 | tf_op jit(solution)/shard_map/all_to_all | solution.py:30
  146.4 3.3 %shard_map.176 = bf16[16,16,8,128]{3,2,1,0:T(8,128)(2,1)} custom-call(bf16[16,16,8,128]{3,2,1,0:T(8,128)(2,1)} %copy-done.1, f32[16,16,128]{2,1,0:T(8,128)} %copy.245.line_ref), custom_call_target="tpu_custom_call" | custom-call | flops 8388608 | bytes 1048576 | tf_op jit(solution)/shard_map/pallas_call | solution.py:71
  149.7 5.1 %all-to-all-start.5 = ((bf16[16,16,8,128]{3,2,1,0:T(8,128)(2,1)}), bf16[16,16,8,128]{3,2,1,0:T(8,128)(2,1)S(1)}, u32[]{:S(2)}, u32[]{:S(2)}) async-start(bf16[16,16,8,128]{3,2,1,0:T(8,128)(2,1)} %shard_map.176), calls=%async_computation.5 | async-start | bytes 1048576 | tf_op jit(solution)/shard_map/all_to_all | solution.py:30
  155.0 13.3 %all-to-all-done.5 = bf16[16,16,8,128]{3,2,1,0:T(8,128)(2,1)S(1)} async-done(((bf16[16,16,8,128]{3,2,1,0:T(8,128)(2,1)}), bf16[16,16,8,128]{3,2,1,0:T(8,128)(2,1)S(1)}, u32[]{:S(2)}, u32[]{:S(2)}) %all-to-all-start.5) | async-done | bytes 524320 | tf_op jit(solution)/shard_map/all_to_all | solution.py:30
  170.5 16.9 %all_to_all.40.tile_ref = bf16[16,16,8,128]{3,2,1,0:T(8,128)(2,1)S(1)} all-to-all(bf16[16,16,8,128]{3,2,1,0:T(8,128)(2,1)S(1)} %broadcast_in_dim.23), channel_id=1, replica_groups={{0,2,4,6,8,10,12,14,16,18,20,22,24,26,28,30},{1,3,5,7,9,11,13,15,17,19,..., dimensions={0} | all-to-all | bytes 1048576 | tf_op jit(solution)/shard_map/all_to_all | solution.py:30
  187.4 7.1 %collective-permute-start.2 = (bf16[16,16,8,128]{3,2,1,0:T(8,128)(2,1)S(1)}, bf16[16,16,8,128]{3,2,1,0:T(8,128)(2,1)S(1)}, u32[]{:S(2)}, u32[]{:S(2)}) collective-permute-start(bf16[16,16,8,128]{3,2,1,0:T(8,128)(2,1)S(1)} %all_to_all.40.tile_ref), channel_id=1, source_target_pairs={{0,1},{1,0},{2,3},{3,2},{4,5},{5,4},{6,7},{7,6},{8,9},{9,8},{10,11... | collective-permute-start | bytes 1572872 | tf_op jit(solution)/shard_map/ppermute | solution.py:176
  194.6 2.6 %shard_map.177 = bf16[16,8,8,128]{3,2,1,0:T(8,128)(2,1)} custom-call(bf16[16,16,8,128]{3,2,1,0:T(8,128)(2,1)} %copy-done.2, f32[8,16,128]{2,1,0:T(8,128)} %get-tuple-element.22.line_ref), custom_call_target="tpu_custom_call" | custom-call | flops 4194304 | bytes 786432 | tf_op jit(solution)/shard_map/pallas_call | solution.py:71
  197.9 2.6 %shard_map.178 = bf16[16,8,8,128]{3,2,1,0:T(8,128)(2,1)} custom-call(bf16[16,16,8,128]{3,2,1,0:T(8,128)(2,1)} %copy-done.5, f32[8,16,128]{2,1,0:T(8,128)} %get-tuple-element.22.line_ref), custom_call_target="tpu_custom_call" | custom-call | flops 4194304 | bytes 786432 | tf_op jit(solution)/shard_map/pallas_call | solution.py:71
  200.5 1.1 select_bitcast_fusion.1
  202.5 7.3 %all-to-all-start.7 = ((bf16[16,2,8,8,128]{4,3,2,1,0:T(8,128)(2,1)}), bf16[16,2,8,8,128]{4,3,2,1,0:T(8,128)(2,1)S(1)}, u32[]{:S(2)}, u32[]{:S(2)}) async-start(bf16[16,2,8,8,128]{4,3,2,1,0:T(8,128)(2,1)} %copy.259), calls=%async_computation.7 | async-start | bytes 1048576 | tf_op jit(solution)/shard_map/all_to_all | solution.py:30
  210.0 17.6 %all-to-all-done.7 = bf16[16,2,8,8,128]{4,3,2,1,0:T(8,128)(2,1)S(1)} async-done(((bf16[16,2,8,8,128]{4,3,2,1,0:T(8,128)(2,1)}), bf16[16,2,8,8,128]{4,3,2,1,0:T(8,128)(2,1)S(1)}, u32[]{:S(2)}, u32[]{:S(2)}) %all-to-all-start.7) | async-done | bytes 524320 | tf_op jit(solution)/shard_map/all_to_all | solution.py:30
  (121 shorter events, 19.9 us)
Async XLA Ops:
  0.6 106.8 %copy-start = (bf16[1024,128]{1,0:T(8,128)(2,1)S(1)}, bf16[1024,128]{1,0:T(8,128)(2,1)}, u32[]{:S(2)}) copy-start(bf16[1024,128]{1,0:T(8,128)(2,1)} %param.27) | copy-start | bytes 786436
  0.6 35.8 %copy-start.3 = (bf16[8,16,256]{2,1,0:T(8,128)(2,1)S(1)}, bf16[8,16,256]{2,1,0:T(8,128)(2,1)}, u32[]{:S(2)}) copy-start(bf16[8,16,256]{2,1,0:T(8,128)(2,1)} %param.17) | copy-start | bytes 196612
  0.7 35.8 %copy-start.7 = (bf16[256,256]{1,0:T(8,128)(2,1)S(1)}, bf16[256,256]{1,0:T(8,128)(2,1)}, u32[]{:S(2)}) copy-start(bf16[256,256]{1,0:T(8,128)(2,1)} %param.19) | copy-start | bytes 393220
  5.0 18.8 %all-to-all-start.1 = ((bf16[32,8,128]{2,1,0:T(8,128)(2,1)}), bf16[32,8,128]{2,1,0:T(8,128)(2,1)S(1)}, u32[]{:S(2)}, u32[]{:S(2)}) async-start(bf16[32,8,128]{2,1,0:T(8,128)(2,1)} %broadcast_in_dim.18), calls=%async_computation.1 | async-start | bytes 131072 | tf_op jit(solution)/shard_map/all_to_all | solution.py:30
  24.9 38.7 %all-to-all-start = ((bf16[16,8,16,256]{3,2,1,0:T(8,128)(2,1)}), bf16[16,8,16,256]{3,2,1,0:T(8,128)(2,1)S(1)}, u32[]{:S(2)}, u32[]{:S(2)}) async-start(bf16[16,8,16,256]{3,2,1,0:T(8,128)(2,1)} %broadcast_in_dim.16), calls=%async_computation | async-start | bytes 2097152 | tf_op jit(solution)/shard_map/all_to_all | solution.py:30
  36.5 27.2 %copy-start.9 = (bf16[256,256]{1,0:T(8,128)(2,1)S(1)}, bf16[256,256]{1,0:T(8,128)(2,1)}, u32[]{:S(2)}) copy-start(bf16[256,256]{1,0:T(8,128)(2,1)} %param.21) | copy-start | bytes 393220
  36.5 27.2 %copy-start.10 = (bf16[256,256]{1,0:T(8,128)(2,1)S(1)}, bf16[256,256]{1,0:T(8,128)(2,1)}, u32[]{:S(2)}) copy-start(bf16[256,256]{1,0:T(8,128)(2,1)} %param.20) | copy-start | bytes 393220
  69.2 2.0 copy-start.16
  69.2 10.5 %copy-start.17 = (bf16[256,32]{0,1:T(8,128)(2,1)S(1)}, bf16[256,32]{0,1:T(8,128)(2,1)}, u32[]{:S(2)}) copy-start(bf16[256,32]{0,1:T(8,128)(2,1)} %param.25) | copy-start | bytes 49156
  71.0 35.4 %copy-start.11 = (bf16[8,16,256]{2,1,0:T(8,128)(2,1)}, bf16[8,16,256]{2,1,0:T(8,128)(2,1)S(1)}, u32[]{:S(2)}) copy-start(bf16[8,16,256]{2,1,0:T(8,128)(2,1)S(1)} %get-tuple-element.31) | copy-start | bytes 196612
  72.2 17.0 %all-to-all-start.3 = ((bf16[32,8,256]{2,1,0:T(8,128)(2,1)}), bf16[32,8,256]{2,1,0:T(8,128)(2,1)S(1)}, u32[]{:S(2)}, u32[]{:S(2)}) async-start(bf16[32,8,256]{2,1,0:T(8,128)(2,1)} %bitcast.18), calls=%async_computation.3 | async-start | bytes 262144 | tf_op jit(solution)/shard_map/all_to_all | solution.py:30
  89.9 15.4 %all-to-all-start.2 = ((bf16[32,8,512]{2,1,0:T(8,128)(2,1)}), bf16[32,8,512]{2,1,0:T(8,128)(2,1)S(1)}, u32[]{:S(2)}, u32[]{:S(2)}) async-start(bf16[32,8,512]{2,1,0:T(8,128)(2,1)} %broadcast_in_dim.20), calls=%async_computation.2 | async-start | bytes 524288 | tf_op jit(solution)/shard_map/all_to_all | solution.py:30
  93.9 0.7 collective-permute-start
  106.1 1.6 copy-start.4
  106.1 1.9 copy-start.8
  108.3 4.3 %collective-permute-start.1 = (bf16[24,8,128]{2,0,1:T(8,128)(2,1)S(1)}, bf16[24,8,128]{2,0,1:T(8,128)(2,1)S(1)}, u32[]{:S(2)}, u32[]{:S(2)}) collective-permute-start(bf16[24,8,128]{2,0,1:T(8,128)(2,1)S(1)} %pad_maximum_fusion.1), channel_id=1, source_target_pairs={{0,1},{1,0},{2,3},{3,2},{4,5},{5,4},{6,7},{7,6},{8,9},{9,8},{10,11... | collective-permute-start | bytes 147464 | tf_op jit(solution)/shard_map/ppermute | solution.py:165
  112.7 42.1 %copy-start.14 = (bf16[128,128]{1,0:T(8,128)(2,1)S(1)}, bf16[128,128]{1,0:T(8,128)(2,1)}, u32[]{:S(2)}) copy-start(bf16[128,128]{1,0:T(8,128)(2,1)} %param.29) | copy-start | bytes 98308
  113.6 32.1 %all-to-all-start.4 = ((bf16[16,16,8,128]{3,2,1,0:T(8,128)(2,1)}), bf16[16,16,8,128]{3,2,1,0:T(8,128)(2,1)S(1)}, u32[]{:S(2)}, u32[]{:S(2)}) async-start(bf16[16,16,8,128]{3,2,1,0:T(8,128)(2,1)} %broadcast_in_dim.22), calls=%async_computation.4 | async-start | bytes 1048576 | tf_op jit(solution)/shard_map/all_to_all | solution.py:30
  128.1 41.0 %copy-start.12 = (bf16[128,128]{1,0:T(8,128)(2,1)S(1)}, bf16[128,128]{1,0:T(8,128)(2,1)}, u32[]{:S(2)}) copy-start(bf16[128,128]{1,0:T(8,128)(2,1)} %param.30) | copy-start | bytes 98308
  128.1 41.4 %copy-start.6 = (bf16[128,512]{1,0:T(8,128)(2,1)S(1)}, bf16[128,512]{1,0:T(8,128)(2,1)}, u32[]{:S(2)}) copy-start(bf16[128,512]{1,0:T(8,128)(2,1)} %param.31) | copy-start | bytes 393220
  145.6 0.8 copy-start.1
  149.7 18.6 %all-to-all-start.5 = ((bf16[16,16,8,128]{3,2,1,0:T(8,128)(2,1)}), bf16[16,16,8,128]{3,2,1,0:T(8,128)(2,1)S(1)}, u32[]{:S(2)}, u32[]{:S(2)}) async-start(bf16[16,16,8,128]{3,2,1,0:T(8,128)(2,1)} %shard_map.176), calls=%async_computation.5 | async-start | bytes 1048576 | tf_op jit(solution)/shard_map/all_to_all | solution.py:30
  187.4 7.1 %copy-start.2 = (bf16[16,16,8,128]{3,2,1,0:T(8,128)(2,1)}, bf16[16,16,8,128]{3,2,1,0:T(8,128)(2,1)S(1)}, u32[]{:S(2)}) copy-start(bf16[16,16,8,128]{3,2,1,0:T(8,128)(2,1)S(1)} %all_to_all.40.tile_ref) | copy-start | bytes 1572868
  187.4 9.7 %collective-permute-start.2 = (bf16[16,16,8,128]{3,2,1,0:T(8,128)(2,1)S(1)}, bf16[16,16,8,128]{3,2,1,0:T(8,128)(2,1)S(1)}, u32[]{:S(2)}, u32[]{:S(2)}) collective-permute-start(bf16[16,16,8,128]{3,2,1,0:T(8,128)(2,1)S(1)} %all_to_all.40.tile_ref), channel_id=1, source_target_pairs={{0,1},{1,0},{2,3},{3,2},{4,5},{5,4},{6,7},{7,6},{8,9},{9,8},{10,11... | collective-permute-start | bytes 1572872 | tf_op jit(solution)/shard_map/ppermute | solution.py:176
  197.1 0.8 copy-start.5
  200.5 9.3 %copy-start.15 = (bf16[128,128]{1,0:T(8,128)(2,1)S(1)}, bf16[128,128]{1,0:T(8,128)(2,1)}, u32[]{:S(2)}) copy-start(bf16[128,128]{1,0:T(8,128)(2,1)} %param.32) | copy-start | bytes 98308
  201.6 26.8 %copy-start.13 = (bf16[128,128]{1,0:T(8,128)(2,1)S(1)}, bf16[128,128]{1,0:T(8,128)(2,1)}, u32[]{:S(2)}) copy-start(bf16[128,128]{1,0:T(8,128)(2,1)} %param.33) | copy-start | bytes 98308
  202.5 25.1 %all-to-all-start.7 = ((bf16[16,2,8,8,128]{4,3,2,1,0:T(8,128)(2,1)}), bf16[16,2,8,8,128]{4,3,2,1,0:T(8,128)(2,1)S(1)}, u32[]{:S(2)}, u32[]{:S(2)}) async-start(bf16[16,2,8,8,128]{4,3,2,1,0:T(8,128)(2,1)} %copy.259), calls=%async_computation.7 | async-start | bytes 1048576 | tf_op jit(solution)/shard_map/all_to_all | solution.py:30

commit v2 on v1

v2 whole, which is shorter than its diff:
```python
import functools

import jax
import jax.numpy as jnp
from jax import lax
from jax.experimental import pallas as pl
from jax.experimental.pallas import tpu as pltpu
from jax.sharding import PartitionSpec as P

F32 = jnp.float32
BF16 = jnp.bfloat16
ROWS, COLS, CHIPS = 16, 32, 16
SAME_CORE = [[2 * chip + core for chip in range(CHIPS)] for core in range(2)]
SWAP = [(c, c ^ 1) for c in range(COLS)]
TURN = [
    (r * COLS + c, (c // 2) * COLS + 2 * r + c % 2) for r in range(ROWS) for c in range(COLS)
]


def layer_norm(values):
    values = values.astype(F32)
    center = values - jnp.mean(values, axis=-1, keepdims=True)
    variance = jnp.mean(center * center, axis=-1, keepdims=True)
    return center * lax.rsqrt(variance + 1e-05)


def sigmoid(values):
    return 1.0 / (1.0 + jnp.exp(-values))


def project(values, weight):
    return jnp.dot(values, weight, preferred_element_type=F32)


def exchange(chunks, axis, groups=None):
    return lax.all_to_all(chunks, axis, 0, 0, axis_index_groups=groups)


def spread(block, axis, count, groups=None):
    return exchange(jnp.broadcast_to(block[None], (count,) + block.shape), axis, groups)


def kernel_call(body, outs, args, scratch=(), flops=0, aliases=None):
    shapes = [jax.ShapeDtypeStruct(s, d) for s, d in outs]
    vmem = pl.BlockSpec(memory_space=pltpu.VMEM)
    size = sum(a.size * a.dtype.itemsize for a in args)
    size += sum(s.size * jnp.dtype(s.dtype).itemsize for s in shapes)
    return pl.pallas_call(
        body,
        out_shape=shapes,
        in_specs=[vmem] * len(args),
        out_specs=[vmem] * len(shapes),
        scratch_shapes=[pltpu.VMEM(s, d) for s, d in scratch],
        input_output_aliases=aliases or {},
        compiler_params=pltpu.CompilerParams(vmem_limit_bytes=40 * 2**20),
        cost_estimate=pl.CostEstimate(flops=flops, bytes_accessed=size, transcendentals=0),
    )(*args)


def double_up(block):
    place = lax.axis_index("col")
    held = block
    for bit in (1, 2, 4, 8, 16):
        met = lax.ppermute(held, "col", [(c, c ^ bit) for c in range(COLS)])
        lower = jnp.where((place & bit) == 0, held, met)
        upper = jnp.where((place & bit) == 0, met, held)
        held = jnp.concatenate([lower, upper], axis=0)
    return held


def normed_kernel(x_ref, chunks_ref):
    normed = layer_norm(x_ref[...]).astype(BF16)
    for member in range(chunks_ref.shape[0]):
        chunks_ref[member] = normed


def start_kernel(x_ref, pair_ref, bias_w_ref, query_w_ref, gate_w_ref, bias_ref, query_ref, gate_ref):
    seqs, rows, channels = x_ref.shape
    height, width, depth = pair_ref.shape
    heads = bias_w_ref.shape[1]
    pair_normed = layer_norm(pair_ref[...].reshape(height * width, depth)).astype(BF16)
    wide = jnp.concatenate(
        [jnp.broadcast_to(bias_w_ref[:, h : h + 1], (depth, rows)) for h in range(heads)], axis=1
    )
    every = project(pair_normed, wide).reshape(height, width, heads * rows)
    lane = lax.broadcasted_iota(jnp.int32, (width, heads * rows), 1) % rows
    bias = jnp.zeros((width, heads * rows), F32)
    for i in range(height):
        bias = jnp.where(lane == i, every[i], bias)
    bias_ref[...] = bias.astype(BF16)
    normed = layer_norm(x_ref[...].reshape(seqs * rows, channels)).astype(BF16)
    query_ref[...] = project(normed, query_w_ref[...]).astype(BF16).reshape(seqs, rows, channels)
    gate_ref[...] = sigmoid(project(normed, gate_w_ref[...]))


def attention_kernel(
    heads, every_ref, bias_ref, query_ref, gate_ref, x_ref, both_w_ref, out_w_ref, factor_w_ref,
    new_ref, left_ref, right_ref, gated_ref, factor_ref,
):
    members, seqs, rows, channels = every_ref.shape
    head_dim = channels // heads
    full = members * rows
    bias = bias_ref[...].astype(F32).T
    head_of = lax.broadcasted_iota(jnp.int32, (rows, channels), 1) // head_dim

    def one(s, carry):
        tokens = every_ref[:, s].reshape(full, channels)
        both = project(tokens, both_w_ref[...]).astype(BF16)
        query = query_ref[s]
        spread_query = jnp.concatenate(
            [jnp.where(head_of == h, query, jnp.zeros_like(query)) for h in range(heads)], axis=0
        )
        scores = lax.dot_general(
            spread_query, both[:, :channels], (((1,), (1,)), ((), ())), preferred_element_type=F32
        )
        scores = scores * head_dim ** (-0.5) + bias
        expo = jnp.exp(scores - jnp.max(scores, axis=-1, keepdims=True))
        weights = (expo / jnp.sum(expo, axis=-1, keepdims=True)).astype(BF16)
        mixed = project(weights, both[:, channels:])
        attended = mixed[0:rows]
        for h in range(1, heads):
            attended = jnp.where(head_of == h, mixed[h * rows : (h + 1) * rows], attended)
        place = pl.ds(pl.multiple_of(s * rows, rows), rows)
        gated_ref[place, :] = (gate_ref[place, :] * attended).astype(BF16)
        return carry

    lax.fori_loop(0, seqs, one, 0, unroll=2)
    tokens = x_ref[...].reshape(seqs * rows, channels).astype(F32)
    new = (tokens + project(gated_ref[...], out_w_ref[...])).astype(BF16)
    new_ref[...] = new.reshape(seqs, rows, channels)
    factor_ref[...] = project(layer_norm(new).astype(BF16), factor_w_ref[...])
    width = left_ref.shape[1] // rows
    pieces = [factor_ref[pl.ds(i, seqs, stride=rows), :] for i in range(rows)]
    left_ref[...] = jnp.concatenate([p[:, :width] for p in pieces], axis=1).astype(BF16)
    right = jnp.concatenate([p[:, width : 2 * width] for p in pieces], axis=1).astype(BF16)
    half = right.shape[1] // 2
    right_ref[0] = right[:, :half]
    right_ref[1] = right[:, half:]


def edge_parts(pair, in_w_ref, gate_w_ref):
    normed = layer_norm(pair).astype(BF16)
    proj = project(normed, in_w_ref[...])
    width = in_w_ref.shape[1] // 4
    left = sigmoid(proj[:, :width]) * proj[:, width : 2 * width]
    right = sigmoid(proj[:, 2 * width : 3 * width]) * proj[:, 3 * width :]
    return left, right, sigmoid(project(normed, gate_w_ref[...]))


def outer_kernel(
    left_ref, right_ref, pair_ref, outer_w_ref, in_w_ref, gate_w_ref,
    pair_out, gate_out, left_out, right_out, products_ref, update_ref, right_scr,
):
    total = left_ref.shape[0]
    rows, cols, depth = pair_ref.shape
    factor = left_ref.shape[1] // rows
    products = lax.dot_general(
        left_ref[...], right_ref[...], (((0,), (0,)), ((), ())), preferred_element_type=F32
    ) * (1.0 / total)
    slabs, _, slab = products_ref.shape
    per_slab = slab // factor
    outer = []
    for part in range(slabs):
        products_ref[part] = products[:, part * slab : (part + 1) * slab]
        lines = [
            products_ref[part, pl.ds(a, rows, stride=factor), :].astype(BF16) for a in range(factor)
        ]
        for j in range(per_slab):
            pieces = [line[:, j * factor : (j + 1) * factor] for line in lines]
            outer.append(jnp.concatenate(pieces, axis=1))
    outer = jnp.concatenate(outer, axis=0)
    update_ref[...] = project(outer, outer_w_ref[...])
    update = jnp.concatenate(
        [update_ref[pl.ds(i, cols, stride=rows), :] for i in range(rows)], axis=0
    )
    pair = (pair_ref[...].reshape(rows * cols, depth).astype(F32) + update).astype(BF16)
    pair_out[...] = pair
    left, right, gate = edge_parts(pair, in_w_ref, gate_w_ref)
    gate_out[...] = gate
    left_out[...] = left.astype(BF16).reshape(rows, cols, depth)
    right_scr[...] = right
    for k in range(cols):
        line = right_scr[pl.ds(k, rows, stride=cols), :].astype(BF16)
        right_out[0, k] = line[:cols]
        right_out[1, k] = line[cols:]


def partial_kernel(axis, tile_ref, *refs):
    line_refs, out_ref, scr = refs[:-2], refs[-2], refs[-1]
    groups, depth = tile_ref.shape[:2]
    lines = out_ref.shape[1]
    start = 0
    for line_ref in line_refs:
        size = line_ref.shape[1]
        scr[:, start : start + size, :] = line_ref[...].astype(F32)
        start += size

    def one(g, carry):
        tiles = [[tile_ref[2 * g + u, k].astype(F32) for k in range(depth)] for u in range(2)]
        for n in range(lines):
            totals = [None, None]
            for k in range(depth):
                line = scr[n, k : k + 1, :]
                for u in range(2):
                    term = tiles[u][k] * line
                    totals[u] = term if k == 0 else totals[u] + term
            for u in range(2):
                out_ref[2 * g + u, n] = totals[u].astype(BF16)
        return carry

    lax.fori_loop(0, groups // 2, one, 0)


def partial_sums(tiles, *lines):
    groups, depth, height, width = tiles.shape
    count = lines[0].shape[0]
    return kernel_call(
        functools.partial(partial_kernel, 0),
        [((groups, count, height, width), BF16)],
        (tiles,) + lines,
        scratch=[((count, depth, width), F32)],
        flops=2 * groups * count * height * width * depth,
    )[0]


def added(partial_ref):
    total = partial_ref[0].astype(F32)
    for member in range(1, partial_ref.shape[0]):
        total = total + partial_ref[member].astype(F32)
    return total


def middle_kernel(
    partial_ref, pair_ref, gate_ref, out_w_ref, in_w_ref, next_gate_w_ref,
    pair_out, gate_out, chunks_out, line_out, right_scr,
):
    rows, cols, depth = partial_ref.shape[1:]
    combined = added(partial_ref).reshape(rows * cols, depth)
    update = project(layer_norm(combined).astype(BF16), out_w_ref[...])
    pair = (pair_ref[...].astype(F32) + gate_ref[...] * update).astype(BF16)
    pair_out[...] = pair
    left, right, gate = edge_parts(pair, in_w_ref, next_gate_w_ref)
    gate_out[...] = gate
    left = left.astype(BF16).reshape(rows, cols, depth)
    for member in range(chunks_out.shape[0]):
        chunks_out[member] = left
    right_scr[...] = right
    for j in range(cols):
        line_out[j] = right_scr[pl.ds(j, rows, stride=cols), :].astype(BF16)


def last_kernel(partial_ref, pair_ref, gate_ref, out_w_ref, new_ref, scr):
    halves, cols, tall, depth = partial_ref.shape[1:]
    scr[...] = added(partial_ref).reshape(halves * cols * tall, depth)
    combined = jnp.concatenate(
        [
            scr[pl.ds(half * cols * tall + i, cols, stride=tall), :]
            for half in range(halves)
            for i in range(tall)
        ],
        axis=0,
    )
    update = project(layer_norm(combined).astype(BF16), out_w_ref[...])
    new = (pair_ref[...].astype(F32) + gate_ref[...] * update).astype(BF16)
    new_ref[...] = new.reshape(new_ref.shape)


def on_device(
    alignment,
    pair_features,
    query_matrix,
    key_matrix,
    value_matrix,
    gate_matrix,
    output_matrix,
    bias_weight,
    left_factor_weight,
    right_factor_weight,
    outer_weight,
    outgoing_project,
    outgoing_gate,
    outgoing_output,
    incoming_project,
    incoming_gate,
    incoming_output,
):
    seqs, rows, channels = alignment.shape
    cols, depth = pair_features.shape[1:]
    heads = bias_weight.shape[1]
    factor = left_factor_weight.shape[1]
    places = rows * cols
    full = COLS * cols
    core = lax.axis_index("col") % 2

    chunks = kernel_call(normed_kernel, [((ROWS, seqs, rows, channels), BF16)], (alignment,))[0]
    everyone = exchange(chunks, "row")
    bias, queries, gates = kernel_call(
        start_kernel,
        [((cols, heads * rows), BF16), ((seqs, rows, channels), BF16), ((seqs * rows, channels), F32)],
        (alignment, pair_features, bias_weight, query_matrix, gate_matrix),
    )
    bias = double_up(bias[None]).reshape(full, heads * rows)
    both_weights = jnp.concatenate([key_matrix, value_matrix], axis=1)
    spare = jnp.zeros((channels, 128 - 2 * factor), BF16)
    factor_weights = jnp.concatenate([left_factor_weight, right_factor_weight, spare], axis=1)
    new_alignment, left, right = kernel_call(
        functools.partial(attention_kernel, heads),
        [
            ((seqs, rows, channels), BF16),
            ((seqs, rows * factor), BF16),
            ((2, seqs, cols * factor), BF16),
        ],
        (everyone, bias, queries, gates, alignment, both_weights, output_matrix, factor_weights),
        scratch=[((seqs * rows, channels), BF16), ((seqs * rows, 128), F32)],
    )

    mine = lax.dynamic_index_in_dim(right, core, 0, keepdims=False)
    theirs = lax.dynamic_index_in_dim(right, 1 - core, 0, keepdims=False)
    swapped = lax.ppermute(theirs, "col", SWAP)
    both = jnp.where(
        core == 0, jnp.concatenate([mine, swapped], axis=0), jnp.concatenate([swapped, mine], axis=0)
    )
    left, both = lax.optimization_barrier((left, both))
    turned = lax.ppermute(both, ("row", "col"), TURN)
    left_all = spread(left, "col", COLS)
    turned, left_all = lax.optimization_barrier((turned, left_all))
    right_all = spread(turned, "row", ROWS).reshape(COLS * seqs, cols * factor)
    left_all = left_all.reshape(COLS * seqs, rows * factor)
    pair_one, gate_one, left_edge, right_edge = kernel_call(
        outer_kernel,
        [
            ((places, depth), BF16),
            ((places, depth), F32),
            ((rows, cols, depth), BF16),
            ((2, cols, cols, depth), BF16),
        ],
        (left_all, right_all, pair_features, outer_weight, outgoing_project, outgoing_gate),
        scratch=[
            ((cols * factor // 128, rows * factor, 128), F32),
            ((places, depth), F32),
            ((places, depth), F32),
        ],
    )

    mine = lax.dynamic_index_in_dim(right_edge, core, 0, keepdims=False)
    theirs = lax.dynamic_index_in_dim(right_edge, 1 - core, 0, keepdims=False)
    swapped = lax.ppermute(jnp.concatenate([left_edge, theirs], axis=0), "col", SWAP)
    tiles = jnp.concatenate([mine, swapped[rows:]], axis=0)
    partial = partial_sums(spread(tiles, "row", ROWS), left_edge, swapped[:rows])
    partial = exchange(partial, "col", SAME_CORE)
    pair_two, gate_two, chunks, lines = kernel_call(
        middle_kernel,
        [
            ((places, depth), BF16),
            ((places, depth), F32),
            ((CHIPS, rows, cols, depth), BF16),
            ((cols, rows, depth), BF16),
        ],
        (partial, pair_one, gate_one, outgoing_output, incoming_project, incoming_gate),
        scratch=[((places, depth), F32)],
    )

    own = exchange(chunks, "col", SAME_CORE)
    other = lax.ppermute(own, "col", SWAP)
    own_sums = partial_sums(own, lines)
    other_sums = partial_sums(other, lines)
    first = jnp.where(core == 0, own_sums, other_sums)
    second = jnp.where(core == 0, other_sums, own_sums)
    partial = exchange(jnp.stack([first, second], axis=1), "row")
    new_pair = kernel_call(
        last_kernel,
        [((rows, cols, depth), BF16)],
        (partial, pair_two, gate_two, incoming_output),
        scratch=[((places, depth), F32)],
    )[0]
    return (new_alignment, new_pair)


def solution(mesh):
    rep = (P(),) * 15
    return jax.shard_map(
        on_device,
        mesh=mesh,
        in_specs=(P("col", "row", None), P("row", "col", None)) + rep,
        out_specs=(P("col", "row", None), P("row", "col", None)),
        check_vma=False,
    )
```

time: 230 us -> 201 us (0.87)
  blocking collectives: 16.9 us -> 78.2 us
  waiting for transfers between devices: 99.1 us -> 40 us
  starting transfers between devices: 71.6 us -> 62.6 us
  other arithmetic: 9.28 us -> 0.3 us
  matrix products: 8.44 us -> 0 us
  local copies, waits for them, and re-layouts: 14 us -> 6.06 us
  Pallas kernels: 8.4 us -> 11.8 us
    all_to_all x7 -> x3, waiting for transfers between devices: 98.3 us -> 32 us  [exchange(): return lax.all_to_all(chunks, axis, 0, 0, axis_index_groups=groups)]
    all_to_all x1 -> x4, blocking collectives: 16.9 us -> 78.2 us  [exchange(): return lax.all_to_all(chunks, axis, 0, 0, axis_index_groups=groups)]
    all_to_all x7 -> x3, starting transfers between devices: 60.3 us -> 18.6 us  [exchange(): return lax.all_to_all(chunks, axis, 0, 0, axis_index_groups=groups)]
    ppermute x1 -> x7, starting transfers between devices: 0.67 us -> 32.2 us  [the longest x5 26 us: double_up(): met = lax.ppermute(held, 'col', [(c, c ^ bit) for c in range(COLS)])]
    dot_general x16 -> x0, matrix products: 8.44 us -> none  [the longest x12 4.23 us: project(): return jnp.dot(values, weight, preferred_element_type=F32)]
    ppermute x1 -> x7, waiting for transfers between devices: 0.01 us -> 6.3 us  [the longest x5 5.5 us: double_up(): met = lax.ppermute(held, 'col', [(c, c ^ bit) for c in range(COLS)])]
    reduce_sum x13 -> x0, other arithmetic: 4.98 us -> none  [the longest x7 2.75 us: layer_norm(): variance = jnp.mean(center * center, axis=-1, keepdims=True)]
    pallas_call x3 -> x9, Pallas kernels: 8.4 us -> 11.8 us  [kernel_call(): pl.pallas_call(body, out_shape=shapes, in_specs=[vmem] * len(args), out_s...]
  transfers between devices with their start and end apart: 10 -> 12, of which waited for: 8 -> 10; matrix products, arithmetic and copies ran while one was open for 3% -> 0% of each run, Pallas kernels for 1% -> 1%
where the time goes in v2:
time: 201 us; the launch traced here: 200 us
  blocking collectives  78.2 us (39%)
  starting transfers between devices  62.6 us (31%)
  waiting for transfers between devices  40 us (20%)
  Pallas kernels  11.8 us (6%)
  local copies, waits for them, and re-layouts  6.06 us (3%)
    all_to_all x4, blocking collectives, exchange(): return lax.all_to_all(chunks, axis, 0, 0, axis_index_groups=groups)  78.2 us
    all_to_all x3, waiting for transfers between devices, exchange(): return lax.all_to_all(chunks, axis, 0, 0, axis_index_groups=groups)  32 us
    ppermute x5, starting transfers between devices, double_up(): met = lax.ppermute(held, 'col', [(c, c ^ bit) for c in range(COLS)])  26 us
    all_to_all x3, starting transfers between devices, exchange(): return lax.all_to_all(chunks, axis, 0, 0, axis_index_groups=groups)  18.6 us
    pallas_call x9, Pallas kernels, kernel_call(): pl.pallas_call(body, out_shape=shapes, in_specs=[vmem] * len(args), out_s...  11.8 us
    ppermute x1, starting transfers between devices, on_device(): other = lax.ppermute(own, 'col', SWAP)  7.19 us
    ppermute x5, waiting for transfers between devices, double_up(): met = lax.ppermute(held, 'col', [(c, c ^ bit) for c in range(COLS)])  5.5 us
    ppermute x1, starting transfers between devices, on_device(): swapped = lax.ppermute(theirs, 'col', SWAP)  5.34 us
  transfers between devices with their start and end apart: 12, of which 10 were waited for; matrix products, arithmetic and copies ran while one was open for 0% of the time, Pallas kernels for 1%

profile of v2, /device:TPU:1, one launch (start us, length us, event | category | flops | bytes accessed | tf_op | source)
XLA Modules:
  0.0 200.0 jit_solution(8107043274938278707)
XLA Ops:
  1.5 0.8 copy-done
  2.3 0.9 copy-done.4
  3.2 0.9 copy-done.5
  4.8 8.8 %collective-permute-start = (bf16[1,8,128]{2,1,0:T(8,128)(2,1)S(1)}, bf16[1,8,128]{2,1,0:T(8,128)(2,1)S(1)}, u32[]{:S(2)}, u32[]{:S(2)}) collective-permute-start(bf16[1,8,128]{2,1,0:T(8,128)(2,1)S(1)} %bitcast.23), channel_id=1, source_target_pairs={{0,1},{1,0},{2,3},{3,2},{4,5},{5,4},{6,7},{7,6},{8,9},{9,8},{10,11... | collective-permute-start | bytes 6152 | tf_op jit(solution)/shard_map/ppermute | solution.py:64
  13.6 1.3 shard_map.176
  14.8 7.2 %all-to-all-start = ((bf16[16,8,16,256]{3,2,1,0:T(8,128)(2,1)}), bf16[16,8,16,256]{3,2,1,0:T(8,128)(2,1)S(1)}, u32[]{:S(2)}, u32[]{:S(2)}) async-start(bf16[16,8,16,256]{3,2,1,0:T(8,128)(2,1)} %shard_map.176), calls=%async_computation | async-start | bytes 2097152 | tf_op jit(solution)/shard_map/all_to_all | solution.py:36
  22.1 2.2 %collective-permute-start.1 = (bf16[2,8,128]{2,1,0:T(8,128)(2,1)S(1)}, bf16[2,8,128]{2,1,0:T(8,128)(2,1)S(1)}, u32[]{:S(2)}, u32[]{:S(2)}) collective-permute-start(bf16[2,8,128]{2,1,0:T(8,128)(2,1)S(1)} %pad_maximum_fusion.7), channel_id=1, source_target_pairs={{0,2},{1,3},{2,0},{3,1},{4,6},{5,7},{6,4},{7,5},{8,10},{9,11},{10,... | collective-permute-start | bytes 12296 | tf_op jit(solution)/shard_map/ppermute | solution.py:64
  24.4 2.1 %collective-permute-done.1 = bf16[2,8,128]{2,1,0:T(8,128)(2,1)S(1)} collective-permute-done((bf16[2,8,128]{2,1,0:T(8,128)(2,1)S(1)}, bf16[2,8,128]{2,1,0:T(8,128)(2,1)S(1)}, u32[]{:S(2)}, u32[]{:S(2)}) %collective-permute-start.1) | collective-permute-done | bytes 4128 | tf_op jit(solution)/shard_map/ppermute | solution.py:64
  26.5 3.2 %collective-permute-start.2 = (bf16[4,8,128]{2,1,0:T(8,128)(2,1)S(1)}, bf16[4,8,128]{2,1,0:T(8,128)(2,1)S(1)}, u32[]{:S(2)}, u32[]{:S(2)}) collective-permute-start(bf16[4,8,128]{2,1,0:T(8,128)(2,1)S(1)} %pad_maximum_fusion.6), channel_id=1, source_target_pairs={{0,4},{1,5},{2,6},{3,7},{4,0},{5,1},{6,2},{7,3},{8,12},{9,13},{10,... | collective-permute-start | bytes 24584 | tf_op jit(solution)/shard_map/ppermute | solution.py:64
  31.2 4.3 %collective-permute-start.3 = (bf16[8,8,128]{2,1,0:T(8,128)(2,1)S(1)}, bf16[8,8,128]{2,1,0:T(8,128)(2,1)S(1)}, u32[]{:S(2)}, u32[]{:S(2)}) collective-permute-start(bf16[8,8,128]{2,1,0:T(8,128)(2,1)S(1)} %pad_maximum_fusion.5), channel_id=1, source_target_pairs={{0,8},{1,9},{2,10},{3,11},{4,12},{5,13},{6,14},{7,15},{8,0},{9,1},... | collective-permute-start | bytes 49160 | tf_op jit(solution)/shard_map/ppermute | solution.py:64
  35.7 1.3 collective-permute-done.3
  37.0 7.5 %collective-permute-start.4 = (bf16[16,8,128]{2,1,0:T(8,128)(2,1)S(1)}, bf16[16,8,128]{2,1,0:T(8,128)(2,1)S(1)}, u32[]{:S(2)}, u32[]{:S(2)}) collective-permute-start(bf16[16,8,128]{2,1,0:T(8,128)(2,1)S(1)} %pad_maximum_fusion.3), channel_id=1, source_target_pairs={{0,16},{1,17},{2,18},{3,19},{4,20},{5,21},{6,22},{7,23},{8,24},{9,... | collective-permute-start | bytes 98312 | tf_op jit(solution)/shard_map/ppermute | solution.py:64
  44.6 1.5 collective-permute-done.4
  46.1 3.7 %all-to-all-done.every_ref = bf16[16,8,16,256]{3,2,1,0:T(8,128)(2,1)S(1)} async-done(((bf16[16,8,16,256]{3,2,1,0:T(8,128)(2,1)}), bf16[16,8,16,256]{3,2,1,0:T(8,128)(2,1)S(1)}, u32[]{:S(2)}, u32[]{:S(2)}) %all-to-all-start) | async-done | bytes 1048608 | tf_op jit(solution)/shard_map/all_to_all | solution.py:36
  49.9 4.4 %shard_map.178 = (bf16[8,16,256]{2,1,0:T(8,128)(2,1)}, bf16[8,512]{1,0:T(8,128)(2,1)S(1)}, bf16[2,8,256]{2,1,0:T(8,128)(2,1)S(1)}) custom-call(bf16[16,8,16,256]{3,2,1,0:T(8,128)(2,1)S(1)} %all-to-all-done.every_ref, bf16[256,128]{1,0:T(8,128)(2,1)S(1)} %maximum_bitcast_fusion.bias_ref, bf16[8,16,256]{2,1,0:T(8,128)(2,1)S(1)} %get-tuple-element.21.query_ref, ...), custom_call_target="tpu_custom_call" | custom-call | bytes 1916928 | tf_op jit(solution)/shard_map/pallas_call | solution.py:48
  54.3 5.3 %collective-permute-start.5 = (bf16[8,256]{1,0:T(8,128)(2,1)S(1)}, bf16[8,256]{1,0:T(8,128)(2,1)S(1)}, u32[]{:S(2)}, u32[]{:S(2)}) collective-permute-start(bf16[8,256]{1,0:T(8,128)(2,1)S(1)} %get-tuple-element.49), channel_id=1, source_target_pairs={{0,1},{1,0},{2,3},{3,2},{4,5},{5,4},{6,7},{7,6},{8,9},{9,8},{10,11... | collective-permute-start | bytes 12296 | tf_op jit(solution)/shard_map/ppermute | solution.py:319
  61.2 7.8 %all-to-all-start.1 = ((bf16[32,8,512]{2,1,0:T(8,128)(2,1)}), bf16[32,8,512]{2,1,0:T(8,128)(2,1)S(1)}, u32[]{:S(2)}, u32[]{:S(2)}) async-start(bf16[32,8,512]{2,1,0:T(8,128)(2,1)} %broadcast_in_dim.12), calls=%async_computation.1 | async-start | bytes 524288 | tf_op jit(solution)/shard_map/all_to_all | solution.py:36
  69.8 10.6 %all-to-all-done.1 = bf16[32,8,512]{2,1,0:T(8,128)(2,1)S(1)} async-done(((bf16[32,8,512]{2,1,0:T(8,128)(2,1)}), bf16[32,8,512]{2,1,0:T(8,128)(2,1)S(1)}, u32[]{:S(2)}, u32[]{:S(2)}) %all-to-all-start.1) | async-done | bytes 262176 | tf_op jit(solution)/shard_map/all_to_all | solution.py:36
  80.4 20.2 %all_to_all.35 = bf16[16,16,256]{2,1,0:T(8,128)(2,1)S(1)} all-to-all(bf16[16,16,256]{2,1,0:T(8,128)(2,1)S(1)} %broadcast_in_dim.13), channel_id=1, replica_groups=mesh['row'=16,'col'=32] {'row'}, dimensions={0} | all-to-all | bytes 262144 | tf_op jit(solution)/shard_map/all_to_all | solution.py:36
  100.6 1.1 shard_map.179
  101.8 4.7 %collective-permute-start.7 = (bf16[24,8,128]{2,1,0:T(8,128)(2,1)S(1)}, bf16[24,8,128]{2,1,0:T(8,128)(2,1)S(1)}, u32[]{:S(2)}, u32[]{:S(2)}) collective-permute-start(bf16[24,8,128]{2,1,0:T(8,128)(2,1)S(1)} %pad_maximum_fusion.2), channel_id=1, source_target_pairs={{0,1},{1,0},{2,3},{3,2},{4,5},{5,4},{6,7},{7,6},{8,9},{9,8},{10,11... | collective-permute-start | bytes 147464 | tf_op jit(solution)/shard_map/ppermute | solution.py:347
  106.5 0.9 collective-permute-done.7
  107.4 0.9 broadcast_in_dim.28
  108.2 3.6 %all-to-all-start.3 = ((bf16[16,16,8,128]{3,2,1,0:T(8,128)(2,1)}), bf16[16,16,8,128]{3,2,1,0:T(8,128)(2,1)S(1)}, u32[]{:S(2)}, u32[]{:S(2)}) async-start(bf16[16,16,8,128]{3,2,1,0:T(8,128)(2,1)} %broadcast_in_dim.28), calls=%async_computation.3 | async-start | bytes 1048576 | tf_op jit(solution)/shard_map/all_to_all | solution.py:36
  111.8 17.7 %all-to-all-done.3.tile_ref = bf16[16,16,8,128]{3,2,1,0:T(8,128)(2,1)S(1)} async-done(((bf16[16,16,8,128]{3,2,1,0:T(8,128)(2,1)}), bf16[16,16,8,128]{3,2,1,0:T(8,128)(2,1)S(1)}, u32[]{:S(2)}, u32[]{:S(2)}) %all-to-all-start.3) | async-done | bytes 524320 | tf_op jit(solution)/shard_map/all_to_all | solution.py:36
  129.5 1.2 shard_map.180
  130.8 16.2 %all_to_all.36.partial_ref = bf16[16,16,8,128]{3,2,1,0:T(8,128)(2,1)S(1)} all-to-all(bf16[16,16,8,128]{3,2,1,0:T(8,128)(2,1)S(1)} %shard_map.180), channel_id=1, replica_groups={{0,2,4,6,8,10,12,14,16,18,20,22,24,26,28,30},{1,3,5,7,9,11,13,15,17,19,..., dimensions={0} | all-to-all | bytes 1048576 | tf_op jit(solution)/shard_map/all_to_all | solution.py:36
  147.8 16.8 %all_to_all.37.tile_ref = bf16[16,16,8,128]{3,2,1,0:T(8,128)(2,1)S(1)} all-to-all(bf16[16,16,8,128]{3,2,1,0:T(8,128)(2,1)S(1)} %get-tuple-element.34), channel_id=1, replica_groups={{0,2,4,6,8,10,12,14,16,18,20,22,24,26,28,30},{1,3,5,7,9,11,13,15,17,19,..., dimensions={0} | all-to-all | bytes 1048576 | tf_op jit(solution)/shard_map/all_to_all | solution.py:36
  164.6 7.2 %collective-permute-start.8 = (bf16[16,16,8,128]{3,2,1,0:T(8,128)(2,1)S(1)}, bf16[16,16,8,128]{3,2,1,0:T(8,128)(2,1)S(1)}, u32[]{:S(2)}, u32[]{:S(2)}) collective-permute-start(bf16[16,16,8,128]{3,2,1,0:T(8,128)(2,1)S(1)} %all_to_all.37.tile_ref), channel_id=1, source_target_pairs={{0,1},{1,0},{2,3},{3,2},{4,5},{5,4},{6,7},{7,6},{8,9},{9,8},{10,11... | collective-permute-start | bytes 1572872 | tf_op jit(solution)/shard_map/ppermute | solution.py:364
  172.4 0.8 collective-permute-done.8.tile_ref
  174.1 25.0 %all_to_all.38.partial_ref = bf16[16,2,8,8,128]{4,3,2,1,0:T(8,128)(2,1)S(1)} all-to-all(bf16[16,2,8,8,128]{4,3,2,1,0:T(8,128)(2,1)S(1)} %pad_maximum_fusion), channel_id=1, replica_groups=mesh['row'=16,'col'=32] {'row'}, dimensions={0} | all-to-all | bytes 1048576 | tf_op jit(solution)/shard_map/all_to_all | solution.py:36
  199.0 1.0 shard_map.184
  (68 shorter events, 7.7 us)
Async XLA Ops:
  0.6 0.8 copy-start.8
  1.4 0.8 copy-start
  2.3 0.9 copy-start.4
  3.2 0.9 copy-start.5
  4.8 17.3 %collective-permute-start = (bf16[1,8,128]{2,1,0:T(8,128)(2,1)S(1)}, bf16[1,8,128]{2,1,0:T(8,128)(2,1)S(1)}, u32[]{:S(2)}, u32[]{:S(2)}) collective-permute-start(bf16[1,8,128]{2,1,0:T(8,128)(2,1)S(1)} %bitcast.23), channel_id=1, source_target_pairs={{0,1},{1,0},{2,3},{3,2},{4,5},{5,4},{6,7},{7,6},{8,9},{9,8},{10,11... | collective-permute-start | bytes 6152 | tf_op jit(solution)/shard_map/ppermute | solution.py:64
  14.8 35.0 %all-to-all-start = ((bf16[16,8,16,256]{3,2,1,0:T(8,128)(2,1)}), bf16[16,8,16,256]{3,2,1,0:T(8,128)(2,1)S(1)}, u32[]{:S(2)}, u32[]{:S(2)}) async-start(bf16[16,8,16,256]{3,2,1,0:T(8,128)(2,1)} %shard_map.176), calls=%async_computation | async-start | bytes 2097152 | tf_op jit(solution)/shard_map/all_to_all | solution.py:36
  22.1 4.4 %collective-permute-start.1 = (bf16[2,8,128]{2,1,0:T(8,128)(2,1)S(1)}, bf16[2,8,128]{2,1,0:T(8,128)(2,1)S(1)}, u32[]{:S(2)}, u32[]{:S(2)}) collective-permute-start(bf16[2,8,128]{2,1,0:T(8,128)(2,1)S(1)} %pad_maximum_fusion.7), channel_id=1, source_target_pairs={{0,2},{1,3},{2,0},{3,1},{4,6},{5,7},{6,4},{7,5},{8,10},{9,11},{10,... | collective-permute-start | bytes 12296 | tf_op jit(solution)/shard_map/ppermute | solution.py:64
  24.4 5.4 %copy-start.15 = (bf16[256,32]{0,1:T(8,128)(2,1)S(1)}, bf16[256,32]{0,1:T(8,128)(2,1)}, u32[]{:S(2)}) copy-start(bf16[256,32]{0,1:T(8,128)(2,1)} %param.26) | copy-start | bytes 49156
  26.5 4.7 %collective-permute-start.2 = (bf16[4,8,128]{2,1,0:T(8,128)(2,1)S(1)}, bf16[4,8,128]{2,1,0:T(8,128)(2,1)S(1)}, u32[]{:S(2)}, u32[]{:S(2)}) collective-permute-start(bf16[4,8,128]{2,1,0:T(8,128)(2,1)S(1)} %pad_maximum_fusion.6), channel_id=1, source_target_pairs={{0,4},{1,5},{2,6},{3,7},{4,0},{5,1},{6,2},{7,3},{8,12},{9,13},{10,... | collective-permute-start | bytes 24584 | tf_op jit(solution)/shard_map/ppermute | solution.py:64
  29.7 0.7 copy-start.16
  31.2 13.3 %copy-start.13 = (bf16[256,256]{1,0:T(8,128)(2,1)S(1)}, bf16[256,256]{1,0:T(8,128)(2,1)}, u32[]{:S(2)}) copy-start(bf16[256,256]{1,0:T(8,128)(2,1)} %param.21) | copy-start | bytes 393220
  31.2 13.3 %copy-start.14 = (bf16[256,256]{1,0:T(8,128)(2,1)S(1)}, bf16[256,256]{1,0:T(8,128)(2,1)}, u32[]{:S(2)}) copy-start(bf16[256,256]{1,0:T(8,128)(2,1)} %param.20) | copy-start | bytes 393220
  31.2 5.8 %collective-permute-start.3 = (bf16[8,8,128]{2,1,0:T(8,128)(2,1)S(1)}, bf16[8,8,128]{2,1,0:T(8,128)(2,1)S(1)}, u32[]{:S(2)}, u32[]{:S(2)}) collective-permute-start(bf16[8,8,128]{2,1,0:T(8,128)(2,1)S(1)} %pad_maximum_fusion.5), channel_id=1, source_target_pairs={{0,8},{1,9},{2,10},{3,11},{4,12},{5,13},{6,14},{7,15},{8,0},{9,1},... | collective-permute-start | bytes 49160 | tf_op jit(solution)/shard_map/ppermute | solution.py:64
  37.0 9.1 %collective-permute-start.4 = (bf16[16,8,128]{2,1,0:T(8,128)(2,1)S(1)}, bf16[16,8,128]{2,1,0:T(8,128)(2,1)S(1)}, u32[]{:S(2)}, u32[]{:S(2)}) collective-permute-start(bf16[16,8,128]{2,1,0:T(8,128)(2,1)S(1)} %pad_maximum_fusion.3), channel_id=1, source_target_pairs={{0,16},{1,17},{2,18},{3,19},{4,20},{5,21},{6,22},{7,23},{8,24},{9,... | collective-permute-start | bytes 98312 | tf_op jit(solution)/shard_map/ppermute | solution.py:64
  44.6 5.3 %copy-start.3 = (bf16[256,256]{1,0:T(8,128)(2,1)S(1)}, bf16[256,256]{1,0:T(8,128)(2,1)}, u32[]{:S(2)}) copy-start(bf16[256,256]{1,0:T(8,128)(2,1)} %out_w_ref.3) | copy-start | bytes 393220
  46.1 3.8 %copy-start.1 = (bf16[8,16,256]{2,1,0:T(8,128)(2,1)S(1)}, bf16[8,16,256]{2,1,0:T(8,128)(2,1)}, u32[]{:S(2)}) copy-start(bf16[8,16,256]{2,1,0:T(8,128)(2,1)} %x_ref.5) | copy-start | bytes 196612
  54.3 6.1 %collective-permute-start.5 = (bf16[8,256]{1,0:T(8,128)(2,1)S(1)}, bf16[8,256]{1,0:T(8,128)(2,1)S(1)}, u32[]{:S(2)}, u32[]{:S(2)}) collective-permute-start(bf16[8,256]{1,0:T(8,128)(2,1)S(1)} %get-tuple-element.49), channel_id=1, source_target_pairs={{0,1},{1,0},{2,3},{3,2},{4,5},{5,4},{6,7},{7,6},{8,9},{9,8},{10,11... | collective-permute-start | bytes 12296 | tf_op jit(solution)/shard_map/ppermute | solution.py:319
  61.2 39.4 %copy-start.11 = (bf16[128,128]{1,0:T(8,128)(2,1)S(1)}, bf16[128,128]{1,0:T(8,128)(2,1)}, u32[]{:S(2)}) copy-start(bf16[128,128]{1,0:T(8,128)(2,1)} %gate_w_ref.3) | copy-start | bytes 98308
  61.2 19.2 %all-to-all-start.1 = ((bf16[32,8,512]{2,1,0:T(8,128)(2,1)}), bf16[32,8,512]{2,1,0:T(8,128)(2,1)S(1)}, u32[]{:S(2)}, u32[]{:S(2)}) async-start(bf16[32,8,512]{2,1,0:T(8,128)(2,1)} %broadcast_in_dim.12), calls=%async_computation.1 | async-start | bytes 524288 | tf_op jit(solution)/shard_map/all_to_all | solution.py:36
  69.0 31.7 %copy-start.2 = (bf16[1024,128]{1,0:T(8,128)(2,1)S(1)}, bf16[1024,128]{1,0:T(8,128)(2,1)}, u32[]{:S(2)}) copy-start(bf16[1024,128]{1,0:T(8,128)(2,1)} %outer_w_ref.1) | copy-start | bytes 786436
  69.0 0.8 collective-permute-start.6
  80.4 20.2 %copy-start.7 = (bf16[128,512]{1,0:T(8,128)(2,1)S(1)}, bf16[128,512]{1,0:T(8,128)(2,1)}, u32[]{:S(2)}) copy-start(bf16[128,512]{1,0:T(8,128)(2,1)} %in_w_ref.2) | copy-start | bytes 393220
  101.8 5.5 %collective-permute-start.7 = (bf16[24,8,128]{2,1,0:T(8,128)(2,1)S(1)}, bf16[24,8,128]{2,1,0:T(8,128)(2,1)S(1)}, u32[]{:S(2)}, u32[]{:S(2)}) collective-permute-start(bf16[24,8,128]{2,1,0:T(8,128)(2,1)S(1)} %pad_maximum_fusion.2), channel_id=1, source_target_pairs={{0,1},{1,0},{2,3},{3,2},{4,5},{5,4},{6,7},{7,6},{8,9},{9,8},{10,11... | collective-permute-start | bytes 147464 | tf_op jit(solution)/shard_map/ppermute | solution.py:347
  108.2 21.3 %all-to-all-start.3 = ((bf16[16,16,8,128]{3,2,1,0:T(8,128)(2,1)}), bf16[16,16,8,128]{3,2,1,0:T(8,128)(2,1)S(1)}, u32[]{:S(2)}, u32[]{:S(2)}) async-start(bf16[16,16,8,128]{3,2,1,0:T(8,128)(2,1)} %broadcast_in_dim.28), calls=%async_computation.3 | async-start | bytes 1048576 | tf_op jit(solution)/shard_map/all_to_all | solution.py:36
  130.8 16.3 %copy-start.6 = (bf16[128,512]{1,0:T(8,128)(2,1)S(1)}, bf16[128,512]{1,0:T(8,128)(2,1)}, u32[]{:S(2)}) copy-start(bf16[128,512]{1,0:T(8,128)(2,1)} %in_w_ref.3) | copy-start | bytes 393220
  130.8 16.3 %copy-start.9 = (bf16[128,128]{1,0:T(8,128)(2,1)S(1)}, bf16[128,128]{1,0:T(8,128)(2,1)}, u32[]{:S(2)}) copy-start(bf16[128,128]{1,0:T(8,128)(2,1)} %out_w_ref.4) | copy-start | bytes 98308
  130.8 16.3 %copy-start.10 = (bf16[128,128]{1,0:T(8,128)(2,1)S(1)}, bf16[128,128]{1,0:T(8,128)(2,1)}, u32[]{:S(2)}) copy-start(bf16[128,128]{1,0:T(8,128)(2,1)} %next_gate_w_ref.1) | copy-start | bytes 98308
  164.6 8.7 %collective-permute-start.8 = (bf16[16,16,8,128]{3,2,1,0:T(8,128)(2,1)S(1)}, bf16[16,16,8,128]{3,2,1,0:T(8,128)(2,1)S(1)}, u32[]{:S(2)}, u32[]{:S(2)}) collective-permute-start(bf16[16,16,8,128]{3,2,1,0:T(8,128)(2,1)S(1)} %all_to_all.37.tile_ref), channel_id=1, source_target_pairs={{0,1},{1,0},{2,3},{3,2},{4,5},{5,4},{6,7},{7,6},{8,9},{9,8},{10,11... | collective-permute-start | bytes 1572872 | tf_op jit(solution)/shard_map/ppermute | solution.py:364
  174.1 25.0 %copy-start.12 = (bf16[128,128]{1,0:T(8,128)(2,1)S(1)}, bf16[128,128]{1,0:T(8,128)(2,1)}, u32[]{:S(2)}) copy-start(bf16[128,128]{1,0:T(8,128)(2,1)} %out_w_ref.5) | copy-start | bytes 98308

commit v3 on v2

v3 whole, which is shorter than its diff:
```python
import functools

import jax
import jax.numpy as jnp
from jax import lax
from jax.experimental import pallas as pl
from jax.experimental.pallas import tpu as pltpu
from jax.sharding import PartitionSpec as P

F32 = jnp.float32
BF16 = jnp.bfloat16
ROWS, COLS = 16, 32
SIZES = {"z": 8, "xh": 2, "y": 8, "xl": 2, "core": 2}
ROW, COL = ("z", "xh"), ("y", "xl", "core")
FLIP = [(0, 1), (1, 0)]
CROSS = [(0, 0), (1, 2), (2, 1), (3, 3)]


def layer_norm(values):
    values = values.astype(F32)
    center = values - jnp.mean(values, axis=-1, keepdims=True)
    variance = jnp.mean(center * center, axis=-1, keepdims=True)
    return center * lax.rsqrt(variance + 1e-05)


def sigmoid(values):
    return 1.0 / (1.0 + jnp.exp(-values))


def project(values, weight):
    return jnp.dot(values, weight, preferred_element_type=F32)


def exchange(chunks, axes):
    return lax.all_to_all(chunks, axes, 0, 0)


def flip(block, axis):
    return lax.ppermute(block, axis, FLIP)


def cross(block):
    return lax.ppermute(block, ("xh", "xl"), CROSS)


def in_order(place, own, other, axis=0):
    lower = jnp.where(place == 0, own, other)
    upper = jnp.where(place == 0, other, own)
    return jnp.concatenate([lower, upper], axis=axis)


def kernel_call(body, outs, args, scratch=(), flops=0, aliases=None):
    shapes = [jax.ShapeDtypeStruct(s, d) for s, d in outs]
    vmem = pl.BlockSpec(memory_space=pltpu.VMEM)
    size = sum(a.size * a.dtype.itemsize for a in args)
    size += sum(s.size * jnp.dtype(s.dtype).itemsize for s in shapes)
    return pl.pallas_call(
        body,
        out_shape=shapes,
        in_specs=[vmem] * len(args),
        out_specs=[vmem] * len(shapes),
        scratch_shapes=[pltpu.VMEM(s, d) for s, d in scratch],
        input_output_aliases=aliases or {},
        compiler_params=pltpu.CompilerParams(vmem_limit_bytes=40 * 2**20),
        cost_estimate=pl.CostEstimate(flops=flops, bytes_accessed=size, transcendentals=0),
    )(*args)


def double_up(block, later):
    held = block
    for axis, bit in (("core", 1), ("xl", 1), ("y", 1), ("y", 2), ("y", 4)):
        size = SIZES[axis]
        met = lax.ppermute(held, axis, [(c, c ^ bit) for c in range(size)])
        held = in_order(lax.axis_index(axis) & bit, held, met)
        if axis == "core":
            held, later = lax.optimization_barrier((held, later))
    return held, later


def normed_kernel(x_ref, chunks_ref):
    normed = layer_norm(x_ref[...]).astype(BF16)
    for member in range(chunks_ref.shape[0]):
        chunks_ref[member] = normed


def bias_kernel(rows, pair_ref, bias_w_ref, bias_ref):
    height, width, depth = pair_ref.shape
    heads = bias_w_ref.shape[0]
    pair_normed = layer_norm(pair_ref[...].reshape(height * width, depth)).astype(BF16)
    wide = jnp.concatenate(
        [jnp.broadcast_to(bias_w_ref[h : h + 1, :], (rows, depth)) for h in range(heads)], axis=0
    )
    every = lax.dot_general(
        pair_normed, wide, (((1,), (1,)), ((), ())), preferred_element_type=F32
    ).reshape(height, width, heads * rows)
    lane = lax.broadcasted_iota(jnp.int32, (width, heads * rows), 1) % rows
    bias = jnp.zeros((width, heads * rows), F32)
    for i in range(height):
        bias = jnp.where(lane == i, every[i], bias)
    bias_ref[...] = bias.astype(BF16)


def query_kernel(x_ref, query_w_ref, gate_w_ref, query_ref, gate_ref):
    seqs, rows, channels = x_ref.shape
    normed = layer_norm(x_ref[...].reshape(seqs * rows, channels)).astype(BF16)
    query_ref[...] = project(normed, query_w_ref[...]).astype(BF16).reshape(seqs, rows, channels)
    gate_ref[...] = sigmoid(project(normed, gate_w_ref[...]))


def attention_kernel(
    heads, every_ref, bias_ref, query_ref, gate_ref, x_ref, key_w_ref, value_w_ref, out_w_ref,
    left_w_ref, right_w_ref, new_ref, left_ref, right_ref, gated_ref, factor_ref,
):
    members, seqs, rows, channels = every_ref.shape
    head_dim = channels // heads
    full = members * rows
    bias = bias_ref[...].astype(F32).T
    head_of = lax.broadcasted_iota(jnp.int32, (rows, channels), 1) // head_dim

    def one(s, carry):
        tokens = every_ref[:, s].reshape(full, channels)
        keys = project(tokens, key_w_ref[...]).astype(BF16)
        values = project(tokens, value_w_ref[...]).astype(BF16)
        query = query_ref[s]
        spread_query = jnp.concatenate(
            [jnp.where(head_of == h, query, jnp.zeros_like(query)) for h in range(heads)], axis=0
        )
        scores = lax.dot_general(
            spread_query, keys, (((1,), (1,)), ((), ())), preferred_element_type=F32
        )
        scores = scores * head_dim ** (-0.5) + bias
        expo = jnp.exp(scores - jnp.max(scores, axis=-1, keepdims=True))
        weights = (expo / jnp.sum(expo, axis=-1, keepdims=True)).astype(BF16)
        mixed = project(weights, values)
        attended = mixed[0:rows]
        for h in range(1, heads):
            attended = jnp.where(head_of == h, mixed[h * rows : (h + 1) * rows], attended)
        place = pl.ds(pl.multiple_of(s * rows, rows), rows)
        gated_ref[place, :] = (gate_ref[place, :] * attended).astype(BF16)
        return carry

    lax.fori_loop(0, seqs, one, 0, unroll=2)
    tokens = x_ref[...].reshape(seqs * rows, channels).astype(F32)
    new = (tokens + project(gated_ref[...], out_w_ref[...])).astype(BF16)
    new_ref[...] = new.reshape(seqs, rows, channels)
    width = left_w_ref.shape[0]
    factor_w = jnp.concatenate([left_w_ref[...], right_w_ref[...]], axis=0)
    factor_ref[:, : 2 * width] = lax.dot_general(
        layer_norm(new).astype(BF16), factor_w, (((1,), (1,)), ((), ())), preferred_element_type=F32
    )
    pieces = [factor_ref[pl.ds(i, seqs, stride=rows), :] for i in range(rows)]
    left_ref[...] = jnp.concatenate([p[:, :width] for p in pieces], axis=1).astype(BF16)
    right = jnp.concatenate([p[:, width : 2 * width] for p in pieces], axis=1).astype(BF16)
    for member in range(right_ref.shape[0]):
        right_ref[member] = right


def factor_kernel(left_ref, right_ref, chunks_ref):
    members, _, size = right_ref.shape
    pieces = chunks_ref.shape[0] // members
    split = size // pieces
    left = left_ref[...]
    for place in range(chunks_ref.shape[0]):
        part = place % pieces
        chunks_ref[place, :, : left.shape[1]] = left
        chunks_ref[place, :, left.shape[1] :] = right_ref[
            place // pieces, :, part * split : (part + 1) * split
        ]


def tile_kernel(mine_ref, theirs_ref, chunks_ref):
    own = mine_ref.shape[0]
    for member in range(chunks_ref.shape[0]):
        chunks_ref[member, :own] = mine_ref[...]
        chunks_ref[member, own:] = theirs_ref[...]


def edge_parts(pair, in_w_ref):
    normed = layer_norm(pair).astype(BF16)
    proj = project(normed, in_w_ref[...])
    width = in_w_ref.shape[1] // 4
    left = sigmoid(proj[:, :width]) * proj[:, width : 2 * width]
    right = sigmoid(proj[:, 2 * width : 3 * width]) * proj[:, 3 * width :]
    return left, right


def updated(combined, pair, gate_w_ref, out_w_ref):
    gate = sigmoid(project(layer_norm(pair).astype(BF16), gate_w_ref[...]))
    update = project(layer_norm(combined).astype(BF16), out_w_ref[...])
    return (pair.astype(F32) + gate * update).astype(BF16)


def outer_kernel(
    factors_ref, pair_ref, outer_w_ref, in_w_ref,
    pair_out, left_out, right_out, products_ref, update_ref, right_scr,
):
    total, size = factors_ref.shape
    rows, cols, depth = pair_ref.shape
    factor = size // (rows + cols)
    products = lax.dot_general(
        factors_ref[:, : rows * factor], factors_ref[:, rows * factor :], (((0,), (0,)), ((), ())), preferred_element_type=F32
    ) * (1.0 / total)
    slabs, _, slab = products_ref.shape
    per_slab = slab // factor
    outer = []
    for part in range(slabs):
        products_ref[part] = products[:, part * slab : (part + 1) * slab]
        lines = [
            products_ref[part, pl.ds(a, rows, stride=factor), :].astype(BF16) for a in range(factor)
        ]
        for j in range(per_slab):
            pieces = [line[:, j * factor : (j + 1) * factor] for line in lines]
            outer.append(jnp.concatenate(pieces, axis=1))
    outer = jnp.concatenate(outer, axis=0)
    update_ref[...] = project(outer, outer_w_ref[...])
    update = jnp.concatenate(
        [update_ref[pl.ds(i, cols, stride=rows), :] for i in range(rows)], axis=0
    )
    pair = (pair_ref[...].reshape(rows * cols, depth).astype(F32) + update).astype(BF16)
    pair_out[...] = pair
    left, right = edge_parts(pair, in_w_ref)
    left_out[...] = left.astype(BF16).reshape(rows, cols, depth)
    right_scr[...] = right
    for k in range(cols):
        line = right_scr[pl.ds(k, rows, stride=cols), :].astype(BF16)
        right_out[0, k] = line[:cols]
        right_out[1, k] = line[cols:]


def partial_kernel(tile_ref, line_ref, *refs):
    before_ref, out_ref, scr = refs if len(refs) == 3 else (None,) + refs
    groups, depth = tile_ref.shape[:2]
    lines = line_ref.shape[0]
    scr[...] = line_ref[...].astype(F32)

    def one(g, carry):
        tiles = [[tile_ref[2 * g + u, k].astype(F32) for k in range(depth)] for u in range(2)]
        for n in range(lines):
            totals = [None, None]
            for k in range(depth):
                line = scr[n, k : k + 1, :]
                for u in range(2):
                    term = tiles[u][k] * line
                    totals[u] = term if k == 0 else totals[u] + term
            for u in range(2):
                if before_ref is None:
                    out_ref[2 * g + u, n] = totals[u].astype(BF16)
                else:
                    part, line_place = divmod(n, out_ref.shape[3])
                    out_ref[2 * g + u, part, 0, line_place] = before_ref[2 * g + u, n]
                    out_ref[2 * g + u, part, 1, line_place] = totals[u].astype(BF16)
        return carry

    lax.fori_loop(0, groups // 2, one, 0)


def partial_sums(tiles, lines, before=None):
    groups, depth, height, width = tiles.shape
    count = lines.shape[0]
    shape = (groups, count, height, width)
    if before is not None:
        shape = (groups, 2, 2, count // 2, height, width)
    return kernel_call(
        partial_kernel,
        [(shape, BF16)],
        (tiles, lines) if before is None else (tiles, lines, before),
        scratch=[((count, depth, width), F32)],
        flops=2 * groups * count * height * width * depth,
    )[0]


def added(partial_ref):
    total = partial_ref[0].astype(F32)
    for member in range(1, partial_ref.shape[0]):
        total = total + partial_ref[member].astype(F32)
    return total


def middle_kernel(
    partial_ref, pair_ref, gate_w_ref, out_w_ref, in_w_ref, pair_out, chunks_out, line_out, right_scr
):
    rows, cols, depth = partial_ref.shape[1:]
    combined = added(partial_ref).reshape(rows * cols, depth)
    pair = updated(combined, pair_ref[...], gate_w_ref, out_w_ref)
    pair_out[...] = pair
    left, right = edge_parts(pair, in_w_ref)
    left = left.astype(BF16).reshape(rows, cols, depth)
    for member in range(chunks_out.shape[0]):
        chunks_out[member] = left
    right_scr[...] = right
    for j in range(cols):
        line_out[j] = right_scr[pl.ds(j, rows, stride=cols), :].astype(BF16)


def last_kernel(core_ref, partial_ref, pair_ref, gate_w_ref, out_w_ref, new_ref, scr):
    halves, cols, tall, depth = partial_ref.shape[1:]
    scr[...] = added(partial_ref).reshape(halves * cols * tall, depth)
    own, other = [
        jnp.concatenate(
            [scr[pl.ds(half * cols * tall + i, cols, stride=tall), :] for i in range(tall)], axis=0
        )
        for half in range(halves)
    ]
    first = core_ref[0:1, :] == 0
    combined = jnp.concatenate(
        [jnp.where(first, own, other), jnp.where(first, other, own)], axis=0
    )
    new_ref[...] = updated(combined, pair_ref[...], gate_w_ref, out_w_ref).reshape(new_ref.shape)


def on_device(
    alignment,
    pair_features,
    query_matrix,
    key_matrix,
    value_matrix,
    gate_matrix,
    output_matrix,
    bias_weight,
    left_factor_weight,
    right_factor_weight,
    outer_weight,
    outgoing_project,
    outgoing_gate,
    outgoing_output,
    incoming_project,
    incoming_gate,
    incoming_output,
):
    seqs, rows, channels = alignment.shape
    cols, depth = pair_features.shape[1:]
    heads = bias_weight.shape[1]
    factor = left_factor_weight.shape[1]
    places = rows * cols
    full = COLS * cols
    core, x_hi = lax.axis_index("core"), lax.axis_index("xh")

    bias = kernel_call(
        functools.partial(bias_kernel, rows), [((cols, heads * rows), BF16)], (pair_features, bias_weight.T)
    )[0]
    chunks = kernel_call(normed_kernel, [((ROWS, seqs, rows, channels), BF16)], (alignment,))[0]
    everyone = exchange(chunks, ROW)
    bias, query_matrix = double_up(bias[None], query_matrix)
    queries, gates = kernel_call(
        query_kernel,
        [((seqs, rows, channels), BF16), ((seqs * rows, channels), F32)],
        (alignment, query_matrix, gate_matrix),
    )
    new_alignment, left, right = kernel_call(
        functools.partial(attention_kernel, heads),
        [
            ((seqs, rows, channels), BF16),
            ((seqs, rows * factor), BF16),
            ((ROWS, seqs, rows * factor), BF16),
        ],
        (
            everyone, bias.reshape(full, heads * rows), queries, gates, alignment, key_matrix,
            value_matrix, output_matrix, left_factor_weight.T, right_factor_weight.T,
        ),
        scratch=[((seqs * rows, channels), BF16), ((seqs * rows, 128), F32)],
    )

    size = (rows + cols) * factor
    chunks = kernel_call(
        factor_kernel, [((COLS, seqs, size), BF16)], (left, exchange(right, ROW))
    )[0]
    factors = exchange(chunks, COL).reshape(COLS * seqs, size)
    pair_one, left_edge, right_edge = kernel_call(
        outer_kernel,
        [((places, depth), BF16), ((rows, cols, depth), BF16), ((2, cols, cols, depth), BF16)],
        (factors, pair_features, outer_weight, outgoing_project),
        scratch=[
            ((cols * factor // 128, rows * factor, 128), F32),
            ((places, depth), F32),
            ((places, depth), F32),
        ],
    )

    mine = lax.dynamic_index_in_dim(right_edge, core, 0, keepdims=False)
    theirs = lax.dynamic_index_in_dim(right_edge, 1 - core, 0, keepdims=False)
    swapped = flip(jnp.concatenate([left_edge, theirs], axis=0), "core")
    chunks = kernel_call(
        tile_kernel, [((SIZES["z"], 2 * cols, cols, depth), BF16)], (mine, swapped[rows:])
    )[0]
    tiles = exchange(chunks, "z")
    lines = jnp.concatenate([left_edge, swapped[:rows]], axis=1)
    lines = in_order(x_hi, lines, flip(lines, "xh"))
    partial = partial_sums(tiles, lines).reshape(ROWS, rows, cols, depth)
    partial = exchange(partial, ("y", "xl"))
    pair_two, chunks, lines = kernel_call(
        middle_kernel,
        [
            ((places, depth), BF16),
            ((SIZES["y"], rows, cols, depth), BF16),
            ((cols, rows, depth), BF16),
        ],
        (partial, cross(pair_one), outgoing_gate, outgoing_output, incoming_project),
        scratch=[((places, depth), F32)],
    )

    own = exchange(chunks, "y")
    lines = in_order(x_hi, lines, flip(lines, "xh"))
    other = flip(own, "core")
    partial = partial_sums(other, lines, partial_sums(own, lines))
    partial = exchange(partial.reshape(ROWS, 2, cols, cols, depth), ("z", "xl"))
    new_pair = kernel_call(
        last_kernel,
        [((rows, cols, depth), BF16)],
        (jnp.full((8, depth), core), partial, cross(pair_two), incoming_gate, incoming_output),
        scratch=[((places, depth), F32)],
    )[0]
    return (new_alignment, new_pair)


def solution(mesh):
    fine = jax.sharding.Mesh(mesh.devices.reshape(tuple(SIZES.values())), tuple(SIZES))
    rep = (P(),) * 15
    return jax.shard_map(
        on_device,
        mesh=fine,
        in_specs=(P(COL, ROW, None), P(ROW, COL, None)) + rep,
        out_specs=(P(COL, ROW, None), P(ROW, COL, None)),
        check_vma=False,
    )
```

time: 201 us -> 184 us (0.915)
  blocking collectives: 78.2 us -> 18.8 us
  waiting for transfers between devices: 40 us -> 68.7 us
  starting transfers between devices: 62.6 us -> 77.8 us
  local copies, waits for them, and re-layouts: 6.06 us -> 0.94 us
  Pallas kernels: 11.8 us -> 15.4 us
    all_to_all x4 -> x1, blocking collectives: 78.2 us -> 18.8 us  [exchange(): return lax.all_to_all(chunks, axes, 0, 0)]
    all_to_all x3 -> x6, waiting for transfers between devices: 32 us -> 56.3 us  [exchange(): return lax.all_to_all(chunks, axes, 0, 0)]
    all_to_all x3 -> x6, starting transfers between devices: 18.6 us -> 41.4 us  [exchange(): return lax.all_to_all(chunks, axes, 0, 0)]
    ppermute x9 -> x11, starting transfers between devices: 44 us -> 36.4 us  [the longest x5 20 us: double_up(): met = lax.ppermute(held, axis, [(c, c ^ bit) for c in range(size)])]
    ppermute x9 -> x11, waiting for transfers between devices: 8 us -> 12.4 us  [the longest x5 7.25 us: double_up(): met = lax.ppermute(held, axis, [(c, c ^ bit) for c in range(size)])]
    pallas_call x9 -> x12, Pallas kernels: 11.8 us -> 15.4 us  [kernel_call(): pl.pallas_call(body, out_shape=shapes, in_specs=[vmem] * len(args), out_s...]
    unnamed x37 -> x36, local copies, waits for them, and re-layouts: 4.35 us -> 0.92 us
  transfers between devices with their start and end apart: 12 -> 17, of which waited for: 10 -> 13; matrix products, arithmetic and copies ran while one was open for 0% -> 0% of each run, Pallas kernels for 1% -> 1%
where the time goes in v3:
time: 184 us; the launch traced here: 183 us
  starting transfers between devices  77.8 us (42%)
  waiting for transfers between devices  68.7 us (37%)
  blocking collectives  18.8 us (10%)
  Pallas kernels  15.4 us (8%)
    all_to_all x6, waiting for transfers between devices, exchange(): return lax.all_to_all(chunks, axes, 0, 0)  56.3 us
    all_to_all x6, starting transfers between devices, exchange(): return lax.all_to_all(chunks, axes, 0, 0)  41.4 us
    ppermute x5, starting transfers between devices, double_up(): met = lax.ppermute(held, axis, [(c, c ^ bit) for c in range(size)])  20 us
    all_to_all x1, blocking collectives, exchange(): return lax.all_to_all(chunks, axes, 0, 0)  18.8 us
    pallas_call x12, Pallas kernels, kernel_call(): pl.pallas_call(body, out_shape=shapes, in_specs=[vmem] * len(args), out_s...  15.4 us
    ppermute x4, starting transfers between devices, flip(): return lax.ppermute(block, axis, FLIP)  15.1 us
    ppermute x5, waiting for transfers between devices, double_up(): met = lax.ppermute(held, axis, [(c, c ^ bit) for c in range(size)])  7.25 us
    ppermute x4, waiting for transfers between devices, flip(): return lax.ppermute(block, axis, FLIP)  5.16 us
  transfers between devices with their start and end apart: 17, of which 13 were waited for; matrix products, arithmetic and copies ran while one was open for 0% of the time, Pallas kernels for 1%

profile of v3, /device:TPU:1, one launch (start us, length us, event | category | flops | bytes accessed | tf_op | source)
XLA Modules:
  0.0 182.9 jit_solution(204994995324125429)
XLA Ops:
  1.5 1.3 shard_map.176
  2.7 13.6 %all-to-all-start = ((bf16[16,8,16,256]{3,2,1,0:T(8,128)(2,1)}), bf16[16,8,16,256]{3,2,1,0:T(8,128)(2,1)S(1)}, u32[]{:S(2)}, u32[]{:S(2)}) async-start(bf16[16,8,16,256]{3,2,1,0:T(8,128)(2,1)} %shard_map.176), calls=%async_computation | async-start | bytes 2097152 | tf_op jit(solution)/shard_map/all_to_all | solution.py:35
  16.6 2.9 %collective-permute-start = (bf16[1,8,128]{2,1,0:T(8,128)(2,1)S(1)}, bf16[1,8,128]{2,1,0:T(8,128)(2,1)S(1)}, u32[]{:S(2)}, u32[]{:S(2)}) collective-permute-start(bf16[1,8,128]{2,1,0:T(8,128)(2,1)S(1)} %bitcast.18), channel_id=1, source_target_pairs={{0,1},{1,0},{2,3},{3,2},{4,5},{5,4},{6,7},{7,6},{8,9},{9,8},{10,11... | collective-permute-start | bytes 6152 | tf_op jit(solution)/shard_map/ppermute | solution.py:73
  20.3 2.2 %collective-permute-start.1 = (bf16[2,8,128]{2,1,0:T(8,128)(2,1)S(1)}, bf16[2,8,128]{2,1,0:T(8,128)(2,1)S(1)}, u32[]{:S(2)}, u32[]{:S(2)}) collective-permute-start(bf16[2,8,128]{2,1,0:T(8,128)(2,1)S(1)} %pad_maximum_fusion.7), channel_id=1, source_target_pairs={{0,2},{2,0},{1,3},{3,1},{4,6},{6,4},{5,7},{7,5},{8,10},{10,8},{9,1... | collective-permute-start | bytes 12296 | tf_op jit(solution)/shard_map/ppermute | solution.py:73
  22.6 2.4 %collective-permute-done.1 = bf16[2,8,128]{2,1,0:T(8,128)(2,1)S(1)} collective-permute-done((bf16[2,8,128]{2,1,0:T(8,128)(2,1)S(1)}, bf16[2,8,128]{2,1,0:T(8,128)(2,1)S(1)}, u32[]{:S(2)}, u32[]{:S(2)}) %collective-permute-start.1) | collective-permute-done | bytes 4128 | tf_op jit(solution)/shard_map/ppermute | solution.py:73
  25.0 3.2 %collective-permute-start.2 = (bf16[4,8,128]{2,1,0:T(8,128)(2,1)S(1)}, bf16[4,8,128]{2,1,0:T(8,128)(2,1)S(1)}, u32[]{:S(2)}, u32[]{:S(2)}) collective-permute-start(bf16[4,8,128]{2,1,0:T(8,128)(2,1)S(1)} %pad_maximum_fusion.6), channel_id=1, source_target_pairs={{0,4},{4,0},{8,12},{12,8},{16,20},{20,16},{24,28},{28,24},{1,5},{5... | collective-permute-start | bytes 24584 | tf_op jit(solution)/shard_map/ppermute | solution.py:73
  28.2 1.5 collective-permute-done.2
  29.7 4.2 %collective-permute-start.3 = (bf16[8,8,128]{2,1,0:T(8,128)(2,1)S(1)}, bf16[8,8,128]{2,1,0:T(8,128)(2,1)S(1)}, u32[]{:S(2)}, u32[]{:S(2)}) collective-permute-start(bf16[8,8,128]{2,1,0:T(8,128)(2,1)S(1)} %pad_maximum_fusion.5), channel_id=1, source_target_pairs={{0,8},{4,12},{8,0},{12,4},{16,24},{20,28},{24,16},{28,20},{1,9},{5... | collective-permute-start | bytes 49160 | tf_op jit(solution)/shard_map/ppermute | solution.py:73
  33.9 1.4 collective-permute-done.3
  35.4 7.5 %collective-permute-start.4 = (bf16[16,8,128]{2,1,0:T(8,128)(2,1)S(1)}, bf16[16,8,128]{2,1,0:T(8,128)(2,1)S(1)}, u32[]{:S(2)}, u32[]{:S(2)}) collective-permute-start(bf16[16,8,128]{2,1,0:T(8,128)(2,1)S(1)} %pad_maximum_fusion.4), channel_id=1, source_target_pairs={{0,16},{4,20},{8,24},{12,28},{16,0},{20,4},{24,8},{28,12},{1,17},{... | collective-permute-start | bytes 98312 | tf_op jit(solution)/shard_map/ppermute | solution.py:73
  43.3 1.1 collective-permute-done.4
  44.5 4.4 %shard_map.179 = (bf16[8,16,256]{2,1,0:T(8,128)(2,1)}, bf16[8,512]{1,0:T(8,128)(2,1)S(1)}, bf16[16,8,512]{2,1,0:T(8,128)(2,1)S(1)}) custom-call(bf16[16,8,16,256]{3,2,1,0:T(8,128)(2,1)S(1)} %all-to-all-done.every_ref, bf16[256,128]{1,0:T(8,128)(2,1)S(1)} %maximum_bitcast_fusion.bias_ref, bf16[8,16,256]{2,1,0:T(8,128)(2,1)S(1)} %get-tuple-element.17.query_ref, ...), custom_call_target="tpu_custom_call" | custom-call | bytes 2007040 | tf_op jit(solution)/shard_map/pallas_call | solution.py:57
  49.0 18.8 %all_to_all.35.right_ref = bf16[16,8,512]{2,1,0:T(8,128)(2,1)S(1)} all-to-all(bf16[16,8,512]{2,1,0:T(8,128)(2,1)S(1)} %get-tuple-element.21), channel_id=1, replica_groups=mesh['z'=8,'xh'=2,'y'=8,'xl'=2,'core'=2] {'z','xh'}, dimensions={0} | all-to-all | bytes 262144 | tf_op jit(solution)/shard_map/all_to_all | solution.py:35
  68.6 12.9 %all-to-all-start.2 = ((bf16[32,8,768]{2,1,0:T(8,128)(2,1)}), bf16[32,8,768]{2,1,0:T(8,128)(2,1)S(1)}, u32[]{:S(2)}, u32[]{:S(2)}) async-start(bf16[32,8,768]{2,1,0:T(8,128)(2,1)} %shard_map.180), calls=%async_computation.2 | async-start | bytes 786432 | tf_op jit(solution)/shard_map/all_to_all | solution.py:35
  81.5 13.8 %all-to-all-done.2 = bf16[32,8,768]{2,1,0:T(8,128)(2,1)S(1)} async-done(((bf16[32,8,768]{2,1,0:T(8,128)(2,1)}), bf16[32,8,768]{2,1,0:T(8,128)(2,1)S(1)}, u32[]{:S(2)}, u32[]{:S(2)}) %all-to-all-start.2) | async-done | bytes 393248 | tf_op jit(solution)/shard_map/all_to_all | solution.py:35
  95.3 1.1 shard_map.181
  96.5 3.6 %collective-permute-start.5 = (bf16[24,8,128]{2,1,0:T(8,128)(2,1)S(1)}, bf16[24,8,128]{2,1,0:T(8,128)(2,1)S(1)}, u32[]{:S(2)}, u32[]{:S(2)}) collective-permute-start(bf16[24,8,128]{2,1,0:T(8,128)(2,1)S(1)} %pad_maximum_fusion.3), channel_id=1, source_target_pairs={{0,1},{1,0},{2,3},{3,2},{4,5},{5,4},{6,7},{7,6},{8,9},{9,8},{10,11... | collective-permute-start | bytes 147464 | tf_op jit(solution)/shard_map/ppermute | solution.py:39
  101.7 3.4 %all-to-all-start.3 = ((bf16[8,16,8,128]{3,2,1,0:T(8,128)(2,1)}), bf16[8,16,8,128]{3,2,1,0:T(8,128)(2,1)S(1)}, u32[]{:S(2)}, u32[]{:S(2)}) async-start(bf16[8,16,8,128]{3,2,1,0:T(8,128)(2,1)} %shard_map.182), calls=%async_computation.3 | async-start | bytes 524288 | tf_op jit(solution)/shard_map/all_to_all | solution.py:35
  105.1 3.0 %collective-permute-start.6 = (bf16[16,16,128]{2,1,0:T(8,128)(2,1)S(1)}, bf16[16,16,128]{2,1,0:T(8,128)(2,1)S(1)}, u32[]{:S(2)}, u32[]{:S(2)}) collective-permute-start(bf16[16,16,128]{2,1,0:T(8,128)(2,1)S(1)} %pad_maximum_fusion.1), channel_id=1, source_target_pairs={{0,32},{32,0},{1,33},{33,1},{2,34},{34,2},{3,35},{35,3},{4,36},{36... | collective-permute-start | bytes 196616 | tf_op jit(solution)/shard_map/ppermute | solution.py:39
  108.1 3.8 %collective-permute-done.6 = bf16[16,16,128]{2,1,0:T(8,128)(2,1)S(1)} collective-permute-done((bf16[16,16,128]{2,1,0:T(8,128)(2,1)S(1)}, bf16[16,16,128]{2,1,0:T(8,128)(2,1)S(1)}, u32[]{:S(2)}, u32[]{:S(2)}) %collective-permute-start.6) | collective-permute-done | bytes 65568 | tf_op jit(solution)/shard_map/ppermute | solution.py:39
  112.0 5.4 %all-to-all-done.3.tile_ref = bf16[8,16,8,128]{3,2,1,0:T(8,128)(2,1)S(1)} async-done(((bf16[8,16,8,128]{3,2,1,0:T(8,128)(2,1)}), bf16[8,16,8,128]{3,2,1,0:T(8,128)(2,1)S(1)}, u32[]{:S(2)}, u32[]{:S(2)}) %all-to-all-start.3) | async-done | bytes 262176 | tf_op jit(solution)/shard_map/all_to_all | solution.py:35
  117.4 1.9 %shard_map.183 = bf16[8,32,8,128]{3,2,1,0:T(8,128)(2,1)} custom-call(bf16[8,16,8,128]{3,2,1,0:T(8,128)(2,1)S(1)} %all-to-all-done.3.tile_ref, bf16[32,16,128]{2,1,0:T(8,128)(2,1)S(1)} %pad_maximum_fusion.line_ref), custom_call_target="tpu_custom_call" | custom-call | flops 8388608 | bytes 917504 | tf_op jit(solution)/shard_map/pallas_call | solution.py:57
  119.3 3.7 %all-to-all-start.4 = ((bf16[16,16,8,128]{3,2,1,0:T(8,128)(2,1)}), bf16[16,16,8,128]{3,2,1,0:T(8,128)(2,1)S(1)}, u32[]{:S(2)}, u32[]{:S(2)}) async-start(bf16[16,16,8,128]{3,2,1,0:T(8,128)(2,1)} %bitcast.8), calls=%async_computation.4 | async-start | bytes 1048576 | tf_op jit(solution)/shard_map/all_to_all | solution.py:35
  123.7 15.4 %all-to-all-done.4.partial_ref = bf16[16,16,8,128]{3,2,1,0:T(8,128)(2,1)S(1)} async-done(((bf16[16,16,8,128]{3,2,1,0:T(8,128)(2,1)}), bf16[16,16,8,128]{3,2,1,0:T(8,128)(2,1)S(1)}, u32[]{:S(2)}, u32[]{:S(2)}) %all-to-all-start.4) | async-done | bytes 524320 | tf_op jit(solution)/shard_map/all_to_all | solution.py:35
  139.2 1.4 shard_map.184
  140.6 4.1 %all-to-all-start.5 = ((bf16[8,16,8,128]{3,2,1,0:T(8,128)(2,1)}), bf16[8,16,8,128]{3,2,1,0:T(8,128)(2,1)S(1)}, u32[]{:S(2)}, u32[]{:S(2)}) async-start(bf16[8,16,8,128]{3,2,1,0:T(8,128)(2,1)} %get-tuple-element.25), calls=%async_computation.5 | async-start | bytes 524288 | tf_op jit(solution)/shard_map/all_to_all | solution.py:35
  144.7 3.0 %collective-permute-start.9 = (bf16[8,16,128]{2,1,0:T(8,128)(2,1)S(1)}, bf16[8,16,128]{2,1,0:T(8,128)(2,1)S(1)}, u32[]{:S(2)}, u32[]{:S(2)}) collective-permute-start(bf16[8,16,128]{2,1,0:T(8,128)(2,1)S(1)} %get-tuple-element.26), channel_id=1, source_target_pairs={{0,32},{32,0},{1,33},{33,1},{2,34},{34,2},{3,35},{35,3},{4,36},{36... | collective-permute-start | bytes 98312 | tf_op jit(solution)/shard_map/ppermute | solution.py:39
  147.6 6.2 %all-to-all-done.5.tile_ref = bf16[8,16,8,128]{3,2,1,0:T(8,128)(2,1)S(1)} async-done(((bf16[8,16,8,128]{3,2,1,0:T(8,128)(2,1)}), bf16[8,16,8,128]{3,2,1,0:T(8,128)(2,1)S(1)}, u32[]{:S(2)}, u32[]{:S(2)}) %all-to-all-start.5) | async-done | bytes 262176 | tf_op jit(solution)/shard_map/all_to_all | solution.py:35
  153.9 5.5 %collective-permute-start.8 = (bf16[8,16,8,128]{3,2,1,0:T(8,128)(2,1)S(1)}, bf16[8,16,8,128]{3,2,1,0:T(8,128)(2,1)S(1)}, u32[]{:S(2)}, u32[]{:S(2)}) collective-permute-start(bf16[8,16,8,128]{3,2,1,0:T(8,128)(2,1)S(1)} %all-to-all-done.5.tile_ref), channel_id=1, source_target_pairs={{0,1},{1,0},{2,3},{3,2},{4,5},{5,4},{6,7},{7,6},{8,9},{9,8},{10,11... | collective-permute-start | bytes 786440 | tf_op jit(solution)/shard_map/ppermute | solution.py:39
  160.6 1.4 shard_map.186
  162.0 3.7 %all-to-all-start.6 = ((bf16[16,2,8,8,128]{4,3,2,1,0:T(8,128)(2,1)}), bf16[16,2,8,8,128]{4,3,2,1,0:T(8,128)(2,1)S(1)}, u32[]{:S(2)}, u32[]{:S(2)}) async-start(bf16[16,2,8,8,128]{4,3,2,1,0:T(8,128)(2,1)} %bitcast.9), calls=%async_computation.6 | async-start | bytes 1048576 | tf_op jit(solution)/shard_map/all_to_all | solution.py:35
  166.4 15.5 %all-to-all-done.6.partial_ref = bf16[16,2,8,8,128]{4,3,2,1,0:T(8,128)(2,1)S(1)} async-done(((bf16[16,2,8,8,128]{4,3,2,1,0:T(8,128)(2,1)}), bf16[16,2,8,8,128]{4,3,2,1,0:T(8,128)(2,1)S(1)}, u32[]{:S(2)}, u32[]{:S(2)}) %all-to-all-start.6) | async-done | bytes 524320 | tf_op jit(solution)/shard_map/all_to_all | solution.py:35
  (71 shorter events, 8.3 us)
Async XLA Ops:
  2.7 13.6 %copy-start.7 = (bf16[16,8,128]{2,1,0:T(8,128)(2,1)S(1)}, bf16[16,8,128]{2,1,0:T(8,128)(2,1)}, u32[]{:S(2)}) copy-start(bf16[16,8,128]{2,1,0:T(8,128)(2,1)} %pair_ref.3) | copy-start | bytes 98308
  2.7 13.6 %copy-start.17 = (bf16[128,8]{0,1:T(8,128)(2,1)S(1)}, bf16[128,8]{0,1:T(8,128)(2,1)}, u32[]{:S(2)}) copy-start(bf16[128,8]{0,1:T(8,128)(2,1)} %param.24) | copy-start | bytes 6148
  2.7 41.7 %all-to-all-start = ((bf16[16,8,16,256]{3,2,1,0:T(8,128)(2,1)}), bf16[16,8,16,256]{3,2,1,0:T(8,128)(2,1)S(1)}, u32[]{:S(2)}, u32[]{:S(2)}) async-start(bf16[16,8,16,256]{3,2,1,0:T(8,128)(2,1)} %shard_map.176), calls=%async_computation | async-start | bytes 2097152 | tf_op jit(solution)/shard_map/all_to_all | solution.py:35
  16.3 26.5 %copy-start.9 = (bf16[256,256]{1,0:T(8,128)(2,1)S(1)}, bf16[256,256]{1,0:T(8,128)(2,1)}, u32[]{:S(2)}) copy-start(bf16[256,256]{1,0:T(8,128)(2,1)} %gate_w_ref.3) | copy-start | bytes 393220
  16.6 3.7 %collective-permute-start = (bf16[1,8,128]{2,1,0:T(8,128)(2,1)S(1)}, bf16[1,8,128]{2,1,0:T(8,128)(2,1)S(1)}, u32[]{:S(2)}, u32[]{:S(2)}) collective-permute-start(bf16[1,8,128]{2,1,0:T(8,128)(2,1)S(1)} %bitcast.18), channel_id=1, source_target_pairs={{0,1},{1,0},{2,3},{3,2},{4,5},{5,4},{6,7},{7,6},{8,9},{9,8},{10,11... | collective-permute-start | bytes 6152 | tf_op jit(solution)/shard_map/ppermute | solution.py:73
  20.3 4.7 %collective-permute-start.1 = (bf16[2,8,128]{2,1,0:T(8,128)(2,1)S(1)}, bf16[2,8,128]{2,1,0:T(8,128)(2,1)S(1)}, u32[]{:S(2)}, u32[]{:S(2)}) collective-permute-start(bf16[2,8,128]{2,1,0:T(8,128)(2,1)S(1)} %pad_maximum_fusion.7), channel_id=1, source_target_pairs={{0,2},{2,0},{1,3},{3,1},{4,6},{6,4},{5,7},{7,5},{8,10},{10,8},{9,1... | collective-permute-start | bytes 12296 | tf_op jit(solution)/shard_map/ppermute | solution.py:73
  22.6 20.3 %copy-start.8 = (bf16[256,256]{1,0:T(8,128)(2,1)S(1)}, bf16[256,256]{1,0:T(8,128)(2,1)}, u32[]{:S(2)}) copy-start(bf16[256,256]{1,0:T(8,128)(2,1)} %query_w_ref) | copy-start | bytes 393220
  25.0 4.7 %collective-permute-start.2 = (bf16[4,8,128]{2,1,0:T(8,128)(2,1)S(1)}, bf16[4,8,128]{2,1,0:T(8,128)(2,1)S(1)}, u32[]{:S(2)}, u32[]{:S(2)}) collective-permute-start(bf16[4,8,128]{2,1,0:T(8,128)(2,1)S(1)} %pad_maximum_fusion.6), channel_id=1, source_target_pairs={{0,4},{4,0},{8,12},{12,8},{16,20},{20,16},{24,28},{28,24},{1,5},{5... | collective-permute-start | bytes 24584 | tf_op jit(solution)/shard_map/ppermute | solution.py:73
  29.7 5.7 %collective-permute-start.3 = (bf16[8,8,128]{2,1,0:T(8,128)(2,1)S(1)}, bf16[8,8,128]{2,1,0:T(8,128)(2,1)S(1)}, u32[]{:S(2)}, u32[]{:S(2)}) collective-permute-start(bf16[8,8,128]{2,1,0:T(8,128)(2,1)S(1)} %pad_maximum_fusion.5), channel_id=1, source_target_pairs={{0,8},{4,12},{8,0},{12,4},{16,24},{20,28},{24,16},{28,20},{1,9},{5... | collective-permute-start | bytes 49160 | tf_op jit(solution)/shard_map/ppermute | solution.py:73
  33.9 9.0 %copy-start.1 = (bf16[8,16,256]{2,1,0:T(8,128)(2,1)S(1)}, bf16[8,16,256]{2,1,0:T(8,128)(2,1)}, u32[]{:S(2)}) copy-start(bf16[8,16,256]{2,1,0:T(8,128)(2,1)} %x_ref.5) | copy-start | bytes 196612
  35.4 9.1 %collective-permute-start.4 = (bf16[16,8,128]{2,1,0:T(8,128)(2,1)S(1)}, bf16[16,8,128]{2,1,0:T(8,128)(2,1)S(1)}, u32[]{:S(2)}, u32[]{:S(2)}) collective-permute-start(bf16[16,8,128]{2,1,0:T(8,128)(2,1)S(1)} %pad_maximum_fusion.4), channel_id=1, source_target_pairs={{0,16},{4,20},{8,24},{12,28},{16,0},{20,4},{24,8},{28,12},{1,17},{... | collective-permute-start | bytes 98312 | tf_op jit(solution)/shard_map/ppermute | solution.py:73
  42.9 1.6 copy-start.5
  42.9 1.6 copy-start.15
  42.9 1.6 copy-start.16
  68.6 26.7 %copy-start.2 = (bf16[1024,128]{1,0:T(8,128)(2,1)S(1)}, bf16[1024,128]{1,0:T(8,128)(2,1)}, u32[]{:S(2)}) copy-start(bf16[1024,128]{1,0:T(8,128)(2,1)} %outer_w_ref.1) | copy-start | bytes 786436
  68.6 26.7 %copy-start.6 = (bf16[128,512]{1,0:T(8,128)(2,1)S(1)}, bf16[128,512]{1,0:T(8,128)(2,1)}, u32[]{:S(2)}) copy-start(bf16[128,512]{1,0:T(8,128)(2,1)} %in_w_ref.2) | copy-start | bytes 393220
  68.6 26.7 %all-to-all-start.2 = ((bf16[32,8,768]{2,1,0:T(8,128)(2,1)}), bf16[32,8,768]{2,1,0:T(8,128)(2,1)S(1)}, u32[]{:S(2)}, u32[]{:S(2)}) async-start(bf16[32,8,768]{2,1,0:T(8,128)(2,1)} %shard_map.180), calls=%async_computation.2 | async-start | bytes 786432 | tf_op jit(solution)/shard_map/all_to_all | solution.py:35
  96.5 4.5 %collective-permute-start.5 = (bf16[24,8,128]{2,1,0:T(8,128)(2,1)S(1)}, bf16[24,8,128]{2,1,0:T(8,128)(2,1)S(1)}, u32[]{:S(2)}, u32[]{:S(2)}) collective-permute-start(bf16[24,8,128]{2,1,0:T(8,128)(2,1)S(1)} %pad_maximum_fusion.3), channel_id=1, source_target_pairs={{0,1},{1,0},{2,3},{3,2},{4,5},{5,4},{6,7},{7,6},{8,9},{9,8},{10,11... | collective-permute-start | bytes 147464 | tf_op jit(solution)/shard_map/ppermute | solution.py:39
  101.7 15.7 %all-to-all-start.3 = ((bf16[8,16,8,128]{3,2,1,0:T(8,128)(2,1)}), bf16[8,16,8,128]{3,2,1,0:T(8,128)(2,1)S(1)}, u32[]{:S(2)}, u32[]{:S(2)}) async-start(bf16[8,16,8,128]{3,2,1,0:T(8,128)(2,1)} %shard_map.182), calls=%async_computation.3 | async-start | bytes 524288 | tf_op jit(solution)/shard_map/all_to_all | solution.py:35
  105.1 6.8 %collective-permute-start.6 = (bf16[16,16,128]{2,1,0:T(8,128)(2,1)S(1)}, bf16[16,16,128]{2,1,0:T(8,128)(2,1)S(1)}, u32[]{:S(2)}, u32[]{:S(2)}) collective-permute-start(bf16[16,16,128]{2,1,0:T(8,128)(2,1)S(1)} %pad_maximum_fusion.1), channel_id=1, source_target_pairs={{0,32},{32,0},{1,33},{33,1},{2,34},{34,2},{3,35},{35,3},{4,36},{36... | collective-permute-start | bytes 196616 | tf_op jit(solution)/shard_map/ppermute | solution.py:39
  119.3 19.8 %copy-start.10 = (bf16[128,512]{1,0:T(8,128)(2,1)S(1)}, bf16[128,512]{1,0:T(8,128)(2,1)}, u32[]{:S(2)}) copy-start(bf16[128,512]{1,0:T(8,128)(2,1)} %in_w_ref.3) | copy-start | bytes 393220
  119.3 19.8 %copy-start.11 = (bf16[128,128]{1,0:T(8,128)(2,1)S(1)}, bf16[128,128]{1,0:T(8,128)(2,1)}, u32[]{:S(2)}) copy-start(bf16[128,128]{1,0:T(8,128)(2,1)} %gate_w_ref.4) | copy-start | bytes 98308
  119.3 19.8 %copy-start.12 = (bf16[128,128]{1,0:T(8,128)(2,1)S(1)}, bf16[128,128]{1,0:T(8,128)(2,1)}, u32[]{:S(2)}) copy-start(bf16[128,128]{1,0:T(8,128)(2,1)} %out_w_ref.4) | copy-start | bytes 98308
  119.3 19.8 %all-to-all-start.4 = ((bf16[16,16,8,128]{3,2,1,0:T(8,128)(2,1)}), bf16[16,16,8,128]{3,2,1,0:T(8,128)(2,1)S(1)}, u32[]{:S(2)}, u32[]{:S(2)}) async-start(bf16[16,16,8,128]{3,2,1,0:T(8,128)(2,1)} %bitcast.8), calls=%async_computation.4 | async-start | bytes 1048576 | tf_op jit(solution)/shard_map/all_to_all | solution.py:35
  123.0 0.7 collective-permute-start.7
  140.6 13.3 %all-to-all-start.5 = ((bf16[8,16,8,128]{3,2,1,0:T(8,128)(2,1)}), bf16[8,16,8,128]{3,2,1,0:T(8,128)(2,1)S(1)}, u32[]{:S(2)}, u32[]{:S(2)}) async-start(bf16[8,16,8,128]{3,2,1,0:T(8,128)(2,1)} %get-tuple-element.25), calls=%async_computation.5 | async-start | bytes 524288 | tf_op jit(solution)/shard_map/all_to_all | solution.py:35
  144.7 14.7 %collective-permute-start.9 = (bf16[8,16,128]{2,1,0:T(8,128)(2,1)S(1)}, bf16[8,16,128]{2,1,0:T(8,128)(2,1)S(1)}, u32[]{:S(2)}, u32[]{:S(2)}) collective-permute-start(bf16[8,16,128]{2,1,0:T(8,128)(2,1)S(1)} %get-tuple-element.26), channel_id=1, source_target_pairs={{0,32},{32,0},{1,33},{33,1},{2,34},{34,2},{3,35},{35,3},{4,36},{36... | collective-permute-start | bytes 98312 | tf_op jit(solution)/shard_map/ppermute | solution.py:39
  153.9 6.7 %collective-permute-start.8 = (bf16[8,16,8,128]{3,2,1,0:T(8,128)(2,1)S(1)}, bf16[8,16,8,128]{3,2,1,0:T(8,128)(2,1)S(1)}, u32[]{:S(2)}, u32[]{:S(2)}) collective-permute-start(bf16[8,16,8,128]{3,2,1,0:T(8,128)(2,1)S(1)} %all-to-all-done.5.tile_ref), channel_id=1, source_target_pairs={{0,1},{1,0},{2,3},{3,2},{4,5},{5,4},{6,7},{7,6},{8,9},{9,8},{10,11... | collective-permute-start | bytes 786440 | tf_op jit(solution)/shard_map/ppermute | solution.py:39
  162.0 19.9 %copy-start.13 = (bf16[128,128]{1,0:T(8,128)(2,1)S(1)}, bf16[128,128]{1,0:T(8,128)(2,1)}, u32[]{:S(2)}) copy-start(bf16[128,128]{1,0:T(8,128)(2,1)} %gate_w_ref.5) | copy-start | bytes 98308
  162.0 19.9 %copy-start.14 = (bf16[128,128]{1,0:T(8,128)(2,1)S(1)}, bf16[128,128]{1,0:T(8,128)(2,1)}, u32[]{:S(2)}) copy-start(bf16[128,128]{1,0:T(8,128)(2,1)} %out_w_ref.5) | copy-start | bytes 98308
  162.0 19.9 %all-to-all-start.6 = ((bf16[16,2,8,8,128]{4,3,2,1,0:T(8,128)(2,1)}), bf16[16,2,8,8,128]{4,3,2,1,0:T(8,128)(2,1)S(1)}, u32[]{:S(2)}, u32[]{:S(2)}) async-start(bf16[16,2,8,8,128]{4,3,2,1,0:T(8,128)(2,1)} %bitcast.9), calls=%async_computation.6 | async-start | bytes 1048576 | tf_op jit(solution)/shard_map/all_to_all | solution.py:35
  165.7 0.7 collective-permute-start.10
  (3 other events, 3.3 us)

commit v4 on v3

--- a/solution.py
+++ b/solution.py
@@ -12,6 +12,7 @@
 ROWS, COLS = 16, 32
 SIZES = {"z": 8, "xh": 2, "y": 8, "xl": 2, "core": 2}
 ROW, COL = ("z", "xh"), ("y", "xl", "core")
+ROW_X_FIRST, COL_X_FIRST = ("xh", "z"), ("core", "xl", "y")
 FLIP = [(0, 1), (1, 0)]
 CROSS = [(0, 0), (1, 2), (2, 1), (3, 3)]
 
@@ -66,15 +67,21 @@
     )(*args)
 
 
-def double_up(block, later):
-    held = block
-    for axis, bit in (("core", 1), ("xl", 1), ("y", 1), ("y", 2), ("y", 4)):
-        size = SIZES[axis]
-        met = lax.ppermute(held, axis, [(c, c ^ bit) for c in range(size)])
-        held = in_order(lax.axis_index(axis) & bit, held, met)
-        if axis == "core":
-            held, later = lax.optimization_barrier((held, later))
-    return held, later
+def shifted(block, step):
+    size = SIZES["y"]
+    return lax.ppermute(block, "y", [(y, (y - step) % size) for y in range(size)])
+
+
+def from_col(block, later):
+    held = block[None, None, None]
+    held = in_order(lax.axis_index("core"), held, flip(held, "core"), 2)
+    held, later = lax.optimization_barrier((held, later))
+    near = jnp.concatenate([shifted(held, -1), held, shifted(held, 1)], axis=1)
+    far = jnp.concatenate([shifted(near[:, 1:], -3), near, shifted(near, 3)], axis=1)
+    size = SIZES["y"]
+    start = lax.rem(size + 3 - lax.axis_index("y"), size)
+    held = lax.dynamic_slice_in_dim(jnp.concatenate([far, far], axis=1), start, size, 1)
+    return in_order(lax.axis_index("xl"), held, flip(held, "xl"), 0), later
 
 
 def normed_kernel(x_ref, chunks_ref):
@@ -139,7 +146,7 @@
         gated_ref[place, :] = (gate_ref[place, :] * attended).astype(BF16)
         return carry
 
-    lax.fori_loop(0, seqs, one, 0, unroll=2)
+    lax.fori_loop(0, seqs, one, 0, unroll=True)
     tokens = x_ref[...].reshape(seqs * rows, channels).astype(F32)
     new = (tokens + project(gated_ref[...], out_w_ref[...])).astype(BF16)
     new_ref[...] = new.reshape(seqs, rows, channels)
@@ -161,10 +168,10 @@
     split = size // pieces
     left = left_ref[...]
     for place in range(chunks_ref.shape[0]):
-        part = place % pieces
+        part = place // members
         chunks_ref[place, :, : left.shape[1]] = left
         chunks_ref[place, :, left.shape[1] :] = right_ref[
-            place // pieces, :, part * split : (part + 1) * split
+            place % members, :, part * split : (part + 1) * split
         ]
 
 
@@ -230,12 +237,13 @@
 def partial_kernel(tile_ref, line_ref, *refs):
     before_ref, out_ref, scr = refs if len(refs) == 3 else (None,) + refs
     groups, depth = tile_ref.shape[:2]
-    lines = line_ref.shape[0]
     scr[...] = line_ref[...].astype(F32)
+    per_part = out_ref.shape[-3]
 
     def one(g, carry):
         tiles = [[tile_ref[2 * g + u, k].astype(F32) for k in range(depth)] for u in range(2)]
-        for n in range(lines):
+        for n in range(line_ref.shape[0]):
+            part, place = divmod(n, per_part)
             totals = [None, None]
             for k in range(depth):
                 line = scr[n, k : k + 1, :]
@@ -244,11 +252,10 @@
                     totals[u] = term if k == 0 else totals[u] + term
             for u in range(2):
                 if before_ref is None:
-                    out_ref[2 * g + u, n] = totals[u].astype(BF16)
+                    out_ref[part, 2 * g + u, place] = totals[u].astype(BF16)
                 else:
-                    part, line_place = divmod(n, out_ref.shape[3])
-                    out_ref[2 * g + u, part, 0, line_place] = before_ref[2 * g + u, n]
-                    out_ref[2 * g + u, part, 1, line_place] = totals[u].astype(BF16)
+                    out_ref[part, 2 * g + u, 0, place] = before_ref[part, 2 * g + u, place]
+                    out_ref[part, 2 * g + u, 1, place] = totals[u].astype(BF16)
         return carry
 
     lax.fori_loop(0, groups // 2, one, 0)
@@ -257,12 +264,10 @@
 def partial_sums(tiles, lines, before=None):
     groups, depth, height, width = tiles.shape
     count = lines.shape[0]
-    shape = (groups, count, height, width)
-    if before is not None:
-        shape = (groups, 2, 2, count // 2, height, width)
+    beside = () if before is None else (2,)
     return kernel_call(
         partial_kernel,
-        [(shape, BF16)],
+        [((2, groups) + beside + (count // 2, height, width), BF16)],
         (tiles, lines) if before is None else (tiles, lines, before),
         scratch=[((count, depth, width), F32)],
         flops=2 * groups * count * height * width * depth,
@@ -339,8 +344,8 @@
         functools.partial(bias_kernel, rows), [((cols, heads * rows), BF16)], (pair_features, bias_weight.T)
     )[0]
     chunks = kernel_call(normed_kernel, [((ROWS, seqs, rows, channels), BF16)], (alignment,))[0]
-    everyone = exchange(chunks, ROW)
-    bias, query_matrix = double_up(bias[None], query_matrix)
+    everyone = exchange(chunks, ROW_X_FIRST)
+    bias, query_matrix = from_col(bias, query_matrix)
     queries, gates = kernel_call(
         query_kernel,
         [((seqs, rows, channels), BF16), ((seqs * rows, channels), F32)],
@@ -362,9 +367,9 @@
 
     size = (rows + cols) * factor
     chunks = kernel_call(
-        factor_kernel, [((COLS, seqs, size), BF16)], (left, exchange(right, ROW))
+        factor_kernel, [((COLS, seqs, size), BF16)], (left, exchange(right, ROW_X_FIRST))
     )[0]
-    factors = exchange(chunks, COL).reshape(COLS * seqs, size)
+    factors = exchange(chunks, COL_X_FIRST).reshape(COLS * seqs, size)
     pair_one, left_edge, right_edge = kernel_call(
         outer_kernel,
         [((places, depth), BF16), ((rows, cols, depth), BF16), ((2, cols, cols, depth), BF16)],
@@ -386,7 +391,7 @@
     lines = jnp.concatenate([left_edge, swapped[:rows]], axis=1)
     lines = in_order(x_hi, lines, flip(lines, "xh"))
     partial = partial_sums(tiles, lines).reshape(ROWS, rows, cols, depth)
-    partial = exchange(partial, ("y", "xl"))
+    partial = exchange(partial, ("xl", "y"))
     pair_two, chunks, lines = kernel_call(
         middle_kernel,
         [
@@ -402,7 +407,7 @@
     lines = in_order(x_hi, lines, flip(lines, "xh"))
     other = flip(own, "core")
     partial = partial_sums(other, lines, partial_sums(own, lines))
-    partial = exchange(partial.reshape(ROWS, 2, cols, cols, depth), ("z", "xl"))
+    partial = exchange(partial.reshape(ROWS, 2, cols, cols, depth), ("xl", "z"))
     new_pair = kernel_call(
         last_kernel,
         [((rows, cols, depth), BF16)],

time: 184 us -> 175 us (0.951)
  waiting for transfers between devices: 68.7 us -> 64.8 us
  blocking collectives: 18.8 us -> 15.2 us
  starting transfers between devices: 77.8 us -> 75.8 us
    ppermute x4 -> x6, starting transfers between devices: 15.1 us -> 24.8 us  [flip(): return lax.ppermute(block, axis, FLIP)]
    all_to_all x6, starting transfers between devices: 41.4 us -> 34.1 us  [exchange(): return lax.all_to_all(chunks, axes, 0, 0)]
    ppermute x5 -> x4, waiting for transfers between devices: 7.25 us -> 2.59 us  [shifted(): lax.ppermute(block, 'y', [(y, (y - step) % size) for y in range(size)])]
    ppermute x5 -> x4, starting transfers between devices: 20 us -> 15.4 us  [shifted(): lax.ppermute(block, 'y', [(y, (y - step) % size) for y in range(size)])]
    all_to_all x1, blocking collectives: 18.8 us -> 15.2 us  [exchange(): return lax.all_to_all(chunks, axes, 0, 0)]
    ppermute x4 -> x6, waiting for transfers between devices: 5.16 us -> 7.43 us  [flip(): return lax.ppermute(block, axis, FLIP)]
  transfers between devices with their start and end apart: 17 -> 18, of which waited for: 13 -> 11; matrix products, arithmetic and copies ran while one was open for 0% -> 0% of each run, Pallas kernels for 1% -> 1%
where the time goes in v4:
time: 175 us; the launch traced here: 173 us
  starting transfers between devices  75.8 us (43%)
  waiting for transfers between devices  64.8 us (37%)
  blocking collectives  15.2 us (9%)
  Pallas kernels  13.8 us (8%)
  local copies, waits for them, and re-layouts  2.46 us (1%)
    all_to_all x6, waiting for transfers between devices, exchange(): return lax.all_to_all(chunks, axes, 0, 0)  54.8 us
    all_to_all x6, starting transfers between devices, exchange(): return lax.all_to_all(chunks, axes, 0, 0)  34.1 us
    ppermute x6, starting transfers between devices, flip(): return lax.ppermute(block, axis, FLIP)  24.8 us
    ppermute x4, starting transfers between devices, shifted(): lax.ppermute(block, 'y', [(y, (y - step) % size) for y in range(size)])  15.4 us
    all_to_all x1, blocking collectives, exchange(): return lax.all_to_all(chunks, axes, 0, 0)  15.2 us
    pallas_call x12, Pallas kernels, kernel_call(): pl.pallas_call(body, out_shape=shapes, in_specs=[vmem] * len(args), out_s...  13.8 us
    ppermute x6, waiting for transfers between devices, flip(): return lax.ppermute(block, axis, FLIP)  7.43 us
  transfers between devices with their start and end apart: 18, of which 11 were waited for; matrix products, arithmetic and copies ran while one was open for 0% of the time, Pallas kernels for 1%

profile of v4, /device:TPU:1, one launch (start us, length us, event | category | flops | bytes accessed | tf_op | source)
XLA Modules:
  0.0 173.4 jit_solution(9352532459026459011)
XLA Ops:
  2.4 8.8 %collective-permute-start = (bf16[1,1,1,8,128]{4,3,2,1,0:T(8,128)(2,1)S(1)}, bf16[1,1,1,8,128]{4,3,2,1,0:T(8,128)(2,1)S(1)}, u32[]{:S(2)}, u32[]{:S(2)}) collective-permute-start(bf16[1,1,1,8,128]{4,3,2,1,0:T(8,128)(2,1)S(1)} %bitcast.18), channel_id=1, source_target_pairs={{0,1},{1,0},{2,3},{3,2},{4,5},{5,4},{6,7},{7,6},{8,9},{9,8},{10,11... | collective-permute-start | bytes 6152 | tf_op jit(solution)/shard_map/ppermute | solution.py:40
  12.0 1.3 shard_map.176
  13.3 7.4 %all-to-all-start = ((bf16[16,8,16,256]{3,2,1,0:T(8,128)(2,1)}), bf16[16,8,16,256]{3,2,1,0:T(8,128)(2,1)S(1)}, u32[]{:S(2)}, u32[]{:S(2)}) async-start(bf16[16,8,16,256]{3,2,1,0:T(8,128)(2,1)} %shard_map.176), calls=%async_computation | async-start | bytes 2097152 | tf_op jit(solution)/shard_map/all_to_all | solution.py:36
  20.7 5.1 %collective-permute-start.1 = (bf16[1,1,2,8,128]{4,3,2,1,0:T(8,128)(2,1)S(1)}, bf16[1,1,2,8,128]{4,3,2,1,0:T(8,128)(2,1)S(1)}, u32[]{:S(2)}, u32[]{:S(2)}) collective-permute-start(bf16[1,1,2,8,128]{4,3,2,1,0:T(8,128)(2,1)S(1)} %pad_maximum_fusion.7), channel_id=1, source_target_pairs={{0,28},{4,0},{8,4},{12,8},{16,12},{20,16},{24,20},{28,24},{1,29},{... | collective-permute-start | bytes 12296 | tf_op jit(solution)/shard_map/ppermute | solution.py:72
  25.8 2.1 %collective-permute-start.3 = (bf16[1,1,2,8,128]{4,3,2,1,0:T(8,128)(2,1)S(1)}, bf16[1,1,2,8,128]{4,3,2,1,0:T(8,128)(2,1)S(1)}, u32[]{:S(2)}, u32[]{:S(2)}) collective-permute-start(bf16[1,1,2,8,128]{4,3,2,1,0:T(8,128)(2,1)S(1)} %pad_maximum_fusion.7), channel_id=1, source_target_pairs={{0,4},{4,8},{8,12},{12,16},{16,20},{20,24},{24,28},{28,0},{1,5},{5... | collective-permute-start | bytes 12296 | tf_op jit(solution)/shard_map/ppermute | solution.py:72
  27.9 4.7 %collective-permute-start.2 = (bf16[1,2,2,8,128]{4,3,2,1,0:T(8,128)(2,1)S(1)}, bf16[1,2,2,8,128]{4,3,2,1,0:T(8,128)(2,1)S(1)}, u32[]{:S(2)}, u32[]{:S(2)}) collective-permute-start(bf16[1,2,2,8,128]{4,3,2,1,0:T(8,128)(2,1)S(1)} %pad_maximum_fusion.6), channel_id=1, source_target_pairs={{0,12},{4,16},{8,20},{12,24},{16,28},{20,0},{24,4},{28,8},{1,13},{... | collective-permute-start | bytes 24584 | tf_op jit(solution)/shard_map/ppermute | solution.py:72
  32.6 3.6 %collective-permute-start.4 = (bf16[1,3,2,8,128]{4,3,2,1,0:T(8,128)(2,1)S(1)}, bf16[1,3,2,8,128]{4,3,2,1,0:T(8,128)(2,1)S(1)}, u32[]{:S(2)}, u32[]{:S(2)}) collective-permute-start(bf16[1,3,2,8,128]{4,3,2,1,0:T(8,128)(2,1)S(1)} %pad_maximum_fusion.5), channel_id=1, source_target_pairs={{0,20},{4,24},{8,28},{12,0},{16,4},{20,8},{24,12},{28,16},{1,21},{... | collective-permute-start | bytes 36872 | tf_op jit(solution)/shard_map/ppermute | solution.py:72
  36.3 2.6 %collective-permute-done.4 = bf16[1,3,2,8,128]{4,3,2,1,0:T(8,128)(2,1)S(1)} collective-permute-done((bf16[1,3,2,8,128]{4,3,2,1,0:T(8,128)(2,1)S(1)}, bf16[1,3,2,8,128]{4,3,2,1,0:T(8,128)(2,1)S(1)}, u32[]{:S(2)}, u32[]{:S(2)}) %collective-permute-start.4) | collective-permute-done | bytes 12320 | tf_op jit(solution)/shard_map/ppermute | solution.py:72
  38.9 2.2 %collective-permute-start.5 = (bf16[1,8,2,8,128]{4,3,2,1,0:T(8,128)(2,1)S(1)}, bf16[1,8,2,8,128]{4,3,2,1,0:T(8,128)(2,1)S(1)}, u32[]{:S(2)}, u32[]{:S(2)}) collective-permute-start(bf16[1,8,2,8,128]{4,3,2,1,0:T(8,128)(2,1)S(1)} %constant_dynamic-slice_fusion), channel_id=1, source_target_pairs={{0,2},{2,0},{1,3},{3,1},{4,6},{6,4},{5,7},{7,5},{8,10},{10,8},{9,1... | collective-permute-start | bytes 98312 | tf_op jit(solution)/shard_map/ppermute | solution.py:40
  41.6 2.5 %collective-permute-done.5 = bf16[1,8,2,8,128]{4,3,2,1,0:T(8,128)(2,1)S(1)} collective-permute-done((bf16[1,8,2,8,128]{4,3,2,1,0:T(8,128)(2,1)S(1)}, bf16[1,8,2,8,128]{4,3,2,1,0:T(8,128)(2,1)S(1)}, u32[]{:S(2)}, u32[]{:S(2)}) %collective-permute-start.5) | collective-permute-done | bytes 32800 | tf_op jit(solution)/shard_map/ppermute | solution.py:40
  44.1 3.1 %all-to-all-done.every_ref = bf16[16,8,16,256]{3,2,1,0:T(8,128)(2,1)S(1)} async-done(((bf16[16,8,16,256]{3,2,1,0:T(8,128)(2,1)}), bf16[16,8,16,256]{3,2,1,0:T(8,128)(2,1)S(1)}, u32[]{:S(2)}, u32[]{:S(2)}) %all-to-all-start) | async-done | bytes 1048608 | tf_op jit(solution)/shard_map/all_to_all | solution.py:36
  47.3 3.0 %shard_map.179 = (bf16[8,16,256]{2,1,0:T(8,128)(2,1)}, bf16[8,512]{1,0:T(8,128)(2,1)S(1)}, bf16[16,8,512]{2,1,0:T(8,128)(2,1)S(1)}) custom-call(bf16[16,8,16,256]{3,2,1,0:T(8,128)(2,1)S(1)} %all-to-all-done.every_ref, bf16[256,128]{1,0:T(8,128)(2,1)S(1)} %bitcast.15, bf16[8,16,256]{2,1,0:T(8,128)(2,1)S(1)} %get-tuple-element.17.query_ref, ...), custom_call_target="tpu_custom_call" | custom-call | bytes 2007040 | tf_op jit(solution)/shard_map/pallas_call | solution.py:58
  50.3 15.2 %all_to_all.35.right_ref = bf16[16,8,512]{2,1,0:T(8,128)(2,1)S(1)} all-to-all(bf16[16,8,512]{2,1,0:T(8,128)(2,1)S(1)} %get-tuple-element.21), channel_id=1, replica_groups=mesh['z'=8,'xh'=2,'y'=8,'xl'=2,'core'=2] {'xh','z'}, dimensions={0} | all-to-all | bytes 262144 | tf_op jit(solution)/shard_map/all_to_all | solution.py:36
  66.3 9.6 %all-to-all-start.2 = ((bf16[32,8,768]{2,1,0:T(8,128)(2,1)}), bf16[32,8,768]{2,1,0:T(8,128)(2,1)S(1)}, u32[]{:S(2)}, u32[]{:S(2)}) async-start(bf16[32,8,768]{2,1,0:T(8,128)(2,1)} %shard_map.180), calls=%async_computation.2 | async-start | bytes 786432 | tf_op jit(solution)/shard_map/all_to_all | solution.py:36
  75.9 13.4 %all-to-all-done.2 = bf16[32,8,768]{2,1,0:T(8,128)(2,1)S(1)} async-done(((bf16[32,8,768]{2,1,0:T(8,128)(2,1)}), bf16[32,8,768]{2,1,0:T(8,128)(2,1)S(1)}, u32[]{:S(2)}, u32[]{:S(2)}) %all-to-all-start.2) | async-done | bytes 393248 | tf_op jit(solution)/shard_map/all_to_all | solution.py:36
  89.2 1.1 shard_map.181
  90.4 2.5 %collective-permute-start.6 = (bf16[24,8,128]{2,1,0:T(8,128)(2,1)S(1)}, bf16[24,8,128]{2,1,0:T(8,128)(2,1)S(1)}, u32[]{:S(2)}, u32[]{:S(2)}) collective-permute-start(bf16[24,8,128]{2,1,0:T(8,128)(2,1)S(1)} %pad_maximum_fusion.4), channel_id=1, source_target_pairs={{0,1},{1,0},{2,3},{3,2},{4,5},{5,4},{6,7},{7,6},{8,9},{9,8},{10,11... | collective-permute-start | bytes 147464 | tf_op jit(solution)/shard_map/ppermute | solution.py:40
  94.6 3.4 %all-to-all-start.3 = ((bf16[8,16,8,128]{3,2,1,0:T(8,128)(2,1)}), bf16[8,16,8,128]{3,2,1,0:T(8,128)(2,1)S(1)}, u32[]{:S(2)}, u32[]{:S(2)}) async-start(bf16[8,16,8,128]{3,2,1,0:T(8,128)(2,1)} %shard_map.182), calls=%async_computation.3 | async-start | bytes 524288 | tf_op jit(solution)/shard_map/all_to_all | solution.py:36
  98.0 3.2 %collective-permute-start.7 = (bf16[16,16,128]{2,1,0:T(8,128)(2,1)S(1)}, bf16[16,16,128]{2,1,0:T(8,128)(2,1)S(1)}, u32[]{:S(2)}, u32[]{:S(2)}) collective-permute-start(bf16[16,16,128]{2,1,0:T(8,128)(2,1)S(1)} %pad_maximum_fusion.2), channel_id=1, source_target_pairs={{0,32},{32,0},{1,33},{33,1},{2,34},{34,2},{3,35},{35,3},{4,36},{36... | collective-permute-start | bytes 196616 | tf_op jit(solution)/shard_map/ppermute | solution.py:40
  101.2 3.6 %collective-permute-done.7 = bf16[16,16,128]{2,1,0:T(8,128)(2,1)S(1)} collective-permute-done((bf16[16,16,128]{2,1,0:T(8,128)(2,1)S(1)}, bf16[16,16,128]{2,1,0:T(8,128)(2,1)S(1)}, u32[]{:S(2)}, u32[]{:S(2)}) %collective-permute-start.7) | collective-permute-done | bytes 65568 | tf_op jit(solution)/shard_map/ppermute | solution.py:40
  104.9 5.4 %all-to-all-done.3.tile_ref = bf16[8,16,8,128]{3,2,1,0:T(8,128)(2,1)S(1)} async-done(((bf16[8,16,8,128]{3,2,1,0:T(8,128)(2,1)}), bf16[8,16,8,128]{3,2,1,0:T(8,128)(2,1)S(1)}, u32[]{:S(2)}, u32[]{:S(2)}) %all-to-all-start.3) | async-done | bytes 262176 | tf_op jit(solution)/shard_map/all_to_all | solution.py:36
  110.2 1.9 %shard_map.183 = bf16[2,8,16,8,128]{4,3,2,1,0:T(8,128)(2,1)} custom-call(bf16[8,16,8,128]{3,2,1,0:T(8,128)(2,1)S(1)} %all-to-all-done.3.tile_ref, bf16[32,16,128]{2,1,0:T(8,128)(2,1)S(1)} %pad_maximum_fusion.line_ref), custom_call_target="tpu_custom_call" | custom-call | flops 8388608 | bytes 917504 | tf_op jit(solution)/shard_map/pallas_call | solution.py:58
  112.2 4.2 %all-to-all-start.4 = ((bf16[16,16,8,128]{3,2,1,0:T(8,128)(2,1)}), bf16[16,16,8,128]{3,2,1,0:T(8,128)(2,1)S(1)}, u32[]{:S(2)}, u32[]{:S(2)}) async-start(bf16[16,16,8,128]{3,2,1,0:T(8,128)(2,1)} %bitcast.8), calls=%async_computation.4 | async-start | bytes 1048576 | tf_op jit(solution)/shard_map/all_to_all | solution.py:36
  117.1 12.5 %all-to-all-done.4.partial_ref = bf16[16,16,8,128]{3,2,1,0:T(8,128)(2,1)S(1)} async-done(((bf16[16,16,8,128]{3,2,1,0:T(8,128)(2,1)}), bf16[16,16,8,128]{3,2,1,0:T(8,128)(2,1)S(1)}, u32[]{:S(2)}, u32[]{:S(2)}) %all-to-all-start.4) | async-done | bytes 524320 | tf_op jit(solution)/shard_map/all_to_all | solution.py:36
  129.7 1.4 shard_map.184
  131.0 5.9 %all-to-all-start.5 = ((bf16[8,16,8,128]{3,2,1,0:T(8,128)(2,1)}), bf16[8,16,8,128]{3,2,1,0:T(8,128)(2,1)S(1)}, u32[]{:S(2)}, u32[]{:S(2)}) async-start(bf16[8,16,8,128]{3,2,1,0:T(8,128)(2,1)} %get-tuple-element.25), calls=%async_computation.5 | async-start | bytes 524288 | tf_op jit(solution)/shard_map/all_to_all | solution.py:36
  137.0 3.2 %collective-permute-start.10 = (bf16[8,16,128]{2,1,0:T(8,128)(2,1)S(1)}, bf16[8,16,128]{2,1,0:T(8,128)(2,1)S(1)}, u32[]{:S(2)}, u32[]{:S(2)}) collective-permute-start(bf16[8,16,128]{2,1,0:T(8,128)(2,1)S(1)} %get-tuple-element.26), channel_id=1, source_target_pairs={{0,32},{32,0},{1,33},{33,1},{2,34},{34,2},{3,35},{35,3},{4,36},{36... | collective-permute-start | bytes 98312 | tf_op jit(solution)/shard_map/ppermute | solution.py:40
  140.1 6.6 %all-to-all-done.5.tile_ref = bf16[8,16,8,128]{3,2,1,0:T(8,128)(2,1)S(1)} async-done(((bf16[8,16,8,128]{3,2,1,0:T(8,128)(2,1)}), bf16[8,16,8,128]{3,2,1,0:T(8,128)(2,1)S(1)}, u32[]{:S(2)}, u32[]{:S(2)}) %all-to-all-start.5) | async-done | bytes 262176 | tf_op jit(solution)/shard_map/all_to_all | solution.py:36
  146.7 4.9 %collective-permute-start.9 = (bf16[8,16,8,128]{3,2,1,0:T(8,128)(2,1)S(1)}, bf16[8,16,8,128]{3,2,1,0:T(8,128)(2,1)S(1)}, u32[]{:S(2)}, u32[]{:S(2)}) collective-permute-start(bf16[8,16,8,128]{3,2,1,0:T(8,128)(2,1)S(1)} %all-to-all-done.5.tile_ref), channel_id=1, source_target_pairs={{0,1},{1,0},{2,3},{3,2},{4,5},{5,4},{6,7},{7,6},{8,9},{9,8},{10,11... | collective-permute-start | bytes 786440 | tf_op jit(solution)/shard_map/ppermute | solution.py:40
  152.8 1.4 shard_map.186
  154.2 3.7 %all-to-all-start.6 = ((bf16[16,2,8,8,128]{4,3,2,1,0:T(8,128)(2,1)}), bf16[16,2,8,8,128]{4,3,2,1,0:T(8,128)(2,1)S(1)}, u32[]{:S(2)}, u32[]{:S(2)}) async-start(bf16[16,2,8,8,128]{4,3,2,1,0:T(8,128)(2,1)} %bitcast.9), calls=%async_computation.6 | async-start | bytes 1048576 | tf_op jit(solution)/shard_map/all_to_all | solution.py:36
  158.6 13.8 %all-to-all-done.6.partial_ref = bf16[16,2,8,8,128]{4,3,2,1,0:T(8,128)(2,1)S(1)} async-done(((bf16[16,2,8,8,128]{4,3,2,1,0:T(8,128)(2,1)}), bf16[16,2,8,8,128]{4,3,2,1,0:T(8,128)(2,1)S(1)}, u32[]{:S(2)}, u32[]{:S(2)}) %all-to-all-start.6) | async-done | bytes 524320 | tf_op jit(solution)/shard_map/all_to_all | solution.py:36
  (82 shorter events, 9.0 us)
Async XLA Ops:
  2.4 18.3 %collective-permute-start = (bf16[1,1,1,8,128]{4,3,2,1,0:T(8,128)(2,1)S(1)}, bf16[1,1,1,8,128]{4,3,2,1,0:T(8,128)(2,1)S(1)}, u32[]{:S(2)}, u32[]{:S(2)}) collective-permute-start(bf16[1,1,1,8,128]{4,3,2,1,0:T(8,128)(2,1)S(1)} %bitcast.18), channel_id=1, source_target_pairs={{0,1},{1,0},{2,3},{3,2},{4,5},{5,4},{6,7},{7,6},{8,9},{9,8},{10,11... | collective-permute-start | bytes 6152 | tf_op jit(solution)/shard_map/ppermute | solution.py:40
  13.3 27.9 %copy-start.10 = (bf16[256,256]{1,0:T(8,128)(2,1)S(1)}, bf16[256,256]{1,0:T(8,128)(2,1)}, u32[]{:S(2)}) copy-start(bf16[256,256]{1,0:T(8,128)(2,1)} %gate_w_ref.3) | copy-start | bytes 393220
  13.3 34.0 %all-to-all-start = ((bf16[16,8,16,256]{3,2,1,0:T(8,128)(2,1)}), bf16[16,8,16,256]{3,2,1,0:T(8,128)(2,1)S(1)}, u32[]{:S(2)}, u32[]{:S(2)}) async-start(bf16[16,8,16,256]{3,2,1,0:T(8,128)(2,1)} %shard_map.176), calls=%async_computation | async-start | bytes 2097152 | tf_op jit(solution)/shard_map/all_to_all | solution.py:36
  20.7 7.2 %collective-permute-start.1 = (bf16[1,1,2,8,128]{4,3,2,1,0:T(8,128)(2,1)S(1)}, bf16[1,1,2,8,128]{4,3,2,1,0:T(8,128)(2,1)S(1)}, u32[]{:S(2)}, u32[]{:S(2)}) collective-permute-start(bf16[1,1,2,8,128]{4,3,2,1,0:T(8,128)(2,1)S(1)} %pad_maximum_fusion.7), channel_id=1, source_target_pairs={{0,28},{4,0},{8,4},{12,8},{16,12},{20,16},{24,20},{28,24},{1,29},{... | collective-permute-start | bytes 12296 | tf_op jit(solution)/shard_map/ppermute | solution.py:72
  25.8 15.4 %copy-start.9 = (bf16[256,256]{1,0:T(8,128)(2,1)S(1)}, bf16[256,256]{1,0:T(8,128)(2,1)}, u32[]{:S(2)}) copy-start(bf16[256,256]{1,0:T(8,128)(2,1)} %query_w_ref) | copy-start | bytes 393220
  25.8 6.8 %collective-permute-start.3 = (bf16[1,1,2,8,128]{4,3,2,1,0:T(8,128)(2,1)S(1)}, bf16[1,1,2,8,128]{4,3,2,1,0:T(8,128)(2,1)S(1)}, u32[]{:S(2)}, u32[]{:S(2)}) collective-permute-start(bf16[1,1,2,8,128]{4,3,2,1,0:T(8,128)(2,1)S(1)} %pad_maximum_fusion.7), channel_id=1, source_target_pairs={{0,4},{4,8},{8,12},{12,16},{16,20},{20,24},{24,28},{28,0},{1,5},{5... | collective-permute-start | bytes 12296 | tf_op jit(solution)/shard_map/ppermute | solution.py:72
  27.9 8.3 %collective-permute-start.2 = (bf16[1,2,2,8,128]{4,3,2,1,0:T(8,128)(2,1)S(1)}, bf16[1,2,2,8,128]{4,3,2,1,0:T(8,128)(2,1)S(1)}, u32[]{:S(2)}, u32[]{:S(2)}) collective-permute-start(bf16[1,2,2,8,128]{4,3,2,1,0:T(8,128)(2,1)S(1)} %pad_maximum_fusion.6), channel_id=1, source_target_pairs={{0,12},{4,16},{8,20},{12,24},{16,28},{20,0},{24,4},{28,8},{1,13},{... | collective-permute-start | bytes 24584 | tf_op jit(solution)/shard_map/ppermute | solution.py:72
  32.6 6.2 %collective-permute-start.4 = (bf16[1,3,2,8,128]{4,3,2,1,0:T(8,128)(2,1)S(1)}, bf16[1,3,2,8,128]{4,3,2,1,0:T(8,128)(2,1)S(1)}, u32[]{:S(2)}, u32[]{:S(2)}) collective-permute-start(bf16[1,3,2,8,128]{4,3,2,1,0:T(8,128)(2,1)S(1)} %pad_maximum_fusion.5), channel_id=1, source_target_pairs={{0,20},{4,24},{8,28},{12,0},{16,4},{20,8},{24,12},{28,16},{1,21},{... | collective-permute-start | bytes 36872 | tf_op jit(solution)/shard_map/ppermute | solution.py:72
  38.9 5.2 %collective-permute-start.5 = (bf16[1,8,2,8,128]{4,3,2,1,0:T(8,128)(2,1)S(1)}, bf16[1,8,2,8,128]{4,3,2,1,0:T(8,128)(2,1)S(1)}, u32[]{:S(2)}, u32[]{:S(2)}) collective-permute-start(bf16[1,8,2,8,128]{4,3,2,1,0:T(8,128)(2,1)S(1)} %constant_dynamic-slice_fusion), channel_id=1, source_target_pairs={{0,2},{2,0},{1,3},{3,1},{4,6},{6,4},{5,7},{7,5},{8,10},{10,8},{9,1... | collective-permute-start | bytes 98312 | tf_op jit(solution)/shard_map/ppermute | solution.py:40
  41.2 6.1 %copy-start.5 = (bf16[256,256]{1,0:T(8,128)(2,1)S(1)}, bf16[256,256]{1,0:T(8,128)(2,1)}, u32[]{:S(2)}) copy-start(bf16[256,256]{1,0:T(8,128)(2,1)} %out_w_ref.3) | copy-start | bytes 393220
  41.2 6.1 %copy-start.16 = (bf16[256,32]{0,1:T(8,128)(2,1)S(1)}, bf16[256,32]{0,1:T(8,128)(2,1)}, u32[]{:S(2)}) copy-start(bf16[256,32]{0,1:T(8,128)(2,1)} %param.25) | copy-start | bytes 49156
  41.2 6.1 %copy-start.17 = (bf16[256,32]{0,1:T(8,128)(2,1)S(1)}, bf16[256,32]{0,1:T(8,128)(2,1)}, u32[]{:S(2)}) copy-start(bf16[256,32]{0,1:T(8,128)(2,1)} %param.26) | copy-start | bytes 49156
  41.6 5.7 %copy-start.3 = (bf16[256,256]{1,0:T(8,128)(2,1)S(1)}, bf16[256,256]{1,0:T(8,128)(2,1)}, u32[]{:S(2)}) copy-start(bf16[256,256]{1,0:T(8,128)(2,1)} %key_w_ref.1) | copy-start | bytes 393220
  66.3 22.9 %copy-start.2 = (bf16[1024,128]{1,0:T(8,128)(2,1)S(1)}, bf16[1024,128]{1,0:T(8,128)(2,1)}, u32[]{:S(2)}) copy-start(bf16[1024,128]{1,0:T(8,128)(2,1)} %outer_w_ref.1) | copy-start | bytes 786436
  66.3 22.9 %copy-start.6 = (bf16[128,512]{1,0:T(8,128)(2,1)S(1)}, bf16[128,512]{1,0:T(8,128)(2,1)}, u32[]{:S(2)}) copy-start(bf16[128,512]{1,0:T(8,128)(2,1)} %in_w_ref.2) | copy-start | bytes 393220
  66.3 22.9 %copy-start.8 = (bf16[16,8,128]{2,1,0:T(8,128)(2,1)S(1)}, bf16[16,8,128]{2,1,0:T(8,128)(2,1)}, u32[]{:S(2)}) copy-start(bf16[16,8,128]{2,1,0:T(8,128)(2,1)} %pair_ref.3) | copy-start | bytes 98308
  66.3 22.9 %all-to-all-start.2 = ((bf16[32,8,768]{2,1,0:T(8,128)(2,1)}), bf16[32,8,768]{2,1,0:T(8,128)(2,1)S(1)}, u32[]{:S(2)}, u32[]{:S(2)}) async-start(bf16[32,8,768]{2,1,0:T(8,128)(2,1)} %shard_map.180), calls=%async_computation.2 | async-start | bytes 786432 | tf_op jit(solution)/shard_map/all_to_all | solution.py:36
  90.4 3.4 %collective-permute-start.6 = (bf16[24,8,128]{2,1,0:T(8,128)(2,1)S(1)}, bf16[24,8,128]{2,1,0:T(8,128)(2,1)S(1)}, u32[]{:S(2)}, u32[]{:S(2)}) collective-permute-start(bf16[24,8,128]{2,1,0:T(8,128)(2,1)S(1)} %pad_maximum_fusion.4), channel_id=1, source_target_pairs={{0,1},{1,0},{2,3},{3,2},{4,5},{5,4},{6,7},{7,6},{8,9},{9,8},{10,11... | collective-permute-start | bytes 147464 | tf_op jit(solution)/shard_map/ppermute | solution.py:40
  94.6 15.7 %all-to-all-start.3 = ((bf16[8,16,8,128]{3,2,1,0:T(8,128)(2,1)}), bf16[8,16,8,128]{3,2,1,0:T(8,128)(2,1)S(1)}, u32[]{:S(2)}, u32[]{:S(2)}) async-start(bf16[8,16,8,128]{3,2,1,0:T(8,128)(2,1)} %shard_map.182), calls=%async_computation.3 | async-start | bytes 524288 | tf_op jit(solution)/shard_map/all_to_all | solution.py:36
  98.0 6.8 %collective-permute-start.7 = (bf16[16,16,128]{2,1,0:T(8,128)(2,1)S(1)}, bf16[16,16,128]{2,1,0:T(8,128)(2,1)S(1)}, u32[]{:S(2)}, u32[]{:S(2)}) collective-permute-start(bf16[16,16,128]{2,1,0:T(8,128)(2,1)S(1)} %pad_maximum_fusion.2), channel_id=1, source_target_pairs={{0,32},{32,0},{1,33},{33,1},{2,34},{34,2},{3,35},{35,3},{4,36},{36... | collective-permute-start | bytes 196616 | tf_op jit(solution)/shard_map/ppermute | solution.py:40
  112.2 17.5 %copy-start.11 = (bf16[128,512]{1,0:T(8,128)(2,1)S(1)}, bf16[128,512]{1,0:T(8,128)(2,1)}, u32[]{:S(2)}) copy-start(bf16[128,512]{1,0:T(8,128)(2,1)} %in_w_ref.3) | copy-start | bytes 393220
  112.2 17.5 %copy-start.12 = (bf16[128,128]{1,0:T(8,128)(2,1)S(1)}, bf16[128,128]{1,0:T(8,128)(2,1)}, u32[]{:S(2)}) copy-start(bf16[128,128]{1,0:T(8,128)(2,1)} %gate_w_ref.4) | copy-start | bytes 98308
  112.2 17.5 %copy-start.13 = (bf16[128,128]{1,0:T(8,128)(2,1)S(1)}, bf16[128,128]{1,0:T(8,128)(2,1)}, u32[]{:S(2)}) copy-start(bf16[128,128]{1,0:T(8,128)(2,1)} %out_w_ref.4) | copy-start | bytes 98308
  112.2 17.5 %all-to-all-start.4 = ((bf16[16,16,8,128]{3,2,1,0:T(8,128)(2,1)}), bf16[16,16,8,128]{3,2,1,0:T(8,128)(2,1)S(1)}, u32[]{:S(2)}, u32[]{:S(2)}) async-start(bf16[16,16,8,128]{3,2,1,0:T(8,128)(2,1)} %bitcast.8), calls=%async_computation.4 | async-start | bytes 1048576 | tf_op jit(solution)/shard_map/all_to_all | solution.py:36
  116.4 0.7 collective-permute-start.8
  131.0 15.7 %all-to-all-start.5 = ((bf16[8,16,8,128]{3,2,1,0:T(8,128)(2,1)}), bf16[8,16,8,128]{3,2,1,0:T(8,128)(2,1)S(1)}, u32[]{:S(2)}, u32[]{:S(2)}) async-start(bf16[8,16,8,128]{3,2,1,0:T(8,128)(2,1)} %get-tuple-element.25), calls=%async_computation.5 | async-start | bytes 524288 | tf_op jit(solution)/shard_map/all_to_all | solution.py:36
  137.0 14.7 %collective-permute-start.10 = (bf16[8,16,128]{2,1,0:T(8,128)(2,1)S(1)}, bf16[8,16,128]{2,1,0:T(8,128)(2,1)S(1)}, u32[]{:S(2)}, u32[]{:S(2)}) collective-permute-start(bf16[8,16,128]{2,1,0:T(8,128)(2,1)S(1)} %get-tuple-element.26), channel_id=1, source_target_pairs={{0,32},{32,0},{1,33},{33,1},{2,34},{34,2},{3,35},{35,3},{4,36},{36... | collective-permute-start | bytes 98312 | tf_op jit(solution)/shard_map/ppermute | solution.py:40
  146.7 6.1 %collective-permute-start.9 = (bf16[8,16,8,128]{3,2,1,0:T(8,128)(2,1)S(1)}, bf16[8,16,8,128]{3,2,1,0:T(8,128)(2,1)S(1)}, u32[]{:S(2)}, u32[]{:S(2)}) collective-permute-start(bf16[8,16,8,128]{3,2,1,0:T(8,128)(2,1)S(1)} %all-to-all-done.5.tile_ref), channel_id=1, source_target_pairs={{0,1},{1,0},{2,3},{3,2},{4,5},{5,4},{6,7},{7,6},{8,9},{9,8},{10,11... | collective-permute-start | bytes 786440 | tf_op jit(solution)/shard_map/ppermute | solution.py:40
  154.2 18.2 %copy-start.14 = (bf16[128,128]{1,0:T(8,128)(2,1)S(1)}, bf16[128,128]{1,0:T(8,128)(2,1)}, u32[]{:S(2)}) copy-start(bf16[128,128]{1,0:T(8,128)(2,1)} %gate_w_ref.5) | copy-start | bytes 98308
  154.2 18.2 %copy-start.15 = (bf16[128,128]{1,0:T(8,128)(2,1)S(1)}, bf16[128,128]{1,0:T(8,128)(2,1)}, u32[]{:S(2)}) copy-start(bf16[128,128]{1,0:T(8,128)(2,1)} %out_w_ref.5) | copy-start | bytes 98308
  154.2 18.1 %all-to-all-start.6 = ((bf16[16,2,8,8,128]{4,3,2,1,0:T(8,128)(2,1)}), bf16[16,2,8,8,128]{4,3,2,1,0:T(8,128)(2,1)S(1)}, u32[]{:S(2)}, u32[]{:S(2)}) async-start(bf16[16,2,8,8,128]{4,3,2,1,0:T(8,128)(2,1)} %bitcast.9), calls=%async_computation.6 | async-start | bytes 1048576 | tf_op jit(solution)/shard_map/all_to_all | solution.py:36
  157.9 0.7 collective-permute-start.11
  (5 other events, 10.3 us)

commit v5 on v4

--- a/solution.py
+++ b/solution.py
@@ -50,7 +50,7 @@
     return jnp.concatenate([lower, upper], axis=axis)
 
 
-def kernel_call(body, outs, args, scratch=(), flops=0, aliases=None):
+def kernel_call(body, outs, args, scratch=(), flops=0, fetched=False):
     shapes = [jax.ShapeDtypeStruct(s, d) for s, d in outs]
     vmem = pl.BlockSpec(memory_space=pltpu.VMEM)
     size = sum(a.size * a.dtype.itemsize for a in args)
@@ -58,10 +58,9 @@
     return pl.pallas_call(
         body,
         out_shape=shapes,
-        in_specs=[vmem] * len(args),
+        in_specs=[pl.BlockSpec() if fetched else vmem] * len(args),
         out_specs=[vmem] * len(shapes),
         scratch_shapes=[pltpu.VMEM(s, d) for s, d in scratch],
-        input_output_aliases=aliases or {},
         compiler_params=pltpu.CompilerParams(vmem_limit_bytes=40 * 2**20),
         cost_estimate=pl.CostEstimate(flops=flops, bytes_accessed=size, transcendentals=0),
     )(*args)
@@ -173,13 +172,6 @@
         chunks_ref[place, :, left.shape[1] :] = right_ref[
             place % members, :, part * split : (part + 1) * split
         ]
-
-
-def tile_kernel(mine_ref, theirs_ref, chunks_ref):
-    own = mine_ref.shape[0]
-    for member in range(chunks_ref.shape[0]):
-        chunks_ref[member, :own] = mine_ref[...]
-        chunks_ref[member, own:] = theirs_ref[...]
 
 
 def edge_parts(pair, in_w_ref):
@@ -230,18 +222,23 @@
     right_scr[...] = right
     for k in range(cols):
         line = right_scr[pl.ds(k, rows, stride=cols), :].astype(BF16)
-        right_out[0, k] = line[:cols]
-        right_out[1, k] = line[cols:]
+        for half in range(right_out.shape[0]):
+            for member in range(right_out.shape[1]):
+                right_out[half, member, k] = line[half * cols : (half + 1) * cols]
 
 
 def partial_kernel(tile_ref, line_ref, *refs):
     before_ref, out_ref, scr = refs if len(refs) == 3 else (None,) + refs
-    groups, depth = tile_ref.shape[:2]
+    sides, groups, side = tile_ref.shape[:3]
+    depth = sides * side
     scr[...] = line_ref[...].astype(F32)
     per_part = out_ref.shape[-3]
 
     def one(g, carry):
-        tiles = [[tile_ref[2 * g + u, k].astype(F32) for k in range(depth)] for u in range(2)]
+        tiles = [
+            [tile_ref[k // side, 2 * g + u, k % side].astype(F32) for k in range(depth)]
+            for u in range(2)
+        ]
         for n in range(line_ref.shape[0]):
             part, place = divmod(n, per_part)
             totals = [None, None]
@@ -262,8 +259,8 @@
 
 
 def partial_sums(tiles, lines, before=None):
-    groups, depth, height, width = tiles.shape
-    count = lines.shape[0]
+    _, groups, _, height, width = tiles.shape
+    count, depth = lines.shape[:2]
     beside = () if before is None else (2,)
     return kernel_call(
         partial_kernel,
@@ -340,10 +337,16 @@
     full = COLS * cols
     core, x_hi = lax.axis_index("core"), lax.axis_index("xh")
 
+    chunks = kernel_call(
+        normed_kernel, [((ROWS, seqs, rows, channels), BF16)], (alignment,), fetched=True
+    )[0]
+    chunks, later_pair = lax.optimization_barrier((chunks, pair_features))
     bias = kernel_call(
-        functools.partial(bias_kernel, rows), [((cols, heads * rows), BF16)], (pair_features, bias_weight.T)
+        functools.partial(bias_kernel, rows),
+        [((cols, heads * rows), BF16)],
+        (later_pair, bias_weight.T),
+        fetched=True,
     )[0]
-    chunks = kernel_call(normed_kernel, [((ROWS, seqs, rows, channels), BF16)], (alignment,))[0]
     everyone = exchange(chunks, ROW_X_FIRST)
     bias, query_matrix = from_col(bias, query_matrix)
     queries, gates = kernel_call(
@@ -372,7 +375,7 @@
     factors = exchange(chunks, COL_X_FIRST).reshape(COLS * seqs, size)
     pair_one, left_edge, right_edge = kernel_call(
         outer_kernel,
-        [((places, depth), BF16), ((rows, cols, depth), BF16), ((2, cols, cols, depth), BF16)],
+        [((places, depth), BF16), ((rows, cols, depth), BF16), ((2, SIZES["z"], cols, cols, depth), BF16)],
         (factors, pair_features, outer_weight, outgoing_project),
         scratch=[
             ((cols * factor // 128, rows * factor, 128), F32),
@@ -381,14 +384,9 @@
         ],
     )
 
-    mine = lax.dynamic_index_in_dim(right_edge, core, 0, keepdims=False)
-    theirs = lax.dynamic_index_in_dim(right_edge, 1 - core, 0, keepdims=False)
-    swapped = flip(jnp.concatenate([left_edge, theirs], axis=0), "core")
-    chunks = kernel_call(
-        tile_kernel, [((SIZES["z"], 2 * cols, cols, depth), BF16)], (mine, swapped[rows:])
-    )[0]
-    tiles = exchange(chunks, "z")
-    lines = jnp.concatenate([left_edge, swapped[:rows]], axis=1)
+    chunks = right_edge.reshape((ROWS,) + right_edge.shape[2:])
+    tiles = exchange(chunks, ("core", "z")).reshape(right_edge.shape)
+    lines = in_order(core, left_edge, flip(left_edge, "core"), axis=1)
     lines = in_order(x_hi, lines, flip(lines, "xh"))
     partial = partial_sums(tiles, lines).reshape(ROWS, rows, cols, depth)
     partial = exchange(partial, ("xl", "y"))
@@ -406,7 +404,7 @@
     own = exchange(chunks, "y")
     lines = in_order(x_hi, lines, flip(lines, "xh"))
     other = flip(own, "core")
-    partial = partial_sums(other, lines, partial_sums(own, lines))
+    partial = partial_sums(other[None], lines, partial_sums(own[None], lines))
     partial = exchange(partial.reshape(ROWS, 2, cols, cols, depth), ("xl", "z"))
     new_pair = kernel_call(
         last_kernel,

time: 175 us -> 170 us (0.971)
  blocking collectives: 15.2 us -> 37.9 us
  waiting for transfers between devices: 64.8 us -> 46.2 us
  starting transfers between devices: 75.8 us -> 68.6 us
    all_to_all x1 -> x2, blocking collectives: 15.2 us -> 37.9 us  [exchange(): return lax.all_to_all(chunks, axes, 0, 0)]
    all_to_all x6 -> x5, waiting for transfers between devices: 54.8 us -> 36.8 us  [exchange(): return lax.all_to_all(chunks, axes, 0, 0)]
    all_to_all x6 -> x5, starting transfers between devices: 34.1 us -> 26.7 us  [exchange(): return lax.all_to_all(chunks, axes, 0, 0)]
    pallas_call x12 -> x11, Pallas kernels: 13.8 us -> 13.2 us  [kernel_call(): pl.pallas_call(body, out_shape=shapes, in_specs=[pl.BlockSpec() if fetche...]
  transfers between devices with their start and end apart: 18 -> 17, of which waited for: 11 -> 9; matrix products, arithmetic and copies ran while one was open for 0% -> 0% of each run, Pallas kernels for 1% -> 1%
where the time goes in v5:
time: 170 us; the launch traced here: 168 us
  starting transfers between devices  68.6 us (40%)
  waiting for transfers between devices  46.2 us (27%)
  blocking collectives  37.9 us (22%)
  Pallas kernels  13.2 us (8%)
    all_to_all x2, blocking collectives, exchange(): return lax.all_to_all(chunks, axes, 0, 0)  37.9 us
    all_to_all x5, waiting for transfers between devices, exchange(): return lax.all_to_all(chunks, axes, 0, 0)  36.8 us
    all_to_all x5, starting transfers between devices, exchange(): return lax.all_to_all(chunks, axes, 0, 0)  26.7 us
    ppermute x6, starting transfers between devices, flip(): return lax.ppermute(block, axis, FLIP)  25.2 us
    ppermute x4, starting transfers between devices, shifted(): lax.ppermute(block, 'y', [(y, (y - step) % size) for y in range(size)])  15.4 us
    pallas_call x11, Pallas kernels, kernel_call(): pl.pallas_call(body, out_shape=shapes, in_specs=[pl.BlockSpec() if fetche...  13.2 us
    ppermute x6, waiting for transfers between devices, flip(): return lax.ppermute(block, axis, FLIP)  6.8 us
  transfers between devices with their start and end apart: 17, of which 9 were waited for; matrix products, arithmetic and copies ran while one was open for 0% of the time, Pallas kernels for 1%

profile of v5, /device:TPU:1, one launch (start us, length us, event | category | flops | bytes accessed | tf_op | source)
XLA Modules:
  0.0 168.2 jit_solution(8529436331918299339)
XLA Ops:
  1.5 1.3 shard_map.176
  3.1 8.8 %collective-permute-start = (bf16[1,1,1,8,128]{4,3,2,1,0:T(8,128)(2,1)S(1)}, bf16[1,1,1,8,128]{4,3,2,1,0:T(8,128)(2,1)S(1)}, u32[]{:S(2)}, u32[]{:S(2)}) collective-permute-start(bf16[1,1,1,8,128]{4,3,2,1,0:T(8,128)(2,1)S(1)} %bitcast.21), channel_id=1, source_target_pairs={{0,1},{1,0},{2,3},{3,2},{4,5},{5,4},{6,7},{7,6},{8,9},{9,8},{10,11... | collective-permute-start | bytes 6152 | tf_op jit(solution)/shard_map/ppermute | solution.py:40
  11.9 7.4 %all-to-all-start = ((bf16[16,8,16,256]{3,2,1,0:T(8,128)(2,1)}), bf16[16,8,16,256]{3,2,1,0:T(8,128)(2,1)S(1)}, u32[]{:S(2)}, u32[]{:S(2)}) async-start(bf16[16,8,16,256]{3,2,1,0:T(8,128)(2,1)} %shard_map.176), calls=%async_computation | async-start | bytes 2097152 | tf_op jit(solution)/shard_map/all_to_all | solution.py:36
  19.3 5.1 %collective-permute-start.1 = (bf16[1,1,2,8,128]{4,3,2,1,0:T(8,128)(2,1)S(1)}, bf16[1,1,2,8,128]{4,3,2,1,0:T(8,128)(2,1)S(1)}, u32[]{:S(2)}, u32[]{:S(2)}) collective-permute-start(bf16[1,1,2,8,128]{4,3,2,1,0:T(8,128)(2,1)S(1)} %pad_maximum_fusion.6), channel_id=1, source_target_pairs={{0,28},{4,0},{8,4},{12,8},{16,12},{20,16},{24,20},{28,24},{1,29},{... | collective-permute-start | bytes 12296 | tf_op jit(solution)/shard_map/ppermute | solution.py:71
  24.4 2.1 %collective-permute-start.3 = (bf16[1,1,2,8,128]{4,3,2,1,0:T(8,128)(2,1)S(1)}, bf16[1,1,2,8,128]{4,3,2,1,0:T(8,128)(2,1)S(1)}, u32[]{:S(2)}, u32[]{:S(2)}) collective-permute-start(bf16[1,1,2,8,128]{4,3,2,1,0:T(8,128)(2,1)S(1)} %pad_maximum_fusion.6), channel_id=1, source_target_pairs={{0,4},{4,8},{8,12},{12,16},{16,20},{20,24},{24,28},{28,0},{1,5},{5... | collective-permute-start | bytes 12296 | tf_op jit(solution)/shard_map/ppermute | solution.py:71
  26.5 4.7 %collective-permute-start.2 = (bf16[1,2,2,8,128]{4,3,2,1,0:T(8,128)(2,1)S(1)}, bf16[1,2,2,8,128]{4,3,2,1,0:T(8,128)(2,1)S(1)}, u32[]{:S(2)}, u32[]{:S(2)}) collective-permute-start(bf16[1,2,2,8,128]{4,3,2,1,0:T(8,128)(2,1)S(1)} %pad_maximum_fusion.5), channel_id=1, source_target_pairs={{0,12},{4,16},{8,20},{12,24},{16,28},{20,0},{24,4},{28,8},{1,13},{... | collective-permute-start | bytes 24584 | tf_op jit(solution)/shard_map/ppermute | solution.py:71
  31.2 3.6 %collective-permute-start.4 = (bf16[1,3,2,8,128]{4,3,2,1,0:T(8,128)(2,1)S(1)}, bf16[1,3,2,8,128]{4,3,2,1,0:T(8,128)(2,1)S(1)}, u32[]{:S(2)}, u32[]{:S(2)}) collective-permute-start(bf16[1,3,2,8,128]{4,3,2,1,0:T(8,128)(2,1)S(1)} %pad_maximum_fusion.4), channel_id=1, source_target_pairs={{0,20},{4,24},{8,28},{12,0},{16,4},{20,8},{24,12},{28,16},{1,21},{... | collective-permute-start | bytes 36872 | tf_op jit(solution)/shard_map/ppermute | solution.py:71
  34.9 2.6 %collective-permute-done.4 = bf16[1,3,2,8,128]{4,3,2,1,0:T(8,128)(2,1)S(1)} collective-permute-done((bf16[1,3,2,8,128]{4,3,2,1,0:T(8,128)(2,1)S(1)}, bf16[1,3,2,8,128]{4,3,2,1,0:T(8,128)(2,1)S(1)}, u32[]{:S(2)}, u32[]{:S(2)}) %collective-permute-start.4) | collective-permute-done | bytes 12320 | tf_op jit(solution)/shard_map/ppermute | solution.py:71
  37.6 2.2 %collective-permute-start.5 = (bf16[1,8,2,8,128]{4,3,2,1,0:T(8,128)(2,1)S(1)}, bf16[1,8,2,8,128]{4,3,2,1,0:T(8,128)(2,1)S(1)}, u32[]{:S(2)}, u32[]{:S(2)}) collective-permute-start(bf16[1,8,2,8,128]{4,3,2,1,0:T(8,128)(2,1)S(1)} %constant_dynamic-slice_fusion), channel_id=1, source_target_pairs={{0,2},{2,0},{1,3},{3,1},{4,6},{6,4},{5,7},{7,5},{8,10},{10,8},{9,1... | collective-permute-start | bytes 98312 | tf_op jit(solution)/shard_map/ppermute | solution.py:40
  40.2 2.5 %collective-permute-done.5 = bf16[1,8,2,8,128]{4,3,2,1,0:T(8,128)(2,1)S(1)} collective-permute-done((bf16[1,8,2,8,128]{4,3,2,1,0:T(8,128)(2,1)S(1)}, bf16[1,8,2,8,128]{4,3,2,1,0:T(8,128)(2,1)S(1)}, u32[]{:S(2)}, u32[]{:S(2)}) %collective-permute-start.5) | collective-permute-done | bytes 32800 | tf_op jit(solution)/shard_map/ppermute | solution.py:40
  42.7 3.1 %all-to-all-done.every_ref = bf16[16,8,16,256]{3,2,1,0:T(8,128)(2,1)S(1)} async-done(((bf16[16,8,16,256]{3,2,1,0:T(8,128)(2,1)}), bf16[16,8,16,256]{3,2,1,0:T(8,128)(2,1)S(1)}, u32[]{:S(2)}, u32[]{:S(2)}) %all-to-all-start) | async-done | bytes 1048608 | tf_op jit(solution)/shard_map/all_to_all | solution.py:36
  45.9 3.0 %shard_map.179 = (bf16[8,16,256]{2,1,0:T(8,128)(2,1)}, bf16[8,512]{1,0:T(8,128)(2,1)S(1)}, bf16[16,8,512]{2,1,0:T(8,128)(2,1)S(1)}) custom-call(bf16[16,8,16,256]{3,2,1,0:T(8,128)(2,1)S(1)} %all-to-all-done.every_ref, bf16[256,128]{1,0:T(8,128)(2,1)S(1)} %bitcast.17, bf16[8,16,256]{2,1,0:T(8,128)(2,1)S(1)} %get-tuple-element.21.query_ref, ...), custom_call_target="tpu_custom_call" | custom-call | bytes 2007040 | tf_op jit(solution)/shard_map/pallas_call | solution.py:58
  48.9 15.2 %all_to_all.35.right_ref = bf16[16,8,512]{2,1,0:T(8,128)(2,1)S(1)} all-to-all(bf16[16,8,512]{2,1,0:T(8,128)(2,1)S(1)} %get-tuple-element.25), channel_id=1, replica_groups=mesh['z'=8,'xh'=2,'y'=8,'xl'=2,'core'=2] {'xh','z'}, dimensions={0} | all-to-all | bytes 262144 | tf_op jit(solution)/shard_map/all_to_all | solution.py:36
  64.2 22.7 %all_to_all.36 = bf16[32,8,768]{2,1,0:T(8,128)(2,1)S(1)} all-to-all(bf16[32,8,768]{2,1,0:T(8,128)(2,1)S(1)} %shard_map.180), channel_id=1, replica_groups=mesh['z'=8,'xh'=2,'y'=8,'xl'=2,'core'=2] {'core','xl','y'}, dimensions={0} | all-to-all | bytes 786432 | tf_op jit(solution)/shard_map/all_to_all | solution.py:36
  86.9 1.9 %shard_map.181 = (bf16[128,128]{1,0:T(8,128)(2,1)S(1)}, bf16[16,8,128]{2,1,0:T(8,128)(2,1)S(1)}, bf16[2,8,8,8,128]{4,3,2,1,0:T(8,128)(2,1)}) custom-call(bf16[256,768]{1,0:T(8,128)(2,1)S(1)} %bitcast.14, bf16[16,8,128]{2,1,0:T(8,128)(2,1)S(1)} %copy-done.7, bf16[1024,128]{1,0:T(8,128)(2,1)S(1)} %copy-done.2, bf16[128,512]{1,0:T(8,128)(2,1)S(1)} %copy-done.6), custom_call_target="tpu_custom_call" | custom-call | bytes 1146880 | tf_op jit(solution)/shard_map/pallas_call | solution.py:58
  88.8 2.5 %collective-permute-start.6 = (bf16[16,8,128]{2,1,0:T(8,128)(2,1)S(1)}, bf16[16,8,128]{2,1,0:T(8,128)(2,1)S(1)}, u32[]{:S(2)}, u32[]{:S(2)}) collective-permute-start(bf16[16,8,128]{2,1,0:T(8,128)(2,1)S(1)} %get-tuple-element.27), channel_id=1, source_target_pairs={{0,1},{1,0},{2,3},{3,2},{4,5},{5,4},{6,7},{7,6},{8,9},{9,8},{10,11... | collective-permute-start | bytes 98312 | tf_op jit(solution)/shard_map/ppermute | solution.py:40
  91.3 3.4 %all-to-all-start.3 = ((bf16[16,8,8,128]{3,2,1,0:T(8,128)(2,1)}), bf16[16,8,8,128]{3,2,1,0:T(8,128)(2,1)S(1)}, u32[]{:S(2)}, u32[]{:S(2)}) async-start(bf16[16,8,8,128]{3,2,1,0:T(8,128)(2,1)} %bitcast.6), calls=%async_computation.3 | async-start | bytes 524288 | tf_op jit(solution)/shard_map/all_to_all | solution.py:36
  94.8 3.2 %collective-permute-start.7 = (bf16[16,16,128]{2,1,0:T(8,128)(2,1)S(1)}, bf16[16,16,128]{2,1,0:T(8,128)(2,1)S(1)}, u32[]{:S(2)}, u32[]{:S(2)}) collective-permute-start(bf16[16,16,128]{2,1,0:T(8,128)(2,1)S(1)} %pad_maximum_fusion.2), channel_id=1, source_target_pairs={{0,32},{32,0},{1,33},{33,1},{2,34},{34,2},{3,35},{35,3},{4,36},{36... | collective-permute-start | bytes 196616 | tf_op jit(solution)/shard_map/ppermute | solution.py:40
  98.1 3.8 %collective-permute-done.7 = bf16[16,16,128]{2,1,0:T(8,128)(2,1)S(1)} collective-permute-done((bf16[16,16,128]{2,1,0:T(8,128)(2,1)S(1)}, bf16[16,16,128]{2,1,0:T(8,128)(2,1)S(1)}, u32[]{:S(2)}, u32[]{:S(2)}) %collective-permute-start.7) | collective-permute-done | bytes 65568 | tf_op jit(solution)/shard_map/ppermute | solution.py:40
  102.0 2.2 %all-to-all-done.3 = bf16[16,8,8,128]{3,2,1,0:T(8,128)(2,1)S(1)} async-done(((bf16[16,8,8,128]{3,2,1,0:T(8,128)(2,1)}), bf16[16,8,8,128]{3,2,1,0:T(8,128)(2,1)S(1)}, u32[]{:S(2)}, u32[]{:S(2)}) %all-to-all-start.3) | async-done | bytes 262176 | tf_op jit(solution)/shard_map/all_to_all | solution.py:36
  104.1 2.0 %shard_map.182 = bf16[2,8,16,8,128]{4,3,2,1,0:T(8,128)(2,1)} custom-call(bf16[2,8,8,8,128]{4,3,2,1,0:T(8,128)(2,1)S(1)} %bitcast.15, bf16[32,16,128]{2,1,0:T(8,128)(2,1)S(1)} %pad_maximum_fusion.line_ref), custom_call_target="tpu_custom_call" | custom-call | flops 8388608 | bytes 917504 | tf_op jit(solution)/shard_map/pallas_call | solution.py:58
  106.1 4.2 %all-to-all-start.4 = ((bf16[16,16,8,128]{3,2,1,0:T(8,128)(2,1)}), bf16[16,16,8,128]{3,2,1,0:T(8,128)(2,1)S(1)}, u32[]{:S(2)}, u32[]{:S(2)}) async-start(bf16[16,16,8,128]{3,2,1,0:T(8,128)(2,1)} %bitcast.8), calls=%async_computation.4 | async-start | bytes 1048576 | tf_op jit(solution)/shard_map/all_to_all | solution.py:36
  111.0 12.3 %all-to-all-done.4.partial_ref = bf16[16,16,8,128]{3,2,1,0:T(8,128)(2,1)S(1)} async-done(((bf16[16,16,8,128]{3,2,1,0:T(8,128)(2,1)}), bf16[16,16,8,128]{3,2,1,0:T(8,128)(2,1)S(1)}, u32[]{:S(2)}, u32[]{:S(2)}) %all-to-all-start.4) | async-done | bytes 524320 | tf_op jit(solution)/shard_map/all_to_all | solution.py:36
  123.3 1.4 shard_map.183
  124.7 5.3 %all-to-all-start.5 = ((bf16[8,16,8,128]{3,2,1,0:T(8,128)(2,1)}), bf16[8,16,8,128]{3,2,1,0:T(8,128)(2,1)S(1)}, u32[]{:S(2)}, u32[]{:S(2)}) async-start(bf16[8,16,8,128]{3,2,1,0:T(8,128)(2,1)} %get-tuple-element.29), calls=%async_computation.5 | async-start | bytes 524288 | tf_op jit(solution)/shard_map/all_to_all | solution.py:36
  130.0 3.2 %collective-permute-start.10 = (bf16[8,16,128]{2,1,0:T(8,128)(2,1)S(1)}, bf16[8,16,128]{2,1,0:T(8,128)(2,1)S(1)}, u32[]{:S(2)}, u32[]{:S(2)}) collective-permute-start(bf16[8,16,128]{2,1,0:T(8,128)(2,1)S(1)} %get-tuple-element.30), channel_id=1, source_target_pairs={{0,32},{32,0},{1,33},{33,1},{2,34},{34,2},{3,35},{35,3},{4,36},{36... | collective-permute-start | bytes 98312 | tf_op jit(solution)/shard_map/ppermute | solution.py:40
  133.1 6.3 %all-to-all-done.5 = bf16[8,16,8,128]{3,2,1,0:T(8,128)(2,1)S(1)} async-done(((bf16[8,16,8,128]{3,2,1,0:T(8,128)(2,1)}), bf16[8,16,8,128]{3,2,1,0:T(8,128)(2,1)S(1)}, u32[]{:S(2)}, u32[]{:S(2)}) %all-to-all-start.5) | async-done | bytes 262176 | tf_op jit(solution)/shard_map/all_to_all | solution.py:36
  139.4 5.2 %collective-permute-start.9 = (bf16[8,16,8,128]{3,2,1,0:T(8,128)(2,1)S(1)}, bf16[8,16,8,128]{3,2,1,0:T(8,128)(2,1)S(1)}, u32[]{:S(2)}, u32[]{:S(2)}) collective-permute-start(bf16[8,16,8,128]{3,2,1,0:T(8,128)(2,1)S(1)} %all-to-all-done.5), channel_id=1, source_target_pairs={{0,1},{1,0},{2,3},{3,2},{4,5},{5,4},{6,7},{7,6},{8,9},{9,8},{10,11... | collective-permute-start | bytes 786440 | tf_op jit(solution)/shard_map/ppermute | solution.py:40
  145.8 1.4 shard_map.185
  147.3 6.4 %all-to-all-start.6 = ((bf16[16,2,8,8,128]{4,3,2,1,0:T(8,128)(2,1)}), bf16[16,2,8,8,128]{4,3,2,1,0:T(8,128)(2,1)S(1)}, u32[]{:S(2)}, u32[]{:S(2)}) async-start(bf16[16,2,8,8,128]{4,3,2,1,0:T(8,128)(2,1)} %bitcast.11), calls=%async_computation.6 | async-start | bytes 1048576 | tf_op jit(solution)/shard_map/all_to_all | solution.py:36
  154.3 12.9 %all-to-all-done.6.partial_ref = bf16[16,2,8,8,128]{4,3,2,1,0:T(8,128)(2,1)S(1)} async-done(((bf16[16,2,8,8,128]{4,3,2,1,0:T(8,128)(2,1)}), bf16[16,2,8,8,128]{4,3,2,1,0:T(8,128)(2,1)S(1)}, u32[]{:S(2)}, u32[]{:S(2)}) %all-to-all-start.6) | async-done | bytes 524320 | tf_op jit(solution)/shard_map/all_to_all | solution.py:36
  167.2 1.0 shard_map.186
  (75 shorter events, 4.2 us)
Async XLA Ops:
  3.1 16.2 %collective-permute-start = (bf16[1,1,1,8,128]{4,3,2,1,0:T(8,128)(2,1)S(1)}, bf16[1,1,1,8,128]{4,3,2,1,0:T(8,128)(2,1)S(1)}, u32[]{:S(2)}, u32[]{:S(2)}) collective-permute-start(bf16[1,1,1,8,128]{4,3,2,1,0:T(8,128)(2,1)S(1)} %bitcast.21), channel_id=1, source_target_pairs={{0,1},{1,0},{2,3},{3,2},{4,5},{5,4},{6,7},{7,6},{8,9},{9,8},{10,11... | collective-permute-start | bytes 6152 | tf_op jit(solution)/shard_map/ppermute | solution.py:40
  11.8 27.9 %copy-start.9 = (bf16[256,256]{1,0:T(8,128)(2,1)S(1)}, bf16[256,256]{1,0:T(8,128)(2,1)}, u32[]{:S(2)}) copy-start(bf16[256,256]{1,0:T(8,128)(2,1)} %gate_w_ref.3) | copy-start | bytes 393220
  11.9 34.0 %all-to-all-start = ((bf16[16,8,16,256]{3,2,1,0:T(8,128)(2,1)}), bf16[16,8,16,256]{3,2,1,0:T(8,128)(2,1)S(1)}, u32[]{:S(2)}, u32[]{:S(2)}) async-start(bf16[16,8,16,256]{3,2,1,0:T(8,128)(2,1)} %shard_map.176), calls=%async_computation | async-start | bytes 2097152 | tf_op jit(solution)/shard_map/all_to_all | solution.py:36
  19.3 7.2 %collective-permute-start.1 = (bf16[1,1,2,8,128]{4,3,2,1,0:T(8,128)(2,1)S(1)}, bf16[1,1,2,8,128]{4,3,2,1,0:T(8,128)(2,1)S(1)}, u32[]{:S(2)}, u32[]{:S(2)}) collective-permute-start(bf16[1,1,2,8,128]{4,3,2,1,0:T(8,128)(2,1)S(1)} %pad_maximum_fusion.6), channel_id=1, source_target_pairs={{0,28},{4,0},{8,4},{12,8},{16,12},{20,16},{24,20},{28,24},{1,29},{... | collective-permute-start | bytes 12296 | tf_op jit(solution)/shard_map/ppermute | solution.py:71
  24.4 15.4 %copy-start.8 = (bf16[256,256]{1,0:T(8,128)(2,1)S(1)}, bf16[256,256]{1,0:T(8,128)(2,1)}, u32[]{:S(2)}) copy-start(bf16[256,256]{1,0:T(8,128)(2,1)} %query_w_ref) | copy-start | bytes 393220
  24.4 6.8 %collective-permute-start.3 = (bf16[1,1,2,8,128]{4,3,2,1,0:T(8,128)(2,1)S(1)}, bf16[1,1,2,8,128]{4,3,2,1,0:T(8,128)(2,1)S(1)}, u32[]{:S(2)}, u32[]{:S(2)}) collective-permute-start(bf16[1,1,2,8,128]{4,3,2,1,0:T(8,128)(2,1)S(1)} %pad_maximum_fusion.6), channel_id=1, source_target_pairs={{0,4},{4,8},{8,12},{12,16},{16,20},{20,24},{24,28},{28,0},{1,5},{5... | collective-permute-start | bytes 12296 | tf_op jit(solution)/shard_map/ppermute | solution.py:71
  26.5 8.3 %collective-permute-start.2 = (bf16[1,2,2,8,128]{4,3,2,1,0:T(8,128)(2,1)S(1)}, bf16[1,2,2,8,128]{4,3,2,1,0:T(8,128)(2,1)S(1)}, u32[]{:S(2)}, u32[]{:S(2)}) collective-permute-start(bf16[1,2,2,8,128]{4,3,2,1,0:T(8,128)(2,1)S(1)} %pad_maximum_fusion.5), channel_id=1, source_target_pairs={{0,12},{4,16},{8,20},{12,24},{16,28},{20,0},{24,4},{28,8},{1,13},{... | collective-permute-start | bytes 24584 | tf_op jit(solution)/shard_map/ppermute | solution.py:71
  31.2 6.2 %collective-permute-start.4 = (bf16[1,3,2,8,128]{4,3,2,1,0:T(8,128)(2,1)S(1)}, bf16[1,3,2,8,128]{4,3,2,1,0:T(8,128)(2,1)S(1)}, u32[]{:S(2)}, u32[]{:S(2)}) collective-permute-start(bf16[1,3,2,8,128]{4,3,2,1,0:T(8,128)(2,1)S(1)} %pad_maximum_fusion.4), channel_id=1, source_target_pairs={{0,20},{4,24},{8,28},{12,0},{16,4},{20,8},{24,12},{28,16},{1,21},{... | collective-permute-start | bytes 36872 | tf_op jit(solution)/shard_map/ppermute | solution.py:71
  37.5 2.3 %copy-start.1 = (bf16[8,16,256]{2,1,0:T(8,128)(2,1)S(1)}, bf16[8,16,256]{2,1,0:T(8,128)(2,1)}, u32[]{:S(2)}) copy-start(bf16[8,16,256]{2,1,0:T(8,128)(2,1)} %x_ref.5) | copy-start | bytes 196612
  37.6 5.2 %collective-permute-start.5 = (bf16[1,8,2,8,128]{4,3,2,1,0:T(8,128)(2,1)S(1)}, bf16[1,8,2,8,128]{4,3,2,1,0:T(8,128)(2,1)S(1)}, u32[]{:S(2)}, u32[]{:S(2)}) collective-permute-start(bf16[1,8,2,8,128]{4,3,2,1,0:T(8,128)(2,1)S(1)} %constant_dynamic-slice_fusion), channel_id=1, source_target_pairs={{0,2},{2,0},{1,3},{3,1},{4,6},{6,4},{5,7},{7,5},{8,10},{10,8},{9,1... | collective-permute-start | bytes 98312 | tf_op jit(solution)/shard_map/ppermute | solution.py:40
  39.8 6.1 %copy-start.5 = (bf16[256,256]{1,0:T(8,128)(2,1)S(1)}, bf16[256,256]{1,0:T(8,128)(2,1)}, u32[]{:S(2)}) copy-start(bf16[256,256]{1,0:T(8,128)(2,1)} %out_w_ref.3) | copy-start | bytes 393220
  39.8 6.1 %copy-start.15 = (bf16[256,32]{0,1:T(8,128)(2,1)S(1)}, bf16[256,32]{0,1:T(8,128)(2,1)}, u32[]{:S(2)}) copy-start(bf16[256,32]{0,1:T(8,128)(2,1)} %param.25) | copy-start | bytes 49156
  39.8 6.1 %copy-start.16 = (bf16[256,32]{0,1:T(8,128)(2,1)S(1)}, bf16[256,32]{0,1:T(8,128)(2,1)}, u32[]{:S(2)}) copy-start(bf16[256,32]{0,1:T(8,128)(2,1)} %param.26) | copy-start | bytes 49156
  40.2 5.7 %copy-start.3 = (bf16[256,256]{1,0:T(8,128)(2,1)S(1)}, bf16[256,256]{1,0:T(8,128)(2,1)}, u32[]{:S(2)}) copy-start(bf16[256,256]{1,0:T(8,128)(2,1)} %key_w_ref.1) | copy-start | bytes 393220
  40.2 5.7 %copy-start.4 = (bf16[256,256]{1,0:T(8,128)(2,1)S(1)}, bf16[256,256]{1,0:T(8,128)(2,1)}, u32[]{:S(2)}) copy-start(bf16[256,256]{1,0:T(8,128)(2,1)} %value_w_ref.1) | copy-start | bytes 393220
  64.2 22.7 %copy-start.2 = (bf16[1024,128]{1,0:T(8,128)(2,1)S(1)}, bf16[1024,128]{1,0:T(8,128)(2,1)}, u32[]{:S(2)}) copy-start(bf16[1024,128]{1,0:T(8,128)(2,1)} %outer_w_ref.1) | copy-start | bytes 786436
  64.2 22.7 %copy-start.6 = (bf16[128,512]{1,0:T(8,128)(2,1)S(1)}, bf16[128,512]{1,0:T(8,128)(2,1)}, u32[]{:S(2)}) copy-start(bf16[128,512]{1,0:T(8,128)(2,1)} %in_w_ref.2) | copy-start | bytes 393220
  88.8 6.0 %collective-permute-start.6 = (bf16[16,8,128]{2,1,0:T(8,128)(2,1)S(1)}, bf16[16,8,128]{2,1,0:T(8,128)(2,1)S(1)}, u32[]{:S(2)}, u32[]{:S(2)}) collective-permute-start(bf16[16,8,128]{2,1,0:T(8,128)(2,1)S(1)} %get-tuple-element.27), channel_id=1, source_target_pairs={{0,1},{1,0},{2,3},{3,2},{4,5},{5,4},{6,7},{7,6},{8,9},{9,8},{10,11... | collective-permute-start | bytes 98312 | tf_op jit(solution)/shard_map/ppermute | solution.py:40
  91.3 12.8 %all-to-all-start.3 = ((bf16[16,8,8,128]{3,2,1,0:T(8,128)(2,1)}), bf16[16,8,8,128]{3,2,1,0:T(8,128)(2,1)S(1)}, u32[]{:S(2)}, u32[]{:S(2)}) async-start(bf16[16,8,8,128]{3,2,1,0:T(8,128)(2,1)} %bitcast.6), calls=%async_computation.3 | async-start | bytes 524288 | tf_op jit(solution)/shard_map/all_to_all | solution.py:36
  94.8 7.1 %collective-permute-start.7 = (bf16[16,16,128]{2,1,0:T(8,128)(2,1)S(1)}, bf16[16,16,128]{2,1,0:T(8,128)(2,1)S(1)}, u32[]{:S(2)}, u32[]{:S(2)}) collective-permute-start(bf16[16,16,128]{2,1,0:T(8,128)(2,1)S(1)} %pad_maximum_fusion.2), channel_id=1, source_target_pairs={{0,32},{32,0},{1,33},{33,1},{2,34},{34,2},{3,35},{35,3},{4,36},{36... | collective-permute-start | bytes 196616 | tf_op jit(solution)/shard_map/ppermute | solution.py:40
  106.1 17.2 %copy-start.10 = (bf16[128,512]{1,0:T(8,128)(2,1)S(1)}, bf16[128,512]{1,0:T(8,128)(2,1)}, u32[]{:S(2)}) copy-start(bf16[128,512]{1,0:T(8,128)(2,1)} %in_w_ref.3) | copy-start | bytes 393220
  106.1 17.2 %copy-start.11 = (bf16[128,128]{1,0:T(8,128)(2,1)S(1)}, bf16[128,128]{1,0:T(8,128)(2,1)}, u32[]{:S(2)}) copy-start(bf16[128,128]{1,0:T(8,128)(2,1)} %gate_w_ref.4) | copy-start | bytes 98308
  106.1 17.2 %copy-start.12 = (bf16[128,128]{1,0:T(8,128)(2,1)S(1)}, bf16[128,128]{1,0:T(8,128)(2,1)}, u32[]{:S(2)}) copy-start(bf16[128,128]{1,0:T(8,128)(2,1)} %out_w_ref.4) | copy-start | bytes 98308
  106.1 17.2 %all-to-all-start.4 = ((bf16[16,16,8,128]{3,2,1,0:T(8,128)(2,1)}), bf16[16,16,8,128]{3,2,1,0:T(8,128)(2,1)S(1)}, u32[]{:S(2)}, u32[]{:S(2)}) async-start(bf16[16,16,8,128]{3,2,1,0:T(8,128)(2,1)} %bitcast.8), calls=%async_computation.4 | async-start | bytes 1048576 | tf_op jit(solution)/shard_map/all_to_all | solution.py:36
  110.3 0.7 collective-permute-start.8
  124.7 14.8 %all-to-all-start.5 = ((bf16[8,16,8,128]{3,2,1,0:T(8,128)(2,1)}), bf16[8,16,8,128]{3,2,1,0:T(8,128)(2,1)S(1)}, u32[]{:S(2)}, u32[]{:S(2)}) async-start(bf16[8,16,8,128]{3,2,1,0:T(8,128)(2,1)} %get-tuple-element.29), calls=%async_computation.5 | async-start | bytes 524288 | tf_op jit(solution)/shard_map/all_to_all | solution.py:36
  130.0 14.7 %collective-permute-start.10 = (bf16[8,16,128]{2,1,0:T(8,128)(2,1)S(1)}, bf16[8,16,128]{2,1,0:T(8,128)(2,1)S(1)}, u32[]{:S(2)}, u32[]{:S(2)}) collective-permute-start(bf16[8,16,128]{2,1,0:T(8,128)(2,1)S(1)} %get-tuple-element.30), channel_id=1, source_target_pairs={{0,32},{32,0},{1,33},{33,1},{2,34},{34,2},{3,35},{35,3},{4,36},{36... | collective-permute-start | bytes 98312 | tf_op jit(solution)/shard_map/ppermute | solution.py:40
  139.4 6.4 %collective-permute-start.9 = (bf16[8,16,8,128]{3,2,1,0:T(8,128)(2,1)S(1)}, bf16[8,16,8,128]{3,2,1,0:T(8,128)(2,1)S(1)}, u32[]{:S(2)}, u32[]{:S(2)}) collective-permute-start(bf16[8,16,8,128]{3,2,1,0:T(8,128)(2,1)S(1)} %all-to-all-done.5), channel_id=1, source_target_pairs={{0,1},{1,0},{2,3},{3,2},{4,5},{5,4},{6,7},{7,6},{8,9},{9,8},{10,11... | collective-permute-start | bytes 786440 | tf_op jit(solution)/shard_map/ppermute | solution.py:40
  147.3 20.0 %copy-start.13 = (bf16[128,128]{1,0:T(8,128)(2,1)S(1)}, bf16[128,128]{1,0:T(8,128)(2,1)}, u32[]{:S(2)}) copy-start(bf16[128,128]{1,0:T(8,128)(2,1)} %gate_w_ref.5) | copy-start | bytes 98308
  147.3 20.0 %copy-start.14 = (bf16[128,128]{1,0:T(8,128)(2,1)S(1)}, bf16[128,128]{1,0:T(8,128)(2,1)}, u32[]{:S(2)}) copy-start(bf16[128,128]{1,0:T(8,128)(2,1)} %out_w_ref.5) | copy-start | bytes 98308
  147.3 20.0 %all-to-all-start.6 = ((bf16[16,2,8,8,128]{4,3,2,1,0:T(8,128)(2,1)}), bf16[16,2,8,8,128]{4,3,2,1,0:T(8,128)(2,1)S(1)}, u32[]{:S(2)}, u32[]{:S(2)}) async-start(bf16[16,2,8,8,128]{4,3,2,1,0:T(8,128)(2,1)} %bitcast.11), calls=%async_computation.6 | async-start | bytes 1048576 | tf_op jit(solution)/shard_map/all_to_all | solution.py:36
  153.6 0.7 collective-permute-start.11
  (3 other events, 3.4 us)

commit v6 on v5

--- a/solution.py
+++ b/solution.py
@@ -12,7 +12,7 @@
 ROWS, COLS = 16, 32
 SIZES = {"z": 8, "xh": 2, "y": 8, "xl": 2, "core": 2}
 ROW, COL = ("z", "xh"), ("y", "xl", "core")
-ROW_X_FIRST, COL_X_FIRST = ("xh", "z"), ("core", "xl", "y")
+ROW_X_FIRST, COL_X_FIRST = ("xh", "z"), ("xl", "core", "y")
 FLIP = [(0, 1), (1, 0)]
 CROSS = [(0, 0), (1, 2), (2, 1), (3, 3)]
 
@@ -92,10 +92,11 @@
 def bias_kernel(rows, pair_ref, bias_w_ref, bias_ref):
     height, width, depth = pair_ref.shape
     heads = bias_w_ref.shape[0]
-    pair_normed = layer_norm(pair_ref[...].reshape(height * width, depth)).astype(BF16)
+    weight = bias_w_ref[...].astype(F32)
+    pair_normed = layer_norm(pair_ref[...].astype(F32).reshape(height * width, depth)).astype(BF16)
     wide = jnp.concatenate(
-        [jnp.broadcast_to(bias_w_ref[h : h + 1, :], (rows, depth)) for h in range(heads)], axis=0
-    )
+        [jnp.broadcast_to(weight[h : h + 1, :], (rows, depth)) for h in range(heads)], axis=0
+    ).astype(BF16)
     every = lax.dot_general(
         pair_normed, wide, (((1,), (1,)), ((), ())), preferred_element_type=F32
     ).reshape(height, width, heads * rows)
@@ -163,14 +164,13 @@
 
 def factor_kernel(left_ref, right_ref, chunks_ref):
     members, _, size = right_ref.shape
-    pieces = chunks_ref.shape[0] // members
-    split = size // pieces
+    split = size // 2
     left = left_ref[...]
     for place in range(chunks_ref.shape[0]):
-        part = place // members
+        x_lo, part, y = place // members, place // SIZES["y"] % 2, place % SIZES["y"]
         chunks_ref[place, :, : left.shape[1]] = left
         chunks_ref[place, :, left.shape[1] :] = right_ref[
-            place % members, :, part * split : (part + 1) * split
+            x_lo * SIZES["y"] + y, :, part * split : (part + 1) * split
         ]
 
 
@@ -215,16 +215,17 @@
     update = jnp.concatenate(
         [update_ref[pl.ds(i, cols, stride=rows), :] for i in range(rows)], axis=0
     )
-    pair = (pair_ref[...].reshape(rows * cols, depth).astype(F32) + update).astype(BF16)
+    pair = (pair_ref[...].astype(F32).reshape(rows * cols, depth) + update).astype(BF16)
     pair_out[...] = pair
     left, right = edge_parts(pair, in_w_ref)
-    left_out[...] = left.astype(BF16).reshape(rows, cols, depth)
+    left_out[...] = left.reshape(rows, cols, depth).astype(BF16)
     right_scr[...] = right
     for k in range(cols):
-        line = right_scr[pl.ds(k, rows, stride=cols), :].astype(BF16)
+        line = right_scr[pl.ds(k, rows, stride=cols), :]
         for half in range(right_out.shape[0]):
+            part = line[half * cols : (half + 1) * cols].astype(BF16)
             for member in range(right_out.shape[1]):
-                right_out[half, member, k] = line[half * cols : (half + 1) * cols]
+                right_out[half, member, k] = part
 
 
 def partial_kernel(tile_ref, line_ref, *refs):
@@ -286,7 +287,7 @@
     pair = updated(combined, pair_ref[...], gate_w_ref, out_w_ref)
     pair_out[...] = pair
     left, right = edge_parts(pair, in_w_ref)
-    left = left.astype(BF16).reshape(rows, cols, depth)
+    left = left.reshape(rows, cols, depth).astype(BF16)
     for member in range(chunks_out.shape[0]):
         chunks_out[member] = left
     right_scr[...] = right
@@ -307,7 +308,8 @@
     combined = jnp.concatenate(
         [jnp.where(first, own, other), jnp.where(first, other, own)], axis=0
     )
-    new_ref[...] = updated(combined, pair_ref[...], gate_w_ref, out_w_ref).reshape(new_ref.shape)
+    new = updated(combined, pair_ref[...], gate_w_ref, out_w_ref)
+    new_ref[...] = new.astype(F32).reshape(new_ref.shape).astype(BF16)
 
 
 def on_device(

time: 170 us -> 170 us (level)
  no operation moved by 1% of the time
where the time goes in v6:
time: 170 us; the launch traced here: 168 us
  starting transfers between devices  68.6 us (40%)
  waiting for transfers between devices  46.3 us (27%)
  blocking collectives  38 us (22%)
  Pallas kernels  13.1 us (8%)
    all_to_all x2, blocking collectives, exchange(): return lax.all_to_all(chunks, axes, 0, 0)  38 us
    all_to_all x5, waiting for transfers between devices, exchange(): return lax.all_to_all(chunks, axes, 0, 0)  37 us
    all_to_all x5, starting transfers between devices, exchange(): return lax.all_to_all(chunks, axes, 0, 0)  26.9 us
    ppermute x6, starting transfers between devices, flip(): return lax.ppermute(block, axis, FLIP)  24.9 us
    ppermute x4, starting transfers between devices, shifted(): lax.ppermute(block, 'y', [(y, (y - step) % size) for y in range(size)])  15.4 us
    pallas_call x11, Pallas kernels, kernel_call(): pl.pallas_call(body, out_shape=shapes, in_specs=[pl.BlockSpec() if fetche...  13.1 us
    ppermute x6, waiting for transfers between devices, flip(): return lax.ppermute(block, axis, FLIP)  6.7 us
  transfers between devices with their start and end apart: 17, of which 9 were waited for; matrix products, arithmetic and copies ran while one was open for 0% of the time, Pallas kernels for 1%

profile of v6, /device:TPU:1, one launch (start us, length us, event | category | flops | bytes accessed | tf_op | source)
XLA Modules:
  0.0 168.2 jit_solution(10180577768431555620)
XLA Ops:
  1.5 1.3 shard_map.176
  3.1 8.8 %collective-permute-start = (bf16[1,1,1,8,128]{4,3,2,1,0:T(8,128)(2,1)S(1)}, bf16[1,1,1,8,128]{4,3,2,1,0:T(8,128)(2,1)S(1)}, u32[]{:S(2)}, u32[]{:S(2)}) collective-permute-start(bf16[1,1,1,8,128]{4,3,2,1,0:T(8,128)(2,1)S(1)} %bitcast.21), channel_id=1, source_target_pairs={{0,1},{1,0},{2,3},{3,2},{4,5},{5,4},{6,7},{7,6},{8,9},{9,8},{10,11... | collective-permute-start | bytes 6152 | tf_op jit(solution)/shard_map/ppermute | solution.py:40
  11.9 7.4 %all-to-all-start = ((bf16[16,8,16,256]{3,2,1,0:T(8,128)(2,1)}), bf16[16,8,16,256]{3,2,1,0:T(8,128)(2,1)S(1)}, u32[]{:S(2)}, u32[]{:S(2)}) async-start(bf16[16,8,16,256]{3,2,1,0:T(8,128)(2,1)} %shard_map.176), calls=%async_computation | async-start | bytes 2097152 | tf_op jit(solution)/shard_map/all_to_all | solution.py:36
  19.3 5.1 %collective-permute-start.1 = (bf16[1,1,2,8,128]{4,3,2,1,0:T(8,128)(2,1)S(1)}, bf16[1,1,2,8,128]{4,3,2,1,0:T(8,128)(2,1)S(1)}, u32[]{:S(2)}, u32[]{:S(2)}) collective-permute-start(bf16[1,1,2,8,128]{4,3,2,1,0:T(8,128)(2,1)S(1)} %pad_maximum_fusion.6), channel_id=1, source_target_pairs={{0,28},{4,0},{8,4},{12,8},{16,12},{20,16},{24,20},{28,24},{1,29},{... | collective-permute-start | bytes 12296 | tf_op jit(solution)/shard_map/ppermute | solution.py:71
  24.4 2.1 %collective-permute-start.3 = (bf16[1,1,2,8,128]{4,3,2,1,0:T(8,128)(2,1)S(1)}, bf16[1,1,2,8,128]{4,3,2,1,0:T(8,128)(2,1)S(1)}, u32[]{:S(2)}, u32[]{:S(2)}) collective-permute-start(bf16[1,1,2,8,128]{4,3,2,1,0:T(8,128)(2,1)S(1)} %pad_maximum_fusion.6), channel_id=1, source_target_pairs={{0,4},{4,8},{8,12},{12,16},{16,20},{20,24},{24,28},{28,0},{1,5},{5... | collective-permute-start | bytes 12296 | tf_op jit(solution)/shard_map/ppermute | solution.py:71
  26.5 4.7 %collective-permute-start.2 = (bf16[1,2,2,8,128]{4,3,2,1,0:T(8,128)(2,1)S(1)}, bf16[1,2,2,8,128]{4,3,2,1,0:T(8,128)(2,1)S(1)}, u32[]{:S(2)}, u32[]{:S(2)}) collective-permute-start(bf16[1,2,2,8,128]{4,3,2,1,0:T(8,128)(2,1)S(1)} %pad_maximum_fusion.5), channel_id=1, source_target_pairs={{0,12},{4,16},{8,20},{12,24},{16,28},{20,0},{24,4},{28,8},{1,13},{... | collective-permute-start | bytes 24584 | tf_op jit(solution)/shard_map/ppermute | solution.py:71
  31.2 3.6 %collective-permute-start.4 = (bf16[1,3,2,8,128]{4,3,2,1,0:T(8,128)(2,1)S(1)}, bf16[1,3,2,8,128]{4,3,2,1,0:T(8,128)(2,1)S(1)}, u32[]{:S(2)}, u32[]{:S(2)}) collective-permute-start(bf16[1,3,2,8,128]{4,3,2,1,0:T(8,128)(2,1)S(1)} %pad_maximum_fusion.4), channel_id=1, source_target_pairs={{0,20},{4,24},{8,28},{12,0},{16,4},{20,8},{24,12},{28,16},{1,21},{... | collective-permute-start | bytes 36872 | tf_op jit(solution)/shard_map/ppermute | solution.py:71
  34.9 2.6 %collective-permute-done.4 = bf16[1,3,2,8,128]{4,3,2,1,0:T(8,128)(2,1)S(1)} collective-permute-done((bf16[1,3,2,8,128]{4,3,2,1,0:T(8,128)(2,1)S(1)}, bf16[1,3,2,8,128]{4,3,2,1,0:T(8,128)(2,1)S(1)}, u32[]{:S(2)}, u32[]{:S(2)}) %collective-permute-start.4) | collective-permute-done | bytes 12320 | tf_op jit(solution)/shard_map/ppermute | solution.py:71
  37.6 2.2 %collective-permute-start.5 = (bf16[1,8,2,8,128]{4,3,2,1,0:T(8,128)(2,1)S(1)}, bf16[1,8,2,8,128]{4,3,2,1,0:T(8,128)(2,1)S(1)}, u32[]{:S(2)}, u32[]{:S(2)}) collective-permute-start(bf16[1,8,2,8,128]{4,3,2,1,0:T(8,128)(2,1)S(1)} %constant_dynamic-slice_fusion), channel_id=1, source_target_pairs={{0,2},{2,0},{1,3},{3,1},{4,6},{6,4},{5,7},{7,5},{8,10},{10,8},{9,1... | collective-permute-start | bytes 98312 | tf_op jit(solution)/shard_map/ppermute | solution.py:40
  40.2 2.5 %collective-permute-done.5 = bf16[1,8,2,8,128]{4,3,2,1,0:T(8,128)(2,1)S(1)} collective-permute-done((bf16[1,8,2,8,128]{4,3,2,1,0:T(8,128)(2,1)S(1)}, bf16[1,8,2,8,128]{4,3,2,1,0:T(8,128)(2,1)S(1)}, u32[]{:S(2)}, u32[]{:S(2)}) %collective-permute-start.5) | collective-permute-done | bytes 32800 | tf_op jit(solution)/shard_map/ppermute | solution.py:40
  42.7 3.1 %all-to-all-done.every_ref = bf16[16,8,16,256]{3,2,1,0:T(8,128)(2,1)S(1)} async-done(((bf16[16,8,16,256]{3,2,1,0:T(8,128)(2,1)}), bf16[16,8,16,256]{3,2,1,0:T(8,128)(2,1)S(1)}, u32[]{:S(2)}, u32[]{:S(2)}) %all-to-all-start) | async-done | bytes 1048608 | tf_op jit(solution)/shard_map/all_to_all | solution.py:36
  45.9 3.0 %shard_map.179 = (bf16[8,16,256]{2,1,0:T(8,128)(2,1)}, bf16[8,512]{1,0:T(8,128)(2,1)S(1)}, bf16[16,8,512]{2,1,0:T(8,128)(2,1)S(1)}) custom-call(bf16[16,8,16,256]{3,2,1,0:T(8,128)(2,1)S(1)} %all-to-all-done.every_ref, bf16[256,128]{1,0:T(8,128)(2,1)S(1)} %bitcast.17, bf16[8,16,256]{2,1,0:T(8,128)(2,1)S(1)} %get-tuple-element.21.query_ref, ...), custom_call_target="tpu_custom_call" | custom-call | bytes 2007040 | tf_op jit(solution)/shard_map/pallas_call | solution.py:58
  48.9 15.2 %all_to_all.35.right_ref = bf16[16,8,512]{2,1,0:T(8,128)(2,1)S(1)} all-to-all(bf16[16,8,512]{2,1,0:T(8,128)(2,1)S(1)} %get-tuple-element.25), channel_id=1, replica_groups=mesh['z'=8,'xh'=2,'y'=8,'xl'=2,'core'=2] {'xh','z'}, dimensions={0} | all-to-all | bytes 262144 | tf_op jit(solution)/shard_map/all_to_all | solution.py:36
  64.2 22.7 %all_to_all.36 = bf16[32,8,768]{2,1,0:T(8,128)(2,1)S(1)} all-to-all(bf16[32,8,768]{2,1,0:T(8,128)(2,1)S(1)} %shard_map.180), channel_id=1, replica_groups=mesh['z'=8,'xh'=2,'y'=8,'xl'=2,'core'=2] {'xl','core','y'}, dimensions={0} | all-to-all | bytes 786432 | tf_op jit(solution)/shard_map/all_to_all | solution.py:36
  86.9 1.9 %shard_map.181 = (bf16[128,128]{1,0:T(8,128)(2,1)S(1)}, bf16[16,8,128]{2,1,0:T(8,128)(2,1)S(1)}, bf16[2,8,8,8,128]{4,3,2,1,0:T(8,128)(2,1)}) custom-call(bf16[256,768]{1,0:T(8,128)(2,1)S(1)} %bitcast.14, bf16[16,8,128]{2,1,0:T(8,128)(2,1)S(1)} %copy-done.7, bf16[1024,128]{1,0:T(8,128)(2,1)S(1)} %copy-done.2, bf16[128,512]{1,0:T(8,128)(2,1)S(1)} %copy-done.6), custom_call_target="tpu_custom_call" | custom-call | bytes 1146880 | tf_op jit(solution)/shard_map/pallas_call | solution.py:58
  88.8 2.3 %collective-permute-start.6 = (bf16[16,8,128]{2,1,0:T(8,128)(2,1)S(1)}, bf16[16,8,128]{2,1,0:T(8,128)(2,1)S(1)}, u32[]{:S(2)}, u32[]{:S(2)}) collective-permute-start(bf16[16,8,128]{2,1,0:T(8,128)(2,1)S(1)} %get-tuple-element.27), channel_id=1, source_target_pairs={{0,1},{1,0},{2,3},{3,2},{4,5},{5,4},{6,7},{7,6},{8,9},{9,8},{10,11... | collective-permute-start | bytes 98312 | tf_op jit(solution)/shard_map/ppermute | solution.py:40
  91.1 3.5 %all-to-all-start.3 = ((bf16[16,8,8,128]{3,2,1,0:T(8,128)(2,1)}), bf16[16,8,8,128]{3,2,1,0:T(8,128)(2,1)S(1)}, u32[]{:S(2)}, u32[]{:S(2)}) async-start(bf16[16,8,8,128]{3,2,1,0:T(8,128)(2,1)} %bitcast.6), calls=%async_computation.3 | async-start | bytes 524288 | tf_op jit(solution)/shard_map/all_to_all | solution.py:36
  94.6 3.2 %collective-permute-start.7 = (bf16[16,16,128]{2,1,0:T(8,128)(2,1)S(1)}, bf16[16,16,128]{2,1,0:T(8,128)(2,1)S(1)}, u32[]{:S(2)}, u32[]{:S(2)}) collective-permute-start(bf16[16,16,128]{2,1,0:T(8,128)(2,1)S(1)} %pad_maximum_fusion.2), channel_id=1, source_target_pairs={{0,32},{32,0},{1,33},{33,1},{2,34},{34,2},{3,35},{35,3},{4,36},{36... | collective-permute-start | bytes 196616 | tf_op jit(solution)/shard_map/ppermute | solution.py:40
  97.8 3.7 %collective-permute-done.7 = bf16[16,16,128]{2,1,0:T(8,128)(2,1)S(1)} collective-permute-done((bf16[16,16,128]{2,1,0:T(8,128)(2,1)S(1)}, bf16[16,16,128]{2,1,0:T(8,128)(2,1)S(1)}, u32[]{:S(2)}, u32[]{:S(2)}) %collective-permute-start.7) | collective-permute-done | bytes 65568 | tf_op jit(solution)/shard_map/ppermute | solution.py:40
  101.6 2.4 %all-to-all-done.3 = bf16[16,8,8,128]{3,2,1,0:T(8,128)(2,1)S(1)} async-done(((bf16[16,8,8,128]{3,2,1,0:T(8,128)(2,1)}), bf16[16,8,8,128]{3,2,1,0:T(8,128)(2,1)S(1)}, u32[]{:S(2)}, u32[]{:S(2)}) %all-to-all-start.3) | async-done | bytes 262176 | tf_op jit(solution)/shard_map/all_to_all | solution.py:36
  104.0 2.0 %shard_map.182 = bf16[2,8,16,8,128]{4,3,2,1,0:T(8,128)(2,1)} custom-call(bf16[2,8,8,8,128]{4,3,2,1,0:T(8,128)(2,1)S(1)} %bitcast.15, bf16[32,16,128]{2,1,0:T(8,128)(2,1)S(1)} %pad_maximum_fusion.line_ref), custom_call_target="tpu_custom_call" | custom-call | flops 8388608 | bytes 917504 | tf_op jit(solution)/shard_map/pallas_call | solution.py:58
  105.9 4.3 %all-to-all-start.4 = ((bf16[16,16,8,128]{3,2,1,0:T(8,128)(2,1)}), bf16[16,16,8,128]{3,2,1,0:T(8,128)(2,1)S(1)}, u32[]{:S(2)}, u32[]{:S(2)}) async-start(bf16[16,16,8,128]{3,2,1,0:T(8,128)(2,1)} %bitcast.8), calls=%async_computation.4 | async-start | bytes 1048576 | tf_op jit(solution)/shard_map/all_to_all | solution.py:36
  111.0 12.3 %all-to-all-done.4.partial_ref = bf16[16,16,8,128]{3,2,1,0:T(8,128)(2,1)S(1)} async-done(((bf16[16,16,8,128]{3,2,1,0:T(8,128)(2,1)}), bf16[16,16,8,128]{3,2,1,0:T(8,128)(2,1)S(1)}, u32[]{:S(2)}, u32[]{:S(2)}) %all-to-all-start.4) | async-done | bytes 524320 | tf_op jit(solution)/shard_map/all_to_all | solution.py:36
  123.3 1.4 shard_map.183
  124.6 5.3 %all-to-all-start.5 = ((bf16[8,16,8,128]{3,2,1,0:T(8,128)(2,1)}), bf16[8,16,8,128]{3,2,1,0:T(8,128)(2,1)S(1)}, u32[]{:S(2)}, u32[]{:S(2)}) async-start(bf16[8,16,8,128]{3,2,1,0:T(8,128)(2,1)} %get-tuple-element.29), calls=%async_computation.5 | async-start | bytes 524288 | tf_op jit(solution)/shard_map/all_to_all | solution.py:36
  129.9 3.2 %collective-permute-start.10 = (bf16[8,16,128]{2,1,0:T(8,128)(2,1)S(1)}, bf16[8,16,128]{2,1,0:T(8,128)(2,1)S(1)}, u32[]{:S(2)}, u32[]{:S(2)}) collective-permute-start(bf16[8,16,128]{2,1,0:T(8,128)(2,1)S(1)} %get-tuple-element.30), channel_id=1, source_target_pairs={{0,32},{32,0},{1,33},{33,1},{2,34},{34,2},{3,35},{35,3},{4,36},{36... | collective-permute-start | bytes 98312 | tf_op jit(solution)/shard_map/ppermute | solution.py:40
  133.1 6.3 %all-to-all-done.5 = bf16[8,16,8,128]{3,2,1,0:T(8,128)(2,1)S(1)} async-done(((bf16[8,16,8,128]{3,2,1,0:T(8,128)(2,1)}), bf16[8,16,8,128]{3,2,1,0:T(8,128)(2,1)S(1)}, u32[]{:S(2)}, u32[]{:S(2)}) %all-to-all-start.5) | async-done | bytes 262176 | tf_op jit(solution)/shard_map/all_to_all | solution.py:36
  139.4 5.2 %collective-permute-start.9 = (bf16[8,16,8,128]{3,2,1,0:T(8,128)(2,1)S(1)}, bf16[8,16,8,128]{3,2,1,0:T(8,128)(2,1)S(1)}, u32[]{:S(2)}, u32[]{:S(2)}) collective-permute-start(bf16[8,16,8,128]{3,2,1,0:T(8,128)(2,1)S(1)} %all-to-all-done.5), channel_id=1, source_target_pairs={{0,1},{1,0},{2,3},{3,2},{4,5},{5,4},{6,7},{7,6},{8,9},{9,8},{10,11... | collective-permute-start | bytes 786440 | tf_op jit(solution)/shard_map/ppermute | solution.py:40
  145.8 1.4 shard_map.185
  147.2 6.4 %all-to-all-start.6 = ((bf16[16,2,8,8,128]{4,3,2,1,0:T(8,128)(2,1)}), bf16[16,2,8,8,128]{4,3,2,1,0:T(8,128)(2,1)S(1)}, u32[]{:S(2)}, u32[]{:S(2)}) async-start(bf16[16,2,8,8,128]{4,3,2,1,0:T(8,128)(2,1)} %bitcast.11), calls=%async_computation.6 | async-start | bytes 1048576 | tf_op jit(solution)/shard_map/all_to_all | solution.py:36
  154.3 12.9 %all-to-all-done.6.partial_ref = bf16[16,2,8,8,128]{4,3,2,1,0:T(8,128)(2,1)S(1)} async-done(((bf16[16,2,8,8,128]{4,3,2,1,0:T(8,128)(2,1)}), bf16[16,2,8,8,128]{4,3,2,1,0:T(8,128)(2,1)S(1)}, u32[]{:S(2)}, u32[]{:S(2)}) %all-to-all-start.6) | async-done | bytes 524320 | tf_op jit(solution)/shard_map/all_to_all | solution.py:36
  167.2 1.0 shard_map.186
  (75 shorter events, 4.2 us)
Async XLA Ops:
  3.1 16.2 %collective-permute-start = (bf16[1,1,1,8,128]{4,3,2,1,0:T(8,128)(2,1)S(1)}, bf16[1,1,1,8,128]{4,3,2,1,0:T(8,128)(2,1)S(1)}, u32[]{:S(2)}, u32[]{:S(2)}) collective-permute-start(bf16[1,1,1,8,128]{4,3,2,1,0:T(8,128)(2,1)S(1)} %bitcast.21), channel_id=1, source_target_pairs={{0,1},{1,0},{2,3},{3,2},{4,5},{5,4},{6,7},{7,6},{8,9},{9,8},{10,11... | collective-permute-start | bytes 6152 | tf_op jit(solution)/shard_map/ppermute | solution.py:40
  11.8 27.9 %copy-start.9 = (bf16[256,256]{1,0:T(8,128)(2,1)S(1)}, bf16[256,256]{1,0:T(8,128)(2,1)}, u32[]{:S(2)}) copy-start(bf16[256,256]{1,0:T(8,128)(2,1)} %gate_w_ref.3) | copy-start | bytes 393220
  11.9 34.0 %all-to-all-start = ((bf16[16,8,16,256]{3,2,1,0:T(8,128)(2,1)}), bf16[16,8,16,256]{3,2,1,0:T(8,128)(2,1)S(1)}, u32[]{:S(2)}, u32[]{:S(2)}) async-start(bf16[16,8,16,256]{3,2,1,0:T(8,128)(2,1)} %shard_map.176), calls=%async_computation | async-start | bytes 2097152 | tf_op jit(solution)/shard_map/all_to_all | solution.py:36
  19.3 7.2 %collective-permute-start.1 = (bf16[1,1,2,8,128]{4,3,2,1,0:T(8,128)(2,1)S(1)}, bf16[1,1,2,8,128]{4,3,2,1,0:T(8,128)(2,1)S(1)}, u32[]{:S(2)}, u32[]{:S(2)}) collective-permute-start(bf16[1,1,2,8,128]{4,3,2,1,0:T(8,128)(2,1)S(1)} %pad_maximum_fusion.6), channel_id=1, source_target_pairs={{0,28},{4,0},{8,4},{12,8},{16,12},{20,16},{24,20},{28,24},{1,29},{... | collective-permute-start | bytes 12296 | tf_op jit(solution)/shard_map/ppermute | solution.py:71
  24.4 15.4 %copy-start.8 = (bf16[256,256]{1,0:T(8,128)(2,1)S(1)}, bf16[256,256]{1,0:T(8,128)(2,1)}, u32[]{:S(2)}) copy-start(bf16[256,256]{1,0:T(8,128)(2,1)} %query_w_ref) | copy-start | bytes 393220
  24.4 6.8 %collective-permute-start.3 = (bf16[1,1,2,8,128]{4,3,2,1,0:T(8,128)(2,1)S(1)}, bf16[1,1,2,8,128]{4,3,2,1,0:T(8,128)(2,1)S(1)}, u32[]{:S(2)}, u32[]{:S(2)}) collective-permute-start(bf16[1,1,2,8,128]{4,3,2,1,0:T(8,128)(2,1)S(1)} %pad_maximum_fusion.6), channel_id=1, source_target_pairs={{0,4},{4,8},{8,12},{12,16},{16,20},{20,24},{24,28},{28,0},{1,5},{5... | collective-permute-start | bytes 12296 | tf_op jit(solution)/shard_map/ppermute | solution.py:71
  26.5 8.3 %collective-permute-start.2 = (bf16[1,2,2,8,128]{4,3,2,1,0:T(8,128)(2,1)S(1)}, bf16[1,2,2,8,128]{4,3,2,1,0:T(8,128)(2,1)S(1)}, u32[]{:S(2)}, u32[]{:S(2)}) collective-permute-start(bf16[1,2,2,8,128]{4,3,2,1,0:T(8,128)(2,1)S(1)} %pad_maximum_fusion.5), channel_id=1, source_target_pairs={{0,12},{4,16},{8,20},{12,24},{16,28},{20,0},{24,4},{28,8},{1,13},{... | collective-permute-start | bytes 24584 | tf_op jit(solution)/shard_map/ppermute | solution.py:71
  31.2 6.2 %collective-permute-start.4 = (bf16[1,3,2,8,128]{4,3,2,1,0:T(8,128)(2,1)S(1)}, bf16[1,3,2,8,128]{4,3,2,1,0:T(8,128)(2,1)S(1)}, u32[]{:S(2)}, u32[]{:S(2)}) collective-permute-start(bf16[1,3,2,8,128]{4,3,2,1,0:T(8,128)(2,1)S(1)} %pad_maximum_fusion.4), channel_id=1, source_target_pairs={{0,20},{4,24},{8,28},{12,0},{16,4},{20,8},{24,12},{28,16},{1,21},{... | collective-permute-start | bytes 36872 | tf_op jit(solution)/shard_map/ppermute | solution.py:71
  37.5 2.3 %copy-start.1 = (bf16[8,16,256]{2,1,0:T(8,128)(2,1)S(1)}, bf16[8,16,256]{2,1,0:T(8,128)(2,1)}, u32[]{:S(2)}) copy-start(bf16[8,16,256]{2,1,0:T(8,128)(2,1)} %x_ref.5) | copy-start | bytes 196612
  37.6 5.2 %collective-permute-start.5 = (bf16[1,8,2,8,128]{4,3,2,1,0:T(8,128)(2,1)S(1)}, bf16[1,8,2,8,128]{4,3,2,1,0:T(8,128)(2,1)S(1)}, u32[]{:S(2)}, u32[]{:S(2)}) collective-permute-start(bf16[1,8,2,8,128]{4,3,2,1,0:T(8,128)(2,1)S(1)} %constant_dynamic-slice_fusion), channel_id=1, source_target_pairs={{0,2},{2,0},{1,3},{3,1},{4,6},{6,4},{5,7},{7,5},{8,10},{10,8},{9,1... | collective-permute-start | bytes 98312 | tf_op jit(solution)/shard_map/ppermute | solution.py:40
  39.8 6.1 %copy-start.5 = (bf16[256,256]{1,0:T(8,128)(2,1)S(1)}, bf16[256,256]{1,0:T(8,128)(2,1)}, u32[]{:S(2)}) copy-start(bf16[256,256]{1,0:T(8,128)(2,1)} %out_w_ref.3) | copy-start | bytes 393220
  39.8 6.1 %copy-start.15 = (bf16[256,32]{0,1:T(8,128)(2,1)S(1)}, bf16[256,32]{0,1:T(8,128)(2,1)}, u32[]{:S(2)}) copy-start(bf16[256,32]{0,1:T(8,128)(2,1)} %param.25) | copy-start | bytes 49156
  39.8 6.1 %copy-start.16 = (bf16[256,32]{0,1:T(8,128)(2,1)S(1)}, bf16[256,32]{0,1:T(8,128)(2,1)}, u32[]{:S(2)}) copy-start(bf16[256,32]{0,1:T(8,128)(2,1)} %param.26) | copy-start | bytes 49156
  40.2 5.7 %copy-start.3 = (bf16[256,256]{1,0:T(8,128)(2,1)S(1)}, bf16[256,256]{1,0:T(8,128)(2,1)}, u32[]{:S(2)}) copy-start(bf16[256,256]{1,0:T(8,128)(2,1)} %key_w_ref.1) | copy-start | bytes 393220
  40.2 5.7 %copy-start.4 = (bf16[256,256]{1,0:T(8,128)(2,1)S(1)}, bf16[256,256]{1,0:T(8,128)(2,1)}, u32[]{:S(2)}) copy-start(bf16[256,256]{1,0:T(8,128)(2,1)} %value_w_ref.1) | copy-start | bytes 393220
  64.2 22.7 %copy-start.2 = (bf16[1024,128]{1,0:T(8,128)(2,1)S(1)}, bf16[1024,128]{1,0:T(8,128)(2,1)}, u32[]{:S(2)}) copy-start(bf16[1024,128]{1,0:T(8,128)(2,1)} %outer_w_ref.1) | copy-start | bytes 786436
  64.2 22.7 %copy-start.6 = (bf16[128,512]{1,0:T(8,128)(2,1)S(1)}, bf16[128,512]{1,0:T(8,128)(2,1)}, u32[]{:S(2)}) copy-start(bf16[128,512]{1,0:T(8,128)(2,1)} %in_w_ref.2) | copy-start | bytes 393220
  88.8 5.8 %collective-permute-start.6 = (bf16[16,8,128]{2,1,0:T(8,128)(2,1)S(1)}, bf16[16,8,128]{2,1,0:T(8,128)(2,1)S(1)}, u32[]{:S(2)}, u32[]{:S(2)}) collective-permute-start(bf16[16,8,128]{2,1,0:T(8,128)(2,1)S(1)} %get-tuple-element.27), channel_id=1, source_target_pairs={{0,1},{1,0},{2,3},{3,2},{4,5},{5,4},{6,7},{7,6},{8,9},{9,8},{10,11... | collective-permute-start | bytes 98312 | tf_op jit(solution)/shard_map/ppermute | solution.py:40
  91.1 12.9 %all-to-all-start.3 = ((bf16[16,8,8,128]{3,2,1,0:T(8,128)(2,1)}), bf16[16,8,8,128]{3,2,1,0:T(8,128)(2,1)S(1)}, u32[]{:S(2)}, u32[]{:S(2)}) async-start(bf16[16,8,8,128]{3,2,1,0:T(8,128)(2,1)} %bitcast.6), calls=%async_computation.3 | async-start | bytes 524288 | tf_op jit(solution)/shard_map/all_to_all | solution.py:36
  94.6 6.9 %collective-permute-start.7 = (bf16[16,16,128]{2,1,0:T(8,128)(2,1)S(1)}, bf16[16,16,128]{2,1,0:T(8,128)(2,1)S(1)}, u32[]{:S(2)}, u32[]{:S(2)}) collective-permute-start(bf16[16,16,128]{2,1,0:T(8,128)(2,1)S(1)} %pad_maximum_fusion.2), channel_id=1, source_target_pairs={{0,32},{32,0},{1,33},{33,1},{2,34},{34,2},{3,35},{35,3},{4,36},{36... | collective-permute-start | bytes 196616 | tf_op jit(solution)/shard_map/ppermute | solution.py:40
  105.9 17.3 %copy-start.10 = (bf16[128,512]{1,0:T(8,128)(2,1)S(1)}, bf16[128,512]{1,0:T(8,128)(2,1)}, u32[]{:S(2)}) copy-start(bf16[128,512]{1,0:T(8,128)(2,1)} %in_w_ref.3) | copy-start | bytes 393220
  105.9 17.3 %copy-start.11 = (bf16[128,128]{1,0:T(8,128)(2,1)S(1)}, bf16[128,128]{1,0:T(8,128)(2,1)}, u32[]{:S(2)}) copy-start(bf16[128,128]{1,0:T(8,128)(2,1)} %gate_w_ref.4) | copy-start | bytes 98308
  105.9 17.3 %copy-start.12 = (bf16[128,128]{1,0:T(8,128)(2,1)S(1)}, bf16[128,128]{1,0:T(8,128)(2,1)}, u32[]{:S(2)}) copy-start(bf16[128,128]{1,0:T(8,128)(2,1)} %out_w_ref.4) | copy-start | bytes 98308
  105.9 17.3 %all-to-all-start.4 = ((bf16[16,16,8,128]{3,2,1,0:T(8,128)(2,1)}), bf16[16,16,8,128]{3,2,1,0:T(8,128)(2,1)S(1)}, u32[]{:S(2)}, u32[]{:S(2)}) async-start(bf16[16,16,8,128]{3,2,1,0:T(8,128)(2,1)} %bitcast.8), calls=%async_computation.4 | async-start | bytes 1048576 | tf_op jit(solution)/shard_map/all_to_all | solution.py:36
  110.3 0.7 collective-permute-start.8
  124.6 14.8 %all-to-all-start.5 = ((bf16[8,16,8,128]{3,2,1,0:T(8,128)(2,1)}), bf16[8,16,8,128]{3,2,1,0:T(8,128)(2,1)S(1)}, u32[]{:S(2)}, u32[]{:S(2)}) async-start(bf16[8,16,8,128]{3,2,1,0:T(8,128)(2,1)} %get-tuple-element.29), calls=%async_computation.5 | async-start | bytes 524288 | tf_op jit(solution)/shard_map/all_to_all | solution.py:36
  129.9 14.7 %collective-permute-start.10 = (bf16[8,16,128]{2,1,0:T(8,128)(2,1)S(1)}, bf16[8,16,128]{2,1,0:T(8,128)(2,1)S(1)}, u32[]{:S(2)}, u32[]{:S(2)}) collective-permute-start(bf16[8,16,128]{2,1,0:T(8,128)(2,1)S(1)} %get-tuple-element.30), channel_id=1, source_target_pairs={{0,32},{32,0},{1,33},{33,1},{2,34},{34,2},{3,35},{35,3},{4,36},{36... | collective-permute-start | bytes 98312 | tf_op jit(solution)/shard_map/ppermute | solution.py:40
  139.4 6.4 %collective-permute-start.9 = (bf16[8,16,8,128]{3,2,1,0:T(8,128)(2,1)S(1)}, bf16[8,16,8,128]{3,2,1,0:T(8,128)(2,1)S(1)}, u32[]{:S(2)}, u32[]{:S(2)}) collective-permute-start(bf16[8,16,8,128]{3,2,1,0:T(8,128)(2,1)S(1)} %all-to-all-done.5), channel_id=1, source_target_pairs={{0,1},{1,0},{2,3},{3,2},{4,5},{5,4},{6,7},{7,6},{8,9},{9,8},{10,11... | collective-permute-start | bytes 786440 | tf_op jit(solution)/shard_map/ppermute | solution.py:40
  147.2 20.0 %copy-start.13 = (bf16[128,128]{1,0:T(8,128)(2,1)S(1)}, bf16[128,128]{1,0:T(8,128)(2,1)}, u32[]{:S(2)}) copy-start(bf16[128,128]{1,0:T(8,128)(2,1)} %gate_w_ref.5) | copy-start | bytes 98308
  147.2 20.0 %copy-start.14 = (bf16[128,128]{1,0:T(8,128)(2,1)S(1)}, bf16[128,128]{1,0:T(8,128)(2,1)}, u32[]{:S(2)}) copy-start(bf16[128,128]{1,0:T(8,128)(2,1)} %out_w_ref.5) | copy-start | bytes 98308
  147.2 20.0 %all-to-all-start.6 = ((bf16[16,2,8,8,128]{4,3,2,1,0:T(8,128)(2,1)}), bf16[16,2,8,8,128]{4,3,2,1,0:T(8,128)(2,1)S(1)}, u32[]{:S(2)}, u32[]{:S(2)}) async-start(bf16[16,2,8,8,128]{4,3,2,1,0:T(8,128)(2,1)} %bitcast.11), calls=%async_computation.6 | async-start | bytes 1048576 | tf_op jit(solution)/shard_map/all_to_all | solution.py:36
  153.6 0.7 collective-permute-start.11
  (3 other events, 3.4 us)

commit v7 on v6

--- a/solution.py
+++ b/solution.py
@@ -183,8 +183,15 @@
     return left, right
 
 
-def updated(combined, pair, gate_w_ref, out_w_ref):
-    gate = sigmoid(project(layer_norm(pair).astype(BF16), gate_w_ref[...]))
+def pair_gate_kernel(pair_ref, gate_w_ref, gate_ref):
+    gate_ref[...] = sigmoid(project(layer_norm(pair_ref[...]).astype(BF16), gate_w_ref[...]))
+
+
+def pair_gate(pair, weight):
+    return kernel_call(pair_gate_kernel, [(pair.shape, F32)], (pair, weight))[0]
+
+
+def updated(combined, pair, gate, out_w_ref):
     update = project(layer_norm(combined).astype(BF16), out_w_ref[...])
     return (pair.astype(F32) + gate * update).astype(BF16)
 
@@ -256,7 +263,7 @@
                     out_ref[part, 2 * g + u, 1, place] = totals[u].astype(BF16)
         return carry
 
-    lax.fori_loop(0, groups // 2, one, 0)
+    lax.fori_loop(0, groups // 2, one, 0, unroll=True)
 
 
 def partial_sums(tiles, lines, before=None):
@@ -280,11 +287,11 @@
 
 
 def middle_kernel(
-    partial_ref, pair_ref, gate_w_ref, out_w_ref, in_w_ref, pair_out, chunks_out, line_out, right_scr
+    partial_ref, pair_ref, gate_ref, out_w_ref, in_w_ref, pair_out, chunks_out, line_out, right_scr
 ):
     rows, cols, depth = partial_ref.shape[1:]
     combined = added(partial_ref).reshape(rows * cols, depth)
-    pair = updated(combined, pair_ref[...], gate_w_ref, out_w_ref)
+    pair = updated(combined, pair_ref[...], gate_ref[...], out_w_ref)
     pair_out[...] = pair
     left, right = edge_parts(pair, in_w_ref)
     left = left.reshape(rows, cols, depth).astype(BF16)
@@ -295,7 +302,7 @@
         line_out[j] = right_scr[pl.ds(j, rows, stride=cols), :].astype(BF16)
 
 
-def last_kernel(core_ref, partial_ref, pair_ref, gate_w_ref, out_w_ref, new_ref, scr):
+def last_kernel(core_ref, partial_ref, pair_ref, gate_ref, out_w_ref, new_ref, scr):
     halves, cols, tall, depth = partial_ref.shape[1:]
     scr[...] = added(partial_ref).reshape(halves * cols * tall, depth)
     own, other = [
@@ -308,7 +315,7 @@
     combined = jnp.concatenate(
         [jnp.where(first, own, other), jnp.where(first, other, own)], axis=0
     )
-    new = updated(combined, pair_ref[...], gate_w_ref, out_w_ref)
+    new = updated(combined, pair_ref[...], gate_ref[...], out_w_ref)
     new_ref[...] = new.astype(F32).reshape(new_ref.shape).astype(BF16)
 
 
@@ -392,6 +399,7 @@
     lines = in_order(x_hi, lines, flip(lines, "xh"))
     partial = partial_sums(tiles, lines).reshape(ROWS, rows, cols, depth)
     partial = exchange(partial, ("xl", "y"))
+    crossed = cross(pair_one)
     pair_two, chunks, lines = kernel_call(
         middle_kernel,
         [
@@ -399,7 +407,7 @@
             ((SIZES["y"], rows, cols, depth), BF16),
             ((cols, rows, depth), BF16),
         ],
-        (partial, cross(pair_one), outgoing_gate, outgoing_output, incoming_project),
+        (partial, crossed, pair_gate(crossed, outgoing_gate), outgoing_output, incoming_project),
         scratch=[((places, depth), F32)],
     )
 
@@ -408,10 +416,12 @@
     other = flip(own, "core")
     partial = partial_sums(other[None], lines, partial_sums(own[None], lines))
     partial = exchange(partial.reshape(ROWS, 2, cols, cols, depth), ("xl", "z"))
+    crossed = cross(pair_two)
+    gate = pair_gate(crossed, incoming_gate)
     new_pair = kernel_call(
         last_kernel,
         [((rows, cols, depth), BF16)],
-        (jnp.full((8, depth), core), partial, cross(pair_two), incoming_gate, incoming_output),
+        (jnp.full((8, depth), core), partial, crossed, gate, incoming_output),
         scratch=[((places, depth), F32)],
     )[0]
     return (new_alignment, new_pair)

time: 170 us -> 170 us (level)
    pallas_call x11 -> x13, Pallas kernels: 13.1 us -> 13.6 us  [kernel_call(): pl.pallas_call(body, out_shape=shapes, in_specs=[pl.BlockSpec() if fetche...]
where the time goes in v7:
time: 170 us; the launch traced here: 168 us
  starting transfers between devices  68.7 us (40%)
  waiting for transfers between devices  45.5 us (27%)
  blocking collectives  38 us (22%)
  Pallas kernels  13.6 us (8%)
    all_to_all x2, blocking collectives, exchange(): return lax.all_to_all(chunks, axes, 0, 0)  38 us
    all_to_all x5, waiting for transfers between devices, exchange(): return lax.all_to_all(chunks, axes, 0, 0)  36.2 us
    all_to_all x5, starting transfers between devices, exchange(): return lax.all_to_all(chunks, axes, 0, 0)  26.9 us
    ppermute x6, starting transfers between devices, flip(): return lax.ppermute(block, axis, FLIP)  24.9 us
    ppermute x4, starting transfers between devices, shifted(): lax.ppermute(block, 'y', [(y, (y - step) % size) for y in range(size)])  15.4 us
    pallas_call x13, Pallas kernels, kernel_call(): pl.pallas_call(body, out_shape=shapes, in_specs=[pl.BlockSpec() if fetche...  13.6 us
    ppermute x6, waiting for transfers between devices, flip(): return lax.ppermute(block, axis, FLIP)  6.73 us
  transfers between devices with their start and end apart: 17, of which 9 were waited for; matrix products, arithmetic and copies ran while one was open for 0% of the time, Pallas kernels for 1%

profile of v7, /device:TPU:1, one launch (start us, length us, event | category | flops | bytes accessed | tf_op | source)
XLA Modules:
  0.0 168.1 jit_solution(10733524433400591978)
XLA Ops:
  1.5 1.3 shard_map.176
  3.1 8.8 %collective-permute-start = (bf16[1,1,1,8,128]{4,3,2,1,0:T(8,128)(2,1)S(1)}, bf16[1,1,1,8,128]{4,3,2,1,0:T(8,128)(2,1)S(1)}, u32[]{:S(2)}, u32[]{:S(2)}) collective-permute-start(bf16[1,1,1,8,128]{4,3,2,1,0:T(8,128)(2,1)S(1)} %bitcast.21), channel_id=1, source_target_pairs={{0,1},{1,0},{2,3},{3,2},{4,5},{5,4},{6,7},{7,6},{8,9},{9,8},{10,11... | collective-permute-start | bytes 6152 | tf_op jit(solution)/shard_map/ppermute | solution.py:40
  11.9 7.4 %all-to-all-start = ((bf16[16,8,16,256]{3,2,1,0:T(8,128)(2,1)}), bf16[16,8,16,256]{3,2,1,0:T(8,128)(2,1)S(1)}, u32[]{:S(2)}, u32[]{:S(2)}) async-start(bf16[16,8,16,256]{3,2,1,0:T(8,128)(2,1)} %shard_map.176), calls=%async_computation | async-start | bytes 2097152 | tf_op jit(solution)/shard_map/all_to_all | solution.py:36
  19.3 5.1 %collective-permute-start.1 = (bf16[1,1,2,8,128]{4,3,2,1,0:T(8,128)(2,1)S(1)}, bf16[1,1,2,8,128]{4,3,2,1,0:T(8,128)(2,1)S(1)}, u32[]{:S(2)}, u32[]{:S(2)}) collective-permute-start(bf16[1,1,2,8,128]{4,3,2,1,0:T(8,128)(2,1)S(1)} %pad_maximum_fusion.6), channel_id=1, source_target_pairs={{0,28},{4,0},{8,4},{12,8},{16,12},{20,16},{24,20},{28,24},{1,29},{... | collective-permute-start | bytes 12296 | tf_op jit(solution)/shard_map/ppermute | solution.py:71
  24.4 2.1 %collective-permute-start.3 = (bf16[1,1,2,8,128]{4,3,2,1,0:T(8,128)(2,1)S(1)}, bf16[1,1,2,8,128]{4,3,2,1,0:T(8,128)(2,1)S(1)}, u32[]{:S(2)}, u32[]{:S(2)}) collective-permute-start(bf16[1,1,2,8,128]{4,3,2,1,0:T(8,128)(2,1)S(1)} %pad_maximum_fusion.6), channel_id=1, source_target_pairs={{0,4},{4,8},{8,12},{12,16},{16,20},{20,24},{24,28},{28,0},{1,5},{5... | collective-permute-start | bytes 12296 | tf_op jit(solution)/shard_map/ppermute | solution.py:71
  26.5 4.7 %collective-permute-start.2 = (bf16[1,2,2,8,128]{4,3,2,1,0:T(8,128)(2,1)S(1)}, bf16[1,2,2,8,128]{4,3,2,1,0:T(8,128)(2,1)S(1)}, u32[]{:S(2)}, u32[]{:S(2)}) collective-permute-start(bf16[1,2,2,8,128]{4,3,2,1,0:T(8,128)(2,1)S(1)} %pad_maximum_fusion.5), channel_id=1, source_target_pairs={{0,12},{4,16},{8,20},{12,24},{16,28},{20,0},{24,4},{28,8},{1,13},{... | collective-permute-start | bytes 24584 | tf_op jit(solution)/shard_map/ppermute | solution.py:71
  31.2 3.6 %collective-permute-start.4 = (bf16[1,3,2,8,128]{4,3,2,1,0:T(8,128)(2,1)S(1)}, bf16[1,3,2,8,128]{4,3,2,1,0:T(8,128)(2,1)S(1)}, u32[]{:S(2)}, u32[]{:S(2)}) collective-permute-start(bf16[1,3,2,8,128]{4,3,2,1,0:T(8,128)(2,1)S(1)} %pad_maximum_fusion.4), channel_id=1, source_target_pairs={{0,20},{4,24},{8,28},{12,0},{16,4},{20,8},{24,12},{28,16},{1,21},{... | collective-permute-start | bytes 36872 | tf_op jit(solution)/shard_map/ppermute | solution.py:71
  34.9 2.6 %collective-permute-done.4 = bf16[1,3,2,8,128]{4,3,2,1,0:T(8,128)(2,1)S(1)} collective-permute-done((bf16[1,3,2,8,128]{4,3,2,1,0:T(8,128)(2,1)S(1)}, bf16[1,3,2,8,128]{4,3,2,1,0:T(8,128)(2,1)S(1)}, u32[]{:S(2)}, u32[]{:S(2)}) %collective-permute-start.4) | collective-permute-done | bytes 12320 | tf_op jit(solution)/shard_map/ppermute | solution.py:71
  37.6 2.2 %collective-permute-start.5 = (bf16[1,8,2,8,128]{4,3,2,1,0:T(8,128)(2,1)S(1)}, bf16[1,8,2,8,128]{4,3,2,1,0:T(8,128)(2,1)S(1)}, u32[]{:S(2)}, u32[]{:S(2)}) collective-permute-start(bf16[1,8,2,8,128]{4,3,2,1,0:T(8,128)(2,1)S(1)} %constant_dynamic-slice_fusion), channel_id=1, source_target_pairs={{0,2},{2,0},{1,3},{3,1},{4,6},{6,4},{5,7},{7,5},{8,10},{10,8},{9,1... | collective-permute-start | bytes 98312 | tf_op jit(solution)/shard_map/ppermute | solution.py:40
  40.2 2.5 %collective-permute-done.5 = bf16[1,8,2,8,128]{4,3,2,1,0:T(8,128)(2,1)S(1)} collective-permute-done((bf16[1,8,2,8,128]{4,3,2,1,0:T(8,128)(2,1)S(1)}, bf16[1,8,2,8,128]{4,3,2,1,0:T(8,128)(2,1)S(1)}, u32[]{:S(2)}, u32[]{:S(2)}) %collective-permute-start.5) | collective-permute-done | bytes 32800 | tf_op jit(solution)/shard_map/ppermute | solution.py:40
  42.7 3.1 %all-to-all-done.every_ref = bf16[16,8,16,256]{3,2,1,0:T(8,128)(2,1)S(1)} async-done(((bf16[16,8,16,256]{3,2,1,0:T(8,128)(2,1)}), bf16[16,8,16,256]{3,2,1,0:T(8,128)(2,1)S(1)}, u32[]{:S(2)}, u32[]{:S(2)}) %all-to-all-start) | async-done | bytes 1048608 | tf_op jit(solution)/shard_map/all_to_all | solution.py:36
  45.9 3.0 %shard_map.179 = (bf16[8,16,256]{2,1,0:T(8,128)(2,1)}, bf16[8,512]{1,0:T(8,128)(2,1)S(1)}, bf16[16,8,512]{2,1,0:T(8,128)(2,1)S(1)}) custom-call(bf16[16,8,16,256]{3,2,1,0:T(8,128)(2,1)S(1)} %all-to-all-done.every_ref, bf16[256,128]{1,0:T(8,128)(2,1)S(1)} %bitcast.17, bf16[8,16,256]{2,1,0:T(8,128)(2,1)S(1)} %get-tuple-element.21.query_ref, ...), custom_call_target="tpu_custom_call" | custom-call | bytes 2007040 | tf_op jit(solution)/shard_map/pallas_call | solution.py:58
  48.9 15.2 %all_to_all.35.right_ref = bf16[16,8,512]{2,1,0:T(8,128)(2,1)S(1)} all-to-all(bf16[16,8,512]{2,1,0:T(8,128)(2,1)S(1)} %get-tuple-element.25), channel_id=1, replica_groups=mesh['z'=8,'xh'=2,'y'=8,'xl'=2,'core'=2] {'xh','z'}, dimensions={0} | all-to-all | bytes 262144 | tf_op jit(solution)/shard_map/all_to_all | solution.py:36
  64.2 22.7 %all_to_all.36 = bf16[32,8,768]{2,1,0:T(8,128)(2,1)S(1)} all-to-all(bf16[32,8,768]{2,1,0:T(8,128)(2,1)S(1)} %shard_map.180), channel_id=1, replica_groups=mesh['z'=8,'xh'=2,'y'=8,'xl'=2,'core'=2] {'xl','core','y'}, dimensions={0} | all-to-all | bytes 786432 | tf_op jit(solution)/shard_map/all_to_all | solution.py:36
  86.9 1.9 %shard_map.181 = (bf16[128,128]{1,0:T(8,128)(2,1)S(1)}, bf16[16,8,128]{2,1,0:T(8,128)(2,1)S(1)}, bf16[2,8,8,8,128]{4,3,2,1,0:T(8,128)(2,1)}) custom-call(bf16[256,768]{1,0:T(8,128)(2,1)S(1)} %bitcast.14, bf16[16,8,128]{2,1,0:T(8,128)(2,1)S(1)} %copy-done.7, bf16[1024,128]{1,0:T(8,128)(2,1)S(1)} %copy-done.2, bf16[128,512]{1,0:T(8,128)(2,1)S(1)} %copy-done.6), custom_call_target="tpu_custom_call" | custom-call | bytes 1146880 | tf_op jit(solution)/shard_map/pallas_call | solution.py:58
  88.8 2.3 %collective-permute-start.6 = (bf16[16,8,128]{2,1,0:T(8,128)(2,1)S(1)}, bf16[16,8,128]{2,1,0:T(8,128)(2,1)S(1)}, u32[]{:S(2)}, u32[]{:S(2)}) collective-permute-start(bf16[16,8,128]{2,1,0:T(8,128)(2,1)S(1)} %get-tuple-element.27), channel_id=1, source_target_pairs={{0,1},{1,0},{2,3},{3,2},{4,5},{5,4},{6,7},{7,6},{8,9},{9,8},{10,11... | collective-permute-start | bytes 98312 | tf_op jit(solution)/shard_map/ppermute | solution.py:40
  91.1 3.5 %all-to-all-start.3 = ((bf16[16,8,8,128]{3,2,1,0:T(8,128)(2,1)}), bf16[16,8,8,128]{3,2,1,0:T(8,128)(2,1)S(1)}, u32[]{:S(2)}, u32[]{:S(2)}) async-start(bf16[16,8,8,128]{3,2,1,0:T(8,128)(2,1)} %bitcast.6), calls=%async_computation.3 | async-start | bytes 524288 | tf_op jit(solution)/shard_map/all_to_all | solution.py:36
  94.6 3.2 %collective-permute-start.7 = (bf16[16,16,128]{2,1,0:T(8,128)(2,1)S(1)}, bf16[16,16,128]{2,1,0:T(8,128)(2,1)S(1)}, u32[]{:S(2)}, u32[]{:S(2)}) collective-permute-start(bf16[16,16,128]{2,1,0:T(8,128)(2,1)S(1)} %pad_maximum_fusion.2), channel_id=1, source_target_pairs={{0,32},{32,0},{1,33},{33,1},{2,34},{34,2},{3,35},{35,3},{4,36},{36... | collective-permute-start | bytes 196616 | tf_op jit(solution)/shard_map/ppermute | solution.py:40
  97.8 3.7 %collective-permute-done.7 = bf16[16,16,128]{2,1,0:T(8,128)(2,1)S(1)} collective-permute-done((bf16[16,16,128]{2,1,0:T(8,128)(2,1)S(1)}, bf16[16,16,128]{2,1,0:T(8,128)(2,1)S(1)}, u32[]{:S(2)}, u32[]{:S(2)}) %collective-permute-start.7) | collective-permute-done | bytes 65568 | tf_op jit(solution)/shard_map/ppermute | solution.py:40
  101.6 2.4 %all-to-all-done.3 = bf16[16,8,8,128]{3,2,1,0:T(8,128)(2,1)S(1)} async-done(((bf16[16,8,8,128]{3,2,1,0:T(8,128)(2,1)}), bf16[16,8,8,128]{3,2,1,0:T(8,128)(2,1)S(1)}, u32[]{:S(2)}, u32[]{:S(2)}) %all-to-all-start.3) | async-done | bytes 262176 | tf_op jit(solution)/shard_map/all_to_all | solution.py:36
  104.0 1.9 %shard_map.182 = bf16[2,8,16,8,128]{4,3,2,1,0:T(8,128)(2,1)} custom-call(bf16[2,8,8,8,128]{4,3,2,1,0:T(8,128)(2,1)S(1)} %bitcast.15, bf16[32,16,128]{2,1,0:T(8,128)(2,1)S(1)} %pad_maximum_fusion.line_ref), custom_call_target="tpu_custom_call" | custom-call | flops 8388608 | bytes 917504 | tf_op jit(solution)/shard_map/pallas_call | solution.py:58
  105.9 4.3 %all-to-all-start.4 = ((bf16[16,16,8,128]{3,2,1,0:T(8,128)(2,1)}), bf16[16,16,8,128]{3,2,1,0:T(8,128)(2,1)S(1)}, u32[]{:S(2)}, u32[]{:S(2)}) async-start(bf16[16,16,8,128]{3,2,1,0:T(8,128)(2,1)} %bitcast.8), calls=%async_computation.4 | async-start | bytes 1048576 | tf_op jit(solution)/shard_map/all_to_all | solution.py:36
  111.4 11.8 %all-to-all-done.4.partial_ref = bf16[16,16,8,128]{3,2,1,0:T(8,128)(2,1)S(1)} async-done(((bf16[16,16,8,128]{3,2,1,0:T(8,128)(2,1)}), bf16[16,16,8,128]{3,2,1,0:T(8,128)(2,1)S(1)}, u32[]{:S(2)}, u32[]{:S(2)}) %all-to-all-start.4) | async-done | bytes 524320 | tf_op jit(solution)/shard_map/all_to_all | solution.py:36
  123.2 1.4 shard_map.184
  124.6 5.3 %all-to-all-start.5 = ((bf16[8,16,8,128]{3,2,1,0:T(8,128)(2,1)}), bf16[8,16,8,128]{3,2,1,0:T(8,128)(2,1)S(1)}, u32[]{:S(2)}, u32[]{:S(2)}) async-start(bf16[8,16,8,128]{3,2,1,0:T(8,128)(2,1)} %get-tuple-element.29), calls=%async_computation.5 | async-start | bytes 524288 | tf_op jit(solution)/shard_map/all_to_all | solution.py:36
  129.9 3.2 %collective-permute-start.10 = (bf16[8,16,128]{2,1,0:T(8,128)(2,1)S(1)}, bf16[8,16,128]{2,1,0:T(8,128)(2,1)S(1)}, u32[]{:S(2)}, u32[]{:S(2)}) collective-permute-start(bf16[8,16,128]{2,1,0:T(8,128)(2,1)S(1)} %get-tuple-element.30), channel_id=1, source_target_pairs={{0,32},{32,0},{1,33},{33,1},{2,34},{34,2},{3,35},{35,3},{4,36},{36... | collective-permute-start | bytes 98312 | tf_op jit(solution)/shard_map/ppermute | solution.py:40
  133.1 6.3 %all-to-all-done.5 = bf16[8,16,8,128]{3,2,1,0:T(8,128)(2,1)S(1)} async-done(((bf16[8,16,8,128]{3,2,1,0:T(8,128)(2,1)}), bf16[8,16,8,128]{3,2,1,0:T(8,128)(2,1)S(1)}, u32[]{:S(2)}, u32[]{:S(2)}) %all-to-all-start.5) | async-done | bytes 262176 | tf_op jit(solution)/shard_map/all_to_all | solution.py:36
  139.4 5.2 %collective-permute-start.9 = (bf16[8,16,8,128]{3,2,1,0:T(8,128)(2,1)S(1)}, bf16[8,16,8,128]{3,2,1,0:T(8,128)(2,1)S(1)}, u32[]{:S(2)}, u32[]{:S(2)}) collective-permute-start(bf16[8,16,8,128]{3,2,1,0:T(8,128)(2,1)S(1)} %all-to-all-done.5), channel_id=1, source_target_pairs={{0,1},{1,0},{2,3},{3,2},{4,5},{5,4},{6,7},{7,6},{8,9},{9,8},{10,11... | collective-permute-start | bytes 786440 | tf_op jit(solution)/shard_map/ppermute | solution.py:40
  145.8 1.4 shard_map.186
  147.1 6.4 %all-to-all-start.6 = ((bf16[16,2,8,8,128]{4,3,2,1,0:T(8,128)(2,1)}), bf16[16,2,8,8,128]{4,3,2,1,0:T(8,128)(2,1)S(1)}, u32[]{:S(2)}, u32[]{:S(2)}) async-start(bf16[16,2,8,8,128]{4,3,2,1,0:T(8,128)(2,1)} %bitcast.11), calls=%async_computation.6 | async-start | bytes 1048576 | tf_op jit(solution)/shard_map/all_to_all | solution.py:36
  154.6 12.6 %all-to-all-done.6.partial_ref = bf16[16,2,8,8,128]{4,3,2,1,0:T(8,128)(2,1)S(1)} async-done(((bf16[16,2,8,8,128]{4,3,2,1,0:T(8,128)(2,1)}), bf16[16,2,8,8,128]{4,3,2,1,0:T(8,128)(2,1)S(1)}, u32[]{:S(2)}, u32[]{:S(2)}) %all-to-all-start.6) | async-done | bytes 524320 | tf_op jit(solution)/shard_map/all_to_all | solution.py:36
  167.1 1.0 shard_map.188
  (77 shorter events, 5.0 us)
Async XLA Ops:
  3.1 16.2 %collective-permute-start = (bf16[1,1,1,8,128]{4,3,2,1,0:T(8,128)(2,1)S(1)}, bf16[1,1,1,8,128]{4,3,2,1,0:T(8,128)(2,1)S(1)}, u32[]{:S(2)}, u32[]{:S(2)}) collective-permute-start(bf16[1,1,1,8,128]{4,3,2,1,0:T(8,128)(2,1)S(1)} %bitcast.21), channel_id=1, source_target_pairs={{0,1},{1,0},{2,3},{3,2},{4,5},{5,4},{6,7},{7,6},{8,9},{9,8},{10,11... | collective-permute-start | bytes 6152 | tf_op jit(solution)/shard_map/ppermute | solution.py:40
  11.8 27.9 %copy-start.9 = (bf16[256,256]{1,0:T(8,128)(2,1)S(1)}, bf16[256,256]{1,0:T(8,128)(2,1)}, u32[]{:S(2)}) copy-start(bf16[256,256]{1,0:T(8,128)(2,1)} %gate_w_ref.3) | copy-start | bytes 393220
  11.9 34.0 %all-to-all-start = ((bf16[16,8,16,256]{3,2,1,0:T(8,128)(2,1)}), bf16[16,8,16,256]{3,2,1,0:T(8,128)(2,1)S(1)}, u32[]{:S(2)}, u32[]{:S(2)}) async-start(bf16[16,8,16,256]{3,2,1,0:T(8,128)(2,1)} %shard_map.176), calls=%async_computation | async-start | bytes 2097152 | tf_op jit(solution)/shard_map/all_to_all | solution.py:36
  19.3 7.2 %collective-permute-start.1 = (bf16[1,1,2,8,128]{4,3,2,1,0:T(8,128)(2,1)S(1)}, bf16[1,1,2,8,128]{4,3,2,1,0:T(8,128)(2,1)S(1)}, u32[]{:S(2)}, u32[]{:S(2)}) collective-permute-start(bf16[1,1,2,8,128]{4,3,2,1,0:T(8,128)(2,1)S(1)} %pad_maximum_fusion.6), channel_id=1, source_target_pairs={{0,28},{4,0},{8,4},{12,8},{16,12},{20,16},{24,20},{28,24},{1,29},{... | collective-permute-start | bytes 12296 | tf_op jit(solution)/shard_map/ppermute | solution.py:71
  24.4 15.4 %copy-start.8 = (bf16[256,256]{1,0:T(8,128)(2,1)S(1)}, bf16[256,256]{1,0:T(8,128)(2,1)}, u32[]{:S(2)}) copy-start(bf16[256,256]{1,0:T(8,128)(2,1)} %query_w_ref) | copy-start | bytes 393220
  24.4 6.8 %collective-permute-start.3 = (bf16[1,1,2,8,128]{4,3,2,1,0:T(8,128)(2,1)S(1)}, bf16[1,1,2,8,128]{4,3,2,1,0:T(8,128)(2,1)S(1)}, u32[]{:S(2)}, u32[]{:S(2)}) collective-permute-start(bf16[1,1,2,8,128]{4,3,2,1,0:T(8,128)(2,1)S(1)} %pad_maximum_fusion.6), channel_id=1, source_target_pairs={{0,4},{4,8},{8,12},{12,16},{16,20},{20,24},{24,28},{28,0},{1,5},{5... | collective-permute-start | bytes 12296 | tf_op jit(solution)/shard_map/ppermute | solution.py:71
  26.5 8.3 %collective-permute-start.2 = (bf16[1,2,2,8,128]{4,3,2,1,0:T(8,128)(2,1)S(1)}, bf16[1,2,2,8,128]{4,3,2,1,0:T(8,128)(2,1)S(1)}, u32[]{:S(2)}, u32[]{:S(2)}) collective-permute-start(bf16[1,2,2,8,128]{4,3,2,1,0:T(8,128)(2,1)S(1)} %pad_maximum_fusion.5), channel_id=1, source_target_pairs={{0,12},{4,16},{8,20},{12,24},{16,28},{20,0},{24,4},{28,8},{1,13},{... | collective-permute-start | bytes 24584 | tf_op jit(solution)/shard_map/ppermute | solution.py:71
  31.2 6.2 %collective-permute-start.4 = (bf16[1,3,2,8,128]{4,3,2,1,0:T(8,128)(2,1)S(1)}, bf16[1,3,2,8,128]{4,3,2,1,0:T(8,128)(2,1)S(1)}, u32[]{:S(2)}, u32[]{:S(2)}) collective-permute-start(bf16[1,3,2,8,128]{4,3,2,1,0:T(8,128)(2,1)S(1)} %pad_maximum_fusion.4), channel_id=1, source_target_pairs={{0,20},{4,24},{8,28},{12,0},{16,4},{20,8},{24,12},{28,16},{1,21},{... | collective-permute-start | bytes 36872 | tf_op jit(solution)/shard_map/ppermute | solution.py:71
  37.5 2.3 %copy-start.1 = (bf16[8,16,256]{2,1,0:T(8,128)(2,1)S(1)}, bf16[8,16,256]{2,1,0:T(8,128)(2,1)}, u32[]{:S(2)}) copy-start(bf16[8,16,256]{2,1,0:T(8,128)(2,1)} %x_ref.5) | copy-start | bytes 196612
  37.6 5.2 %collective-permute-start.5 = (bf16[1,8,2,8,128]{4,3,2,1,0:T(8,128)(2,1)S(1)}, bf16[1,8,2,8,128]{4,3,2,1,0:T(8,128)(2,1)S(1)}, u32[]{:S(2)}, u32[]{:S(2)}) collective-permute-start(bf16[1,8,2,8,128]{4,3,2,1,0:T(8,128)(2,1)S(1)} %constant_dynamic-slice_fusion), channel_id=1, source_target_pairs={{0,2},{2,0},{1,3},{3,1},{4,6},{6,4},{5,7},{7,5},{8,10},{10,8},{9,1... | collective-permute-start | bytes 98312 | tf_op jit(solution)/shard_map/ppermute | solution.py:40
  39.8 6.1 %copy-start.5 = (bf16[256,256]{1,0:T(8,128)(2,1)S(1)}, bf16[256,256]{1,0:T(8,128)(2,1)}, u32[]{:S(2)}) copy-start(bf16[256,256]{1,0:T(8,128)(2,1)} %out_w_ref.3) | copy-start | bytes 393220
  39.8 6.1 %copy-start.15 = (bf16[256,32]{0,1:T(8,128)(2,1)S(1)}, bf16[256,32]{0,1:T(8,128)(2,1)}, u32[]{:S(2)}) copy-start(bf16[256,32]{0,1:T(8,128)(2,1)} %param.25) | copy-start | bytes 49156
  39.8 6.1 %copy-start.16 = (bf16[256,32]{0,1:T(8,128)(2,1)S(1)}, bf16[256,32]{0,1:T(8,128)(2,1)}, u32[]{:S(2)}) copy-start(bf16[256,32]{0,1:T(8,128)(2,1)} %param.26) | copy-start | bytes 49156
  40.2 5.7 %copy-start.3 = (bf16[256,256]{1,0:T(8,128)(2,1)S(1)}, bf16[256,256]{1,0:T(8,128)(2,1)}, u32[]{:S(2)}) copy-start(bf16[256,256]{1,0:T(8,128)(2,1)} %key_w_ref.1) | copy-start | bytes 393220
  40.2 5.7 %copy-start.4 = (bf16[256,256]{1,0:T(8,128)(2,1)S(1)}, bf16[256,256]{1,0:T(8,128)(2,1)}, u32[]{:S(2)}) copy-start(bf16[256,256]{1,0:T(8,128)(2,1)} %value_w_ref.1) | copy-start | bytes 393220
  64.2 22.7 %copy-start.2 = (bf16[1024,128]{1,0:T(8,128)(2,1)S(1)}, bf16[1024,128]{1,0:T(8,128)(2,1)}, u32[]{:S(2)}) copy-start(bf16[1024,128]{1,0:T(8,128)(2,1)} %outer_w_ref.1) | copy-start | bytes 786436
  64.2 22.7 %copy-start.6 = (bf16[128,512]{1,0:T(8,128)(2,1)S(1)}, bf16[128,512]{1,0:T(8,128)(2,1)}, u32[]{:S(2)}) copy-start(bf16[128,512]{1,0:T(8,128)(2,1)} %in_w_ref.2) | copy-start | bytes 393220
  88.8 5.8 %collective-permute-start.6 = (bf16[16,8,128]{2,1,0:T(8,128)(2,1)S(1)}, bf16[16,8,128]{2,1,0:T(8,128)(2,1)S(1)}, u32[]{:S(2)}, u32[]{:S(2)}) collective-permute-start(bf16[16,8,128]{2,1,0:T(8,128)(2,1)S(1)} %get-tuple-element.27), channel_id=1, source_target_pairs={{0,1},{1,0},{2,3},{3,2},{4,5},{5,4},{6,7},{7,6},{8,9},{9,8},{10,11... | collective-permute-start | bytes 98312 | tf_op jit(solution)/shard_map/ppermute | solution.py:40
  91.1 12.9 %all-to-all-start.3 = ((bf16[16,8,8,128]{3,2,1,0:T(8,128)(2,1)}), bf16[16,8,8,128]{3,2,1,0:T(8,128)(2,1)S(1)}, u32[]{:S(2)}, u32[]{:S(2)}) async-start(bf16[16,8,8,128]{3,2,1,0:T(8,128)(2,1)} %bitcast.6), calls=%async_computation.3 | async-start | bytes 524288 | tf_op jit(solution)/shard_map/all_to_all | solution.py:36
  94.6 6.9 %collective-permute-start.7 = (bf16[16,16,128]{2,1,0:T(8,128)(2,1)S(1)}, bf16[16,16,128]{2,1,0:T(8,128)(2,1)S(1)}, u32[]{:S(2)}, u32[]{:S(2)}) collective-permute-start(bf16[16,16,128]{2,1,0:T(8,128)(2,1)S(1)} %pad_maximum_fusion.2), channel_id=1, source_target_pairs={{0,32},{32,0},{1,33},{33,1},{2,34},{34,2},{3,35},{35,3},{4,36},{36... | collective-permute-start | bytes 196616 | tf_op jit(solution)/shard_map/ppermute | solution.py:40
  105.9 5.2 %copy-start.12 = (bf16[128,128]{1,0:T(8,128)(2,1)S(1)}, bf16[128,128]{1,0:T(8,128)(2,1)}, u32[]{:S(2)}) copy-start(bf16[128,128]{1,0:T(8,128)(2,1)} %gate_w_ref.4) | copy-start | bytes 98308
  105.9 17.3 %copy-start.11 = (bf16[128,128]{1,0:T(8,128)(2,1)S(1)}, bf16[128,128]{1,0:T(8,128)(2,1)}, u32[]{:S(2)}) copy-start(bf16[128,128]{1,0:T(8,128)(2,1)} %out_w_ref.4) | copy-start | bytes 98308
  105.9 17.3 %all-to-all-start.4 = ((bf16[16,16,8,128]{3,2,1,0:T(8,128)(2,1)}), bf16[16,16,8,128]{3,2,1,0:T(8,128)(2,1)S(1)}, u32[]{:S(2)}, u32[]{:S(2)}) async-start(bf16[16,16,8,128]{3,2,1,0:T(8,128)(2,1)} %bitcast.8), calls=%async_computation.4 | async-start | bytes 1048576 | tf_op jit(solution)/shard_map/all_to_all | solution.py:36
  110.3 13.0 %copy-start.10 = (bf16[128,512]{1,0:T(8,128)(2,1)S(1)}, bf16[128,512]{1,0:T(8,128)(2,1)}, u32[]{:S(2)}) copy-start(bf16[128,512]{1,0:T(8,128)(2,1)} %in_w_ref.3) | copy-start | bytes 393220
  110.3 0.8 collective-permute-start.8
  124.6 14.8 %all-to-all-start.5 = ((bf16[8,16,8,128]{3,2,1,0:T(8,128)(2,1)}), bf16[8,16,8,128]{3,2,1,0:T(8,128)(2,1)S(1)}, u32[]{:S(2)}, u32[]{:S(2)}) async-start(bf16[8,16,8,128]{3,2,1,0:T(8,128)(2,1)} %get-tuple-element.29), calls=%async_computation.5 | async-start | bytes 524288 | tf_op jit(solution)/shard_map/all_to_all | solution.py:36
  129.9 14.7 %collective-permute-start.10 = (bf16[8,16,128]{2,1,0:T(8,128)(2,1)S(1)}, bf16[8,16,128]{2,1,0:T(8,128)(2,1)S(1)}, u32[]{:S(2)}, u32[]{:S(2)}) collective-permute-start(bf16[8,16,128]{2,1,0:T(8,128)(2,1)S(1)} %get-tuple-element.30), channel_id=1, source_target_pairs={{0,32},{32,0},{1,33},{33,1},{2,34},{34,2},{3,35},{35,3},{4,36},{36... | collective-permute-start | bytes 98312 | tf_op jit(solution)/shard_map/ppermute | solution.py:40
  139.4 6.4 %collective-permute-start.9 = (bf16[8,16,8,128]{3,2,1,0:T(8,128)(2,1)S(1)}, bf16[8,16,8,128]{3,2,1,0:T(8,128)(2,1)S(1)}, u32[]{:S(2)}, u32[]{:S(2)}) collective-permute-start(bf16[8,16,8,128]{3,2,1,0:T(8,128)(2,1)S(1)} %all-to-all-done.5), channel_id=1, source_target_pairs={{0,1},{1,0},{2,3},{3,2},{4,5},{5,4},{6,7},{7,6},{8,9},{9,8},{10,11... | collective-permute-start | bytes 786440 | tf_op jit(solution)/shard_map/ppermute | solution.py:40
  147.1 7.1 %copy-start.13 = (bf16[128,128]{1,0:T(8,128)(2,1)S(1)}, bf16[128,128]{1,0:T(8,128)(2,1)}, u32[]{:S(2)}) copy-start(bf16[128,128]{1,0:T(8,128)(2,1)} %gate_w_ref.5) | copy-start | bytes 98308
  147.1 20.0 %all-to-all-start.6 = ((bf16[16,2,8,8,128]{4,3,2,1,0:T(8,128)(2,1)}), bf16[16,2,8,8,128]{4,3,2,1,0:T(8,128)(2,1)S(1)}, u32[]{:S(2)}, u32[]{:S(2)}) async-start(bf16[16,2,8,8,128]{4,3,2,1,0:T(8,128)(2,1)} %bitcast.11), calls=%async_computation.6 | async-start | bytes 1048576 | tf_op jit(solution)/shard_map/all_to_all | solution.py:36
  153.5 13.6 %copy-start.14 = (bf16[128,128]{1,0:T(8,128)(2,1)S(1)}, bf16[128,128]{1,0:T(8,128)(2,1)}, u32[]{:S(2)}) copy-start(bf16[128,128]{1,0:T(8,128)(2,1)} %out_w_ref.5) | copy-start | bytes 98308
  153.5 0.7 collective-permute-start.11
  (3 other events, 3.4 us)
